TPU v7x, 512 devices: a whole 4x8x8 slice. The times are simulated.
512 devices in a mesh: tok: 8 (over y), head: 8 (over z_lo, core), wid: 8 (over x, z_hi).
Axes of the slice: x: 4, y: 8, z: 8 (z_hi: 2, z_lo: 4; z = z_hi * 4 + z_lo), core: 2. Of those that a mesh axis runs over, the one named last changes fastest.
Arguments:
- inputs: bfloat16 [4096, 8192], P('tok', 'wid'), may hold values from -3 to 3
- q_grad: bfloat16 [4096, 8192], P(('tok', 'wid'), 'head'), may hold values from -0.59765625 to 0.59765625
- key_value_share_gradient: bfloat16 [4096, 2048], P(('tok', 'wid'), 'head'), may hold values from -0.59765625 to 0.59765625
- q_weight: bfloat16 [8192, 8192], P('wid', 'head'), may hold values from -0.59765625 to 0.59765625
- key_value_weight: bfloat16 [8192, 1024], P('wid', 'head'), may hold values from -0.59765625 to 0.59765625
Outputs:
- input_grad: bfloat16 [4096, 8192], P('tok', ('wid', 'head'))
- q_weight_grad: float32 [8192, 8192], P(('wid', 'tok'), 'head')
- kv_weight_grad: float32 [8192, 1024], P(('wid', 'tok'), 'head')
All inputs are finite; a program needn't handle non-finite values.
Results may differ from a plain program's by a relative error of at most 0.017.
Values may be sent and summed in bfloat16 or wider, within the bound.
No kernel may reach another device: no remote copies, remote signals or barrier semaphores. Data moves between devices by JAX's collectives and lax.ppermute only.
A program may use at most 64 MiB of HBM per device.

v0:
```python
import jax
import jax.numpy as jnp
from jax import lax
from jax.sharding import PartitionSpec as P


def partner(x, axis, bit):
    return lax.ppermute(x, axis, [(i, i ^ 1 << bit) for i in range(lax.axis_size(axis))])


def contract_last(left_rows, right_rows):
    return lax.dot_general(
        left_rows, right_rows, (((1,), (1,)), ((), ())), preferred_element_type=jnp.float32
    )


def contract_first(left_rows, right_rows):
    return lax.dot_general(
        left_rows, right_rows, (((0,), (0,)), ((), ())), preferred_element_type=jnp.float32
    )


def local(inputs, q_grad, key_value_share_gradient, q_weight, key_value_weight):
    head_dim = key_value_weight.shape[1]
    parity = lax.axis_index("head") % 2
    q_rows, part_rows = (
        lax.all_gather(q_grad, "wid", axis=0, tiled=True),
        lax.all_gather(key_value_share_gradient, "wid", axis=0, tiled=True),
    )
    outgoing = lax.dynamic_slice_in_dim(part_rows, (1 - parity) * head_dim, head_dim, 1)
    incoming = partner(outgoing, "head", 0)
    own_part = lax.dynamic_slice_in_dim(part_rows, parity * head_dim, head_dim, 1)
    kv_rows = (own_part.astype(jnp.float32) + incoming.astype(jnp.float32)).astype(jnp.bfloat16)
    partial_terms = contract_last(q_rows, q_weight) + contract_last(kv_rows, key_value_weight)
    input_grad = lax.psum_scatter(
        partial_terms.astype(jnp.bfloat16), "head", scatter_dimension=1, tiled=True
    )
    combined = jnp.concatenate([q_rows, kv_rows], axis=1)
    reduced = lax.psum_scatter(
        contract_first(inputs, combined).astype(jnp.bfloat16),
        "tok",
        scatter_dimension=0,
        tiled=True,
    ).astype(jnp.float32)
    q_columns = q_rows.shape[1]
    return (input_grad, reduced[:, :q_columns], reduced[:, q_columns:])


def solution(mesh):
    return jax.shard_map(
        local,
        mesh=mesh,
        in_specs=(
            P("tok", "wid"),
            P(("tok", "wid"), "head"),
            P(("tok", "wid"), "head"),
            P("wid", "head"),
            P("wid", "head"),
        ),
        out_specs=(P("tok", ("wid", "head")), P(("wid", "tok"), "head"), P(("wid", "tok"), "head")),
        check_vma=False,
    )
```

profile of v0, /device:TPU:6, one launch (start us, length us, event | category | flops | bytes accessed | tf_op | source)
XLA Modules:
  0.0 182.5 jit_solution(3867470586869715559)
XLA Ops:
  7.2 0.0 copy-start
  7.2 0.0 all-gather.2.cloned.1.call-start
  7.2 0.7 all-gather.2.cloned.1.call-update
  7.9 0.0 reduce-scatter.7.cloned.1.call-start
  8.0 48.0 %all_gather.7 = bf16[512,256]{1,0:T(8,128)(2,1)S(1)} all-gather(bf16[64,256]{1,0:T(8,128)(2,1)} %param.7), channel_id=1, replica_groups=mesh['tok'=8,'head'=8,'wid'=8] {'wid'}, dimensions={0}, use_global_device_ids=true | all-gather | bytes 294912 | tf_op jit(solution)/shard_map/all_gather | solution.py:28
  56.0 1.9 %collective-permute-start = (bf16[512,128]{1,0:T(8,128)(2,1)S(1)}, bf16[512,128]{1,0:T(8,128)(2,1)S(1)}, u32[]{:S(2)}, u32[]{:S(2)}) collective-permute-start(bf16[512,128]{1,0:T(8,128)(2,1)S(1)} %constant_dynamic-slice_fusion), channel_id=1, source_target_pairs={{0,8},{8,0},{16,24},{24,16},{32,40},{40,32},{48,56},{56,48},{1,9},... | collective-permute-start | bytes 393224 | tf_op jit(solution)/shard_map/ppermute | solution.py:8
  58.0 1.3 collective-permute-done
  59.3 0.0 copy-start.1
  59.3 24.9 %all-gather.2.cloned.1.call-done = bf16[512,1024]{1,0:T(8,128)(2,1)} async-done(((bf16[64,1024]{1,0:T(8,128)(2,1)}), bf16[512,1024]{1,0:T(8,128)(2,1)}) %all-gather.2.cloned.1.call-update) | async-done | bytes 1048592 | tf_op jit(solution)/shard_map/all_gather | solution.py:27
  84.2 0.0 copy-done
  84.2 2.5 %fusion.5 = f32[512,1024]{1,0:T(8,128)S(1)} fusion(bf16[512,1024]{1,0:T(8,128)(2,1)} %all-gather.2.cloned.1.call-done, bf16[1024,1024]{1,0:T(8,128)(2,1)S(1)} %copy-done), kind=kOutput, calls=%fused_computation.9 | convolution fusion | flops 1073741824 | bytes 5242880 | tf_op jit(solution)/shard_map/dot_general | solution.py:12
  86.7 0.0 copy-done.1
  86.8 0.4 add_convert_fusion
  87.2 1.3 copy.12
  88.5 0.0 reduce-scatter.7.cloned.1.call-update
  88.6 0.0 reduce-scatter.9.cloned.1.call-start
  88.6 4.4 %fusion = bf16[1024,1152]{0,1:T(8,128)(2,1)} fusion(bf16[512,1024]{1,0:T(8,128)(2,1)} %param.5, bf16[512,128]{1,0:T(8,128)(2,1)S(1)} %add_convert_fusion.1, bf16[512,1024]{1,0:T(8,128)(2,1)} %all-gather.2.cloned.1.call-done), kind=kOutput, calls=%fused_computation.1 | convolution fusion | flops 1211498496 | bytes 4587520 | tf_op jit(solution)/shard_map/dot_general | solution.py:18
  93.0 4.3 %copy.14 = bf16[1024,1152]{1,0:T(8,128)(2,1)} copy(bf16[1024,1152]{0,1:T(8,128)(2,1)} %fusion) | data formatting | bytes 4718592
  97.3 0.0 reduce-scatter.9.cloned.1.call-update
  97.3 28.0 %reduce-scatter.7.cloned.1.call-done = bf16[128,512]{1,0:T(8,128)(2,1)} async-done(((bf16[1024,512]{1,0:T(8,128)(2,1)}), bf16[128,512]{1,0:T(8,128)(2,1)}) %reduce-scatter.7.cloned.1.call-update) | async-done | bytes 131088
  125.4 1.7 copy.13
  127.0 45.1 %reduce-scatter.9.cloned.1.call-done = bf16[128,1152]{1,0:T(8,128)(2,1)} async-done(((bf16[1024,1152]{1,0:T(8,128)(2,1)}), bf16[128,1152]{1,0:T(8,128)(2,1)}) %reduce-scatter.9.cloned.1.call-update) | async-done | bytes 294928
  172.2 0.8 slice.9
  172.9 0.1 copy.17
  173.0 0.7 copy.11
  173.8 1.0 slice.8
  174.8 0.2 copy.16
  174.9 1.0 copy.10
  (2 shorter events, 0.0 us)
Async XLA Ops:
  7.2 77.1 %copy-start = (bf16[1024,1024]{1,0:T(8,128)(2,1)S(1)}, bf16[1024,1024]{1,0:T(8,128)(2,1)}, u32[]{:S(2)}) copy-start(bf16[1024,1024]{1,0:T(8,128)(2,1)} %param.8) | copy-start | bytes 6291460
  7.2 77.0 %all-gather.2.cloned.1.call-start = ((), (), s32[]{:S(2)}) async-start(), calls=%async_computation.2 | async-start | bytes 1179648 | tf_op jit(solution)/shard_map/all_gather | solution.py:27
  7.9 117.5 %reduce-scatter.7.cloned.1.call-start = ((), (), s32[]{:S(2)}) async-start(), calls=%async_computation.3 | async-start | bytes 1179648
  56.0 3.2 %collective-permute-start = (bf16[512,128]{1,0:T(8,128)(2,1)S(1)}, bf16[512,128]{1,0:T(8,128)(2,1)S(1)}, u32[]{:S(2)}, u32[]{:S(2)}) collective-permute-start(bf16[512,128]{1,0:T(8,128)(2,1)S(1)} %constant_dynamic-slice_fusion), channel_id=1, source_target_pairs={{0,8},{8,0},{16,24},{24,16},{32,40},{40,32},{48,56},{56,48},{1,9},... | collective-permute-start | bytes 393224 | tf_op jit(solution)/shard_map/ppermute | solution.py:8
  59.3 27.4 %copy-start.1 = (bf16[1024,128]{1,0:T(8,128)(2,1)S(1)}, bf16[1024,128]{1,0:T(8,128)(2,1)}, u32[]{:S(2)}) copy-start(bf16[1024,128]{1,0:T(8,128)(2,1)} %param.9) | copy-start | bytes 786436
  88.6 83.6 %reduce-scatter.9.cloned.1.call-start = ((), (), s32[]{:S(2)}) async-start(), calls=%async_computation.4 | async-start | bytes 2654208
Sparse Core Ops, SparseCore 0:
  11.2 72.9 all-gather.1
  88.7 36.6 reduce-scatter.6
  128.2 43.8 reduce-scatter.8
where the time goes:
time: 183 us; the launch traced here: 182 us
  waiting for transfers between devices  100 us (55%)
  blocking collectives  48 us (26%)
  between operations  13.9 us (8%)
  local copies, waits for them, and re-layouts  11.1 us (6%)
  matrix products  7.32 us (4%)
  starting transfers between devices  2.04 us (1%)
    unnamed x5, waiting for transfers between devices  73.9 us
    all_gather x1, blocking collectives, local(): lax.all_gather(key_value_share_gradient, 'wid', axis=0, tiled=True)  48 us
    all_gather x1, waiting for transfers between devices, local(): lax.all_gather(q_grad, 'wid', axis=0, tiled=True)  24.9 us
    unnamed x11, local copies, waits for them, and re-layouts  9.34 us
    dot_general x1, matrix products, contract_first(): lax.dot_general(left_rows, right_rows, (((0,), (0,)), ((), ())), preferre...  4.38 us
  transfers between devices with their start and end apart: 4, of which 4 were waited for; matrix products, arithmetic and copies ran while one was open for 6% of the time, Pallas kernels for 0%

commit v1 on v0

v1 whole, which is shorter than its diff:
```python
import jax
import jax.numpy as jnp
from jax import lax
from jax.sharding import Mesh
from jax.sharding import PartitionSpec as P

SWAP = [(0, 1), (1, 0)]


def spread(rows):
    n = lax.axis_size("x")
    copies = jnp.broadcast_to(rows[None], (n, *rows.shape))
    return lax.all_to_all(copies, "x", 0, 0, tiled=True)


def contract_last(left, right):
    return lax.dot_general(
        left, right, (((1,), (1,)), ((), ())), preferred_element_type=jnp.float32
    )


def contract_first(left, right):
    return lax.dot_general(
        left, right, (((0,), (0,)), ((), ())), preferred_element_type=jnp.float32
    )


def local(inputs, q_grad, key_value_share_gradient, q_weight, key_value_weight):
    head_dim = key_value_weight.shape[1]
    q_columns = q_grad.shape[1]
    core = lax.axis_index("core")
    zhi = lax.axis_index("zhi")
    n_zlo = lax.axis_size("zlo")

    share = key_value_share_gradient
    outgoing = lax.dynamic_slice_in_dim(share, (1 - core) * head_dim, head_dim, 1)
    incoming = lax.ppermute(outgoing, "core", SWAP)
    own_part = lax.dynamic_slice_in_dim(share, core * head_dim, head_dim, 1)
    kv_rows = (own_part.astype(jnp.float32) + incoming.astype(jnp.float32)).astype(jnp.bfloat16)
    mine = jnp.concatenate([q_grad, kv_rows], axis=1)

    far = lax.ppermute(mine, "zhi", SWAP)
    near_all = spread(mine)
    far_all = spread(far)
    first = jnp.where(zhi == 0, near_all, far_all)
    second = jnp.where(zhi == 0, far_all, near_all)
    combined = jnp.stack([first, second], axis=1).reshape(-1, mine.shape[1])

    reduced = lax.psum_scatter(
        contract_first(inputs, combined).astype(jnp.bfloat16),
        "tok",
        scatter_dimension=0,
        tiled=True,
    ).astype(jnp.float32)

    weight = jnp.concatenate([q_weight, key_value_weight], axis=1)
    width = weight.shape[0] // (2 * n_zlo)
    weight = weight.reshape(n_zlo, 2, width, weight.shape[1])
    keep = lax.dynamic_index_in_dim(weight, core, 1, keepdims=False)
    give = lax.dynamic_index_in_dim(weight, 1 - core, 1, keepdims=False)

    def terms(part):
        return contract_last(combined, part.reshape(-1, part.shape[-1]))

    got = lax.ppermute(terms(give).astype(jnp.bfloat16), "core", SWAP)
    pair = (terms(keep) + got.astype(jnp.float32)).astype(jnp.bfloat16)
    pieces = jnp.swapaxes(pair.reshape(-1, n_zlo, width), 0, 1)
    pieces = lax.all_to_all(pieces, "zlo", 0, 0, tiled=True)
    input_grad = jnp.sum(pieces.astype(jnp.float32), axis=0).astype(jnp.bfloat16)
    return (input_grad, reduced[:, :q_columns], reduced[:, q_columns:])


def solution(mesh):
    fine = Mesh(
        mesh.devices.reshape(8, 4, 2, 4, 2), ("tok", "zlo", "core", "x", "zhi")
    )
    tok, head, wid = "tok", ("zlo", "core"), ("x", "zhi")
    return jax.shard_map(
        local,
        mesh=fine,
        in_specs=(
            P(tok, wid),
            P((tok, *wid), head),
            P((tok, *wid), head),
            P(wid, head),
            P(wid, head),
        ),
        out_specs=(P(tok, (*wid, *head)), P((*wid, tok), head), P((*wid, tok), head)),
        check_vma=False,
    )
```

time: 183 us -> 113 us (0.62)
  waiting for transfers between devices: 100 us -> 35.1 us
  blocking collectives: 48 us -> 19.9 us
  starting transfers between devices: 2.04 us -> 24.3 us
  matrix products: 7.32 us -> 3.17 us
  local copies, waits for them, and re-layouts: 11.1 us -> 13.4 us
  other arithmetic: 0.04 us -> 2.17 us
    unnamed x5 -> x2, waiting for transfers between devices: 73.9 us -> 19.7 us
    all_gather x1 -> x0, blocking collectives: 48 us -> none  [local(): lax.all_gather(key_value_share_gradient, 'wid', axis=0, tiled=True)]
    all_gather x1 -> x0, waiting for transfers between devices: 24.9 us -> none  [local(): lax.all_gather(q_grad, 'wid', axis=0, tiled=True)]
    all_to_all x0 -> x1, blocking collectives: none -> 19.9 us  [local(): pieces = lax.all_to_all(pieces, 'zlo', 0, 0, tiled=True)]
    all_to_all x0 -> x2, starting transfers between devices: none -> 14.1 us  [spread(): return lax.all_to_all(copies, 'x', 0, 0, tiled=True)]
    ppermute x1 -> x3, starting transfers between devices: 1.92 us -> 10.2 us  [the longest x1 6.37 us: local(): far = lax.ppermute(mine, 'zhi', SWAP)]
    all_to_all x0 -> x2, waiting for transfers between devices: none -> 7.28 us  [spread(): return lax.all_to_all(copies, 'x', 0, 0, tiled=True)]
    ppermute x1 -> x3, waiting for transfers between devices: 1.31 us -> 8.17 us  [the longest x1 5.15 us: local(): far = lax.ppermute(mine, 'zhi', SWAP)]
  transfers between devices with their start and end apart: 4 -> 6, of which waited for: 4 -> 5; matrix products, arithmetic and copies ran while one was open for 6% -> 3% of each run, Pallas kernels for 0% -> 0%
where the time goes in v1:
time: 113 us; the launch traced here: 112 us
  waiting for transfers between devices  35.1 us (31%)
  starting transfers between devices  24.3 us (22%)
  blocking collectives  19.9 us (18%)
  between operations  14.2 us (13%)
  local copies, waits for them, and re-layouts  13.4 us (12%)
  matrix products  3.17 us (3%)
  other arithmetic  2.17 us (2%)
    all_to_all x1, blocking collectives, local(): pieces = lax.all_to_all(pieces, 'zlo', 0, 0, tiled=True)  19.9 us
    unnamed x2, waiting for transfers between devices  19.7 us
    all_to_all x2, starting transfers between devices, spread(): return lax.all_to_all(copies, 'x', 0, 0, tiled=True)  14.1 us
    unnamed x16, local copies, waits for them, and re-layouts  8.96 us
    all_to_all x2, waiting for transfers between devices, spread(): return lax.all_to_all(copies, 'x', 0, 0, tiled=True)  7.28 us
    ppermute x1, starting transfers between devices, local(): far = lax.ppermute(mine, 'zhi', SWAP)  6.37 us
    ppermute x1, waiting for transfers between devices, local(): far = lax.ppermute(mine, 'zhi', SWAP)  5.15 us
  transfers between devices with their start and end apart: 6, of which 5 were waited for; matrix products, arithmetic and copies ran while one was open for 3% of the time, Pallas kernels for 0%

profile of v1, /device:TPU:6, one launch (start us, length us, event | category | flops | bytes accessed | tf_op | source)
XLA Modules:
  0.0 112.3 jit_solution(17051973287683355981)
XLA Ops:
  7.2 0.0 copy-start
  7.2 0.8 constant_dynamic-slice_fusion.2
  8.0 1.9 %collective-permute-start = (bf16[64,128]{1,0:T(8,128)(2,1)S(1)}, bf16[64,128]{1,0:T(8,128)(2,1)S(1)}, u32[]{:S(2)}, u32[]{:S(2)}) collective-permute-start(bf16[64,128]{1,0:T(8,128)(2,1)S(1)} %constant_dynamic-slice_fusion.2), channel_id=1, source_target_pairs={{0,8},{8,0},{1,9},{9,1},{2,10},{10,2},{3,11},{11,3},{4,12},{12,4},... | collective-permute-start | bytes 49160 | tf_op jit(solution)/shard_map/ppermute | solution.py:37
  9.9 1.1 %collective-permute-done = bf16[64,128]{1,0:T(8,128)(2,1)S(1)} collective-permute-done((bf16[64,128]{1,0:T(8,128)(2,1)S(1)}, bf16[64,128]{1,0:T(8,128)(2,1)S(1)}, u32[]{:S(2)}, u32[]{:S(2)}) %collective-permute-start) | collective-permute-done | bytes 16416 | tf_op jit(solution)/shard_map/ppermute | solution.py:37
  11.1 0.7 add_convert_fusion.1
  11.8 0.9 pad_maximum_fusion.2
  12.7 0.9 broadcast_in_dim.4
  13.6 9.3 %all-to-all-start = ((bf16[4,64,1152]{2,1,0:T(8,128)(2,1)}), bf16[4,64,1152]{2,1,0:T(8,128)(2,1)S(1)}, u32[]{:S(2)}, u32[]{:S(2)}) async-start(bf16[4,64,1152]{2,1,0:T(8,128)(2,1)} %broadcast_in_dim.4), calls=%async_computation | async-start | bytes 1179648 | tf_op jit(solution)/shard_map/all_to_all | solution.py:13
  22.9 6.4 %collective-permute-start.1 = (bf16[64,1152]{1,0:T(8,128)(2,1)S(1)}, bf16[64,1152]{1,0:T(8,128)(2,1)S(1)}, u32[]{:S(2)}, u32[]{:S(2)}) collective-permute-start(bf16[64,1152]{1,0:T(8,128)(2,1)S(1)} %pad_maximum_fusion.2), channel_id=1, source_target_pairs={{0,1},{1,0},{2,3},{3,2},{4,5},{5,4},{6,7},{7,6},{8,9},{9,8},{10,11... | collective-permute-start | bytes 442376 | tf_op jit(solution)/shard_map/ppermute | solution.py:42
  29.2 5.1 %collective-permute-done.1 = bf16[64,1152]{1,0:T(8,128)(2,1)S(1)} collective-permute-done((bf16[64,1152]{1,0:T(8,128)(2,1)S(1)}, bf16[64,1152]{1,0:T(8,128)(2,1)S(1)}, u32[]{:S(2)}, u32[]{:S(2)}) %collective-permute-start.1) | collective-permute-done | bytes 147488 | tf_op jit(solution)/shard_map/ppermute | solution.py:42
  34.4 0.0 all-to-all-done
  34.4 0.9 broadcast_in_dim.5
  35.2 4.8 %all-to-all-start.1 = ((bf16[4,64,1152]{2,1,0:T(8,128)(2,1)}), bf16[4,64,1152]{2,1,0:T(8,128)(2,1)S(1)}, u32[]{:S(2)}, u32[]{:S(2)}) async-start(bf16[4,64,1152]{2,1,0:T(8,128)(2,1)} %broadcast_in_dim.5), calls=%async_computation.1 | async-start | bytes 1179648 | tf_op jit(solution)/shard_map/all_to_all | solution.py:13
  40.0 0.0 reduce-scatter.4.cloned.1.call-start
  40.0 7.3 %all-to-all-done.1 = bf16[4,64,1152]{2,1,0:T(8,128)(2,1)S(1)} async-done(((bf16[4,64,1152]{2,1,0:T(8,128)(2,1)}), bf16[4,64,1152]{2,1,0:T(8,128)(2,1)S(1)}, u32[]{:S(2)}, u32[]{:S(2)}) %all-to-all-start.1) | async-done | bytes 589856 | tf_op jit(solution)/shard_map/all_to_all | solution.py:13
  47.3 0.1 select_bitcast_fusion.1
  47.4 0.1 pad_maximum_fusion.1
  47.6 0.0 copy-start.2
  47.6 1.0 copy-done.2
  48.6 0.0 copy-done
  48.6 1.4 %fusion = bf16[1024,1152]{0,1:T(8,128)(2,1)S(1)} fusion(bf16[512,1152]{1,0:T(8,128)(2,1)S(1)} %bitcast.25, bf16[512,1024]{1,0:T(8,128)(2,1)S(1)} %copy-done), kind=kOutput, calls=%fused_computation.1 | convolution fusion | flops 1209139200 | bytes 4587520 | tf_op jit(solution)/shard_map/dot_general | solution.py:23
  50.0 2.5 %copy.21 = bf16[1024,1152]{1,0:T(8,128)(2,1)} copy(bf16[1024,1152]{0,1:T(8,128)(2,1)S(1)} %fusion) | data formatting | bytes 4718592
  52.6 0.0 copy-start.1
  52.6 0.0 copy-start.4
  52.6 0.0 reduce-scatter.4.cloned.1.call-update
  52.6 1.6 %copy-done.1 = bf16[1024,1024]{1,0:T(8,128)(2,1)S(1)} copy-done((bf16[1024,1024]{1,0:T(8,128)(2,1)S(1)}, bf16[1024,1024]{1,0:T(8,128)(2,1)}, u32[]{:S(2)}) %copy-start.1) | copy-done | bytes 2097176
  54.2 0.0 copy-done.4
  54.2 0.2 pad_maximum_fusion
  54.4 0.0 copy-start.3
  54.4 0.2 constant_dynamic-slice_fusion
  54.6 1.0 copy-done.3
  55.6 0.9 convolution_convert_fusion.1
  56.5 1.9 %collective-permute-start.2 = (bf16[512,512]{0,1:T(8,128)(2,1)S(1)}, bf16[512,512]{0,1:T(8,128)(2,1)S(1)}, u32[]{:S(2)}, u32[]{:S(2)}) collective-permute-start(bf16[512,512]{0,1:T(8,128)(2,1)S(1)} %convolution_convert_fusion.1), channel_id=1, source_target_pairs={{0,8},{8,0},{1,9},{9,1},{2,10},{10,2},{3,11},{11,3},{4,12},{12,4},... | collective-permute-start | bytes 1572872 | tf_op jit(solution)/shard_map/ppermute | solution.py:65
  58.5 1.9 %collective-permute-done.2 = bf16[512,512]{0,1:T(8,128)(2,1)S(1)} collective-permute-done((bf16[512,512]{0,1:T(8,128)(2,1)S(1)}, bf16[512,512]{0,1:T(8,128)(2,1)S(1)}, u32[]{:S(2)}, u32[]{:S(2)}) %collective-permute-start.2) | collective-permute-done | bytes 524320 | tf_op jit(solution)/shard_map/ppermute | solution.py:65
  60.3 0.9 add_convert_fusion
  61.2 19.9 %all_to_all.15 = bf16[4,512,128]{1,2,0:T(8,128)(2,1)S(1)} all-to-all(bf16[4,512,128]{1,2,0:T(8,128)(2,1)S(1)} %bitcast.28), channel_id=1, replica_groups=mesh['tok'=8,'zlo'=4,'core'=2,'x'=4,'zhi'=2] {'zlo'}, dimensions={0} | all-to-all | bytes 1048576 | tf_op jit(solution)/shard_map/all_to_all | solution.py:68
  81.1 0.1 reduce_sum.12
  81.2 0.8 copy.17
  81.9 19.7 %reduce-scatter.4.cloned.1.call-done = bf16[128,1152]{1,0:T(8,128)(2,1)} async-done(((bf16[1024,1152]{1,0:T(8,128)(2,1)}), bf16[128,1152]{1,0:T(8,128)(2,1)}) %reduce-scatter.4.cloned.1.call-update) | async-done | bytes 294928
  101.6 1.0 slice.8
  102.6 0.2 copy.23
  102.8 1.0 copy.18
  103.8 0.8 slice.9
  104.6 0.1 copy.24
  104.7 0.7 copy.19
Async XLA Ops:
  7.2 41.4 %copy-start = (bf16[512,1024]{1,0:T(8,128)(2,1)S(1)}, bf16[512,1024]{1,0:T(8,128)(2,1)}, u32[]{:S(2)}) copy-start(bf16[512,1024]{1,0:T(8,128)(2,1)} %param.5) | copy-start | bytes 3145732
  8.0 3.1 %collective-permute-start = (bf16[64,128]{1,0:T(8,128)(2,1)S(1)}, bf16[64,128]{1,0:T(8,128)(2,1)S(1)}, u32[]{:S(2)}, u32[]{:S(2)}) collective-permute-start(bf16[64,128]{1,0:T(8,128)(2,1)S(1)} %constant_dynamic-slice_fusion.2), channel_id=1, source_target_pairs={{0,8},{8,0},{1,9},{9,1},{2,10},{10,2},{3,11},{11,3},{4,12},{12,4},... | collective-permute-start | bytes 49160 | tf_op jit(solution)/shard_map/ppermute | solution.py:37
  13.6 20.8 %all-to-all-start = ((bf16[4,64,1152]{2,1,0:T(8,128)(2,1)}), bf16[4,64,1152]{2,1,0:T(8,128)(2,1)S(1)}, u32[]{:S(2)}, u32[]{:S(2)}) async-start(bf16[4,64,1152]{2,1,0:T(8,128)(2,1)} %broadcast_in_dim.4), calls=%async_computation | async-start | bytes 1179648 | tf_op jit(solution)/shard_map/all_to_all | solution.py:13
  22.9 11.5 %collective-permute-start.1 = (bf16[64,1152]{1,0:T(8,128)(2,1)S(1)}, bf16[64,1152]{1,0:T(8,128)(2,1)S(1)}, u32[]{:S(2)}, u32[]{:S(2)}) collective-permute-start(bf16[64,1152]{1,0:T(8,128)(2,1)S(1)} %pad_maximum_fusion.2), channel_id=1, source_target_pairs={{0,1},{1,0},{2,3},{3,2},{4,5},{5,4},{6,7},{7,6},{8,9},{9,8},{10,11... | collective-permute-start | bytes 442376 | tf_op jit(solution)/shard_map/ppermute | solution.py:42
  35.2 12.1 %all-to-all-start.1 = ((bf16[4,64,1152]{2,1,0:T(8,128)(2,1)}), bf16[4,64,1152]{2,1,0:T(8,128)(2,1)S(1)}, u32[]{:S(2)}, u32[]{:S(2)}) async-start(bf16[4,64,1152]{2,1,0:T(8,128)(2,1)} %broadcast_in_dim.5), calls=%async_computation.1 | async-start | bytes 1179648 | tf_op jit(solution)/shard_map/all_to_all | solution.py:13
  40.0 61.6 %reduce-scatter.4.cloned.1.call-start = ((), (), s32[]{:S(2)}) async-start(), calls=%async_computation.4 | async-start | bytes 2654208
  47.6 1.0 copy-start.2
  52.6 1.6 %copy-start.1 = (bf16[1024,1024]{1,0:T(8,128)(2,1)S(1)}, bf16[1024,1024]{1,0:T(8,128)(2,1)}, u32[]{:S(2)}) copy-start(bf16[1024,1024]{1,0:T(8,128)(2,1)} %param.8) | copy-start | bytes 6291460
  52.6 1.6 %copy-start.4 = (bf16[1024,128]{1,0:T(8,128)(2,1)S(1)}, bf16[1024,128]{1,0:T(8,128)(2,1)}, u32[]{:S(2)}) copy-start(bf16[1024,128]{1,0:T(8,128)(2,1)} %param.9) | copy-start | bytes 786436
  54.4 1.3 %copy-start.3 = (bf16[4,2,64,1152]{3,2,1,0:T(8,128)(2,1)S(1)}, bf16[4,2,64,1152]{3,2,1,0:T(8,128)(2,1)}, u32[]{:S(2)}) copy-start(bf16[4,2,64,1152]{3,2,1,0:T(8,128)(2,1)} %copy-done.2) | copy-start | bytes 3538948
  56.5 3.8 %collective-permute-start.2 = (bf16[512,512]{0,1:T(8,128)(2,1)S(1)}, bf16[512,512]{0,1:T(8,128)(2,1)S(1)}, u32[]{:S(2)}, u32[]{:S(2)}) collective-permute-start(bf16[512,512]{0,1:T(8,128)(2,1)S(1)} %convolution_convert_fusion.1), channel_id=1, source_target_pairs={{0,8},{8,0},{1,9},{9,1},{2,10},{10,2},{3,11},{11,3},{4,12},{12,4},... | collective-permute-start | bytes 1572872 | tf_op jit(solution)/shard_map/ppermute | solution.py:65
Sparse Core Ops, SparseCore 0:
  52.7 48.8 reduce-scatter.3

commit v2 on v1

v2 whole, which is shorter than its diff:
```python
import jax
import jax.numpy as jnp
from jax import lax
from jax.sharding import Mesh
from jax.sharding import PartitionSpec as P

SWAP = [(0, 1), (1, 0)]
WID = ("x", "zhi")
TOK = ("th", "tl")
HEAD = ("zlo", "core")
CHUNKS = (384, 384, 384)


def neighbour(at):
    y, core = divmod(at, 2)
    other = y ^ 1 if core == 0 else (y + (1 if y % 2 else -1)) % 8
    return other * 2 + core


NEIGHBOUR = [(i, neighbour(i)) for i in range(16)]


def spread(rows):
    n = lax.axis_size(WID)
    copies = jnp.broadcast_to(rows[None], (n, *rows.shape))
    return lax.all_to_all(copies, WID, 0, 0, tiled=True).reshape(-1, rows.shape[1])


def contract_last(left, right):
    return lax.dot_general(
        left, right, (((1,), (1,)), ((), ())), preferred_element_type=jnp.float32
    )


def matmul(left, right):
    return jnp.dot(left, right, preferred_element_type=jnp.float32)


def local(inputs, q_grad, key_value_share_gradient, q_weight, key_value_weight):
    head_dim = key_value_weight.shape[1]
    q_columns = q_grad.shape[1]
    core = lax.axis_index("core")
    tl = lax.axis_index("tl")
    n_zlo, n_th = lax.axis_size("zlo"), lax.axis_size("th")

    share = key_value_share_gradient
    outgoing = lax.dynamic_slice_in_dim(share, (1 - core) * head_dim, head_dim, 1)
    incoming = lax.ppermute(outgoing, "core", SWAP)
    own_part = lax.dynamic_slice_in_dim(share, core * head_dim, head_dim, 1)
    kv_rows = (own_part.astype(jnp.float32) + incoming.astype(jnp.float32)).astype(jnp.bfloat16)

    chunks = []
    at = 0
    for size in CHUNKS[:-1]:
        chunks.append(spread(q_grad[:, at : at + size]))
        at += size
    chunks.append(spread(jnp.concatenate([q_grad[:, at:], kv_rows], axis=1)))

    flipped = inputs.T
    tall = flipped.shape[0] // (2 * n_th)
    flipped = flipped.reshape(n_th, 2, tall, -1)
    keep_in = lax.dynamic_index_in_dim(flipped, tl, 1, keepdims=False).reshape(n_th * tall, -1)
    give_in = lax.dynamic_index_in_dim(flipped, 1 - tl, 1, keepdims=False).reshape(n_th * tall, -1)

    sums = []
    for chunk in chunks:
        give = matmul(give_in, chunk).astype(jnp.bfloat16)
        got = lax.ppermute(give, (*TOK, "core"), NEIGHBOUR)
        pair = (matmul(keep_in, chunk) + got.astype(jnp.float32)).astype(jnp.bfloat16)
        pieces = lax.all_to_all(pair.reshape(n_th, tall, -1), "th", 0, 0, tiled=True)
        sums.append(jnp.sum(pieces.astype(jnp.float32), axis=0))

    combined = jnp.concatenate(chunks, axis=1)
    weight = jnp.concatenate([q_weight, key_value_weight], axis=1)
    width = weight.shape[0] // (2 * n_zlo)
    weight = weight.reshape(n_zlo, 2, width, weight.shape[1])
    keep_w = lax.dynamic_index_in_dim(weight, core, 1, keepdims=False)
    give_w = lax.dynamic_index_in_dim(weight, 1 - core, 1, keepdims=False)

    def terms(part):
        return contract_last(combined, part.reshape(-1, part.shape[-1]))

    got = lax.ppermute(terms(give_w).astype(jnp.bfloat16), "core", SWAP)
    pair = (terms(keep_w) + got.astype(jnp.float32)).astype(jnp.bfloat16)
    pieces = jnp.swapaxes(pair.reshape(-1, n_zlo, width), 0, 1)
    pieces = lax.all_to_all(pieces, "zlo", 0, 0, tiled=True)
    input_grad = jnp.sum(pieces.astype(jnp.float32), axis=0).astype(jnp.bfloat16)

    last = q_columns - sum(CHUNKS[:-1])
    q_out = jnp.concatenate([*sums[:-1], sums[-1][:, :last]], axis=1)
    return (input_grad, q_out, sums[-1][:, last:])


def solution(mesh):
    fine = Mesh(
        mesh.devices.reshape(4, 2, 4, 2, 4, 2), ("th", "tl", "zlo", "core", "x", "zhi")
    )
    return jax.shard_map(
        local,
        mesh=fine,
        in_specs=(
            P(TOK, WID),
            P((*TOK, *WID), HEAD),
            P((*TOK, *WID), HEAD),
            P(WID, HEAD),
            P(WID, HEAD),
        ),
        out_specs=(P(TOK, (*WID, *HEAD)), P((*WID, *TOK), HEAD), P((*WID, *TOK), HEAD)),
        check_vma=False,
    )
```

time: 113 us -> 138 us (1.22)
  the two profiles are of different devices: /device:TPU:6 before, /device:TPU:8 now
where the time goes in v2:
time: 138 us; the launch traced here: 137 us
  starting transfers between devices  46.1 us (33%)
  waiting for transfers between devices  38.3 us (28%)
  blocking collectives  25.3 us (18%)
  matrix products  13.9 us (10%)
  local copies, waits for them, and re-layouts  7.04 us (5%)
  other arithmetic  5.03 us (4%)
    all_to_all x1, blocking collectives, spread(): lax.all_to_all(copies, WID, 0, 0, tiled=True).reshape(-1, rows.shape[1])  25.3 us
    all_to_all x3, waiting for transfers between devices, local(): lax.all_to_all(pair.reshape(n_th, tall, -1), 'th', 0, 0, tiled=True)  16.5 us
    all_to_all x3, starting transfers between devices, local(): lax.all_to_all(pair.reshape(n_th, tall, -1), 'th', 0, 0, tiled=True)  16 us
    all_to_all x2, starting transfers between devices, spread(): lax.all_to_all(copies, WID, 0, 0, tiled=True).reshape(-1, rows.shape[1])  9.54 us
    dot_general x6, matrix products, matmul(): return jnp.dot(left, right, preferred_element_type=jnp.float32)  9.48 us
    all_to_all x2, waiting for transfers between devices, spread(): lax.all_to_all(copies, WID, 0, 0, tiled=True).reshape(-1, rows.shape[1])  9.47 us
    all_to_all x1, waiting for transfers between devices, local(): pieces = lax.all_to_all(pieces, 'zlo', 0, 0, tiled=True)  9.25 us
    ppermute x3, starting transfers between devices, local(): got = lax.ppermute(give, (*TOK, 'core'), NEIGHBOUR)  9.08 us
  transfers between devices with their start and end apart: 11, of which 8 were waited for; matrix products, arithmetic and copies ran while one was open for 16% of the time, Pallas kernels for 0%

profile of v2, /device:TPU:8, one launch (start us, length us, event | category | flops | bytes accessed | tf_op | source)
XLA Modules:
  0.0 136.5 jit_solution(14905265300873210635)
XLA Ops:
  0.6 0.9 fusion.3
  1.6 25.3 %all_to_all.35 = bf16[8,64,384]{2,1,0:T(8,128)(2,1)S(1)} all-to-all(bf16[8,64,384]{2,1,0:T(8,128)(2,1)S(1)} %broadcast_in_dim.7), channel_id=1, replica_groups=mesh['th'=4,'tl'=2,'zlo'=4,'core'=2,'x'=4,'zhi'=2] {'x','zhi'}, dimensions={0} | all-to-all | bytes 786432 | tf_op jit(solution)/shard_map/all_to_all | solution.py:26
  27.0 0.8 broadcast_in_dim.6
  27.8 4.6 %all-to-all-start = ((bf16[8,64,384]{2,1,0:T(8,128)(2,1)}), bf16[8,64,384]{2,1,0:T(8,128)(2,1)S(1)}, u32[]{:S(2)}, u32[]{:S(2)}) async-start(bf16[8,64,384]{2,1,0:T(8,128)(2,1)} %broadcast_in_dim.6), calls=%async_computation | async-start | bytes 786432 | tf_op jit(solution)/shard_map/all_to_all | solution.py:26
  32.5 1.9 %collective-permute-start = (bf16[64,128]{1,0:T(8,128)(2,1)S(1)}, bf16[64,128]{1,0:T(8,128)(2,1)S(1)}, u32[]{:S(2)}, u32[]{:S(2)}) collective-permute-start(bf16[64,128]{1,0:T(8,128)(2,1)S(1)} %constant_dynamic-slice_fusion.4), channel_id=1, source_target_pairs={{0,8},{8,0},{1,9},{9,1},{2,10},{10,2},{3,11},{11,3},{4,12},{12,4},... | collective-permute-start | bytes 49160 | tf_op jit(solution)/shard_map/ppermute | solution.py:48
  34.4 0.0 slice-start
  34.4 0.5 copy.13
  35.0 0.1 constant_dynamic-slice_fusion
  35.0 0.5 collective-permute-done
  35.5 0.0 slice-done
  35.6 8.8 %all-to-all-done = bf16[8,64,384]{2,1,0:T(8,128)(2,1)S(1)} async-done(((bf16[8,64,384]{2,1,0:T(8,128)(2,1)}), bf16[8,64,384]{2,1,0:T(8,128)(2,1)S(1)}, u32[]{:S(2)}, u32[]{:S(2)}) %all-to-all-start) | async-done | bytes 393248 | tf_op jit(solution)/shard_map/all_to_all | solution.py:26
  44.4 0.9 broadcast_in_dim.8
  45.2 4.9 %all-to-all-start.2 = ((bf16[8,64,384]{2,1,0:T(8,128)(2,1)}), bf16[8,64,384]{2,1,0:T(8,128)(2,1)S(1)}, u32[]{:S(2)}, u32[]{:S(2)}) async-start(bf16[8,64,384]{2,1,0:T(8,128)(2,1)} %broadcast_in_dim.8), calls=%async_computation.2 | async-start | bytes 786432 | tf_op jit(solution)/shard_map/all_to_all | solution.py:26
  50.1 0.4 convolution_convert_fusion.2
  50.6 2.4 %collective-permute-start.3 = (bf16[512,384]{1,0:T(8,128)(2,1)S(1)}, bf16[512,384]{1,0:T(8,128)(2,1)S(1)}, u32[]{:S(2)}, u32[]{:S(2)}) collective-permute-start(bf16[512,384]{1,0:T(8,128)(2,1)S(1)} %convolution_convert_fusion.2), channel_id=1, source_target_pairs={{0,64},{8,456},{64,0},{72,136},{128,192},{136,72},{192,128},{200,2... | collective-permute-start | bytes 1179656 | tf_op jit(solution)/shard_map/ppermute | solution.py:68
  52.9 1.2 convolution_convert_fusion.3
  54.1 3.5 %collective-permute-start.2 = (bf16[512,384]{1,0:T(8,128)(2,1)}, bf16[512,384]{1,0:T(8,128)(2,1)}, u32[]{:S(2)}, u32[]{:S(2)}) collective-permute-start(bf16[512,384]{1,0:T(8,128)(2,1)} %convolution_convert_fusion.3), channel_id=1, source_target_pairs={{0,64},{8,456},{64,0},{72,136},{128,192},{136,72},{192,128},{200,2... | collective-permute-start | bytes 1179656 | tf_op jit(solution)/shard_map/ppermute | solution.py:68
  57.6 2.6 %collective-permute-done.3 = bf16[512,384]{1,0:T(8,128)(2,1)S(1)} collective-permute-done((bf16[512,384]{1,0:T(8,128)(2,1)S(1)}, bf16[512,384]{1,0:T(8,128)(2,1)S(1)}, u32[]{:S(2)}, u32[]{:S(2)}) %collective-permute-start.3) | collective-permute-done | bytes 393248 | tf_op jit(solution)/shard_map/ppermute | solution.py:68
  60.2 1.2 add_convert_fusion.2
  61.4 0.7 all-to-all-done.2
  62.1 0.8 copy-done.5
  62.9 6.2 %all-to-all-start.5 = ((bf16[4,128,384]{2,1,0:T(8,128)(2,1)}), bf16[4,128,384]{2,1,0:T(8,128)(2,1)}, u32[]{:S(2)}, u32[]{:S(2)}) async-start(bf16[4,128,384]{2,1,0:T(8,128)(2,1)} %bitcast.14), calls=%async_computation.5 | async-start | bytes 786432 | tf_op jit(solution)/shard_map/all_to_all | solution.py:70
  69.1 1.9 %pad_maximum_fusion = bf16[1024,1152]{1,0:T(8,128)(2,1)S(1)} fusion(bf16[1024,128]{1,0:T(8,128)(2,1)} %param.9, bf16[1024,1024]{1,0:T(8,128)(2,1)} %param.8), kind=kLoop, calls=%fused_computation | loop fusion | flops 4718592 | bytes 4718592 | tf_op jit(solution)/shard_map/concatenate | solution.py:74
  71.0 2.2 %convolution_convert_fusion.1 = bf16[512,384]{1,0:T(8,128)(2,1)} fusion(bf16[512,512]{1,0:T(8,128)(2,1)S(1)} %bitcast.37, bf16[512,384]{1,0:T(8,128)(2,1)} %bitcast.47), kind=kOutput, calls=%fused_computation.2 | convolution fusion | flops 201523200 | bytes 1310720 | tf_op jit(solution)/shard_map/dot_general | solution.py:36
  73.2 3.2 %collective-permute-start.4 = (bf16[512,384]{1,0:T(8,128)(2,1)}, bf16[512,384]{1,0:T(8,128)(2,1)}, u32[]{:S(2)}, u32[]{:S(2)}) collective-permute-start(bf16[512,384]{1,0:T(8,128)(2,1)} %convolution_convert_fusion.1), channel_id=1, source_target_pairs={{0,64},{8,456},{64,0},{72,136},{128,192},{136,72},{192,128},{200,2... | collective-permute-start | bytes 1179656 | tf_op jit(solution)/shard_map/ppermute | solution.py:68
  76.4 0.0 collective-permute-done.2
  76.4 2.3 %add_convert_fusion.3 = bf16[512,384]{1,0:T(8,128)(2,1)} fusion(bf16[512,384]{1,0:T(8,128)(2,1)} %collective-permute-done.2, bf16[512,512]{1,0:T(8,128)(2,1)S(1)} %bitcast.33, bf16[512,384]{1,0:T(8,128)(2,1)} %bitcast.44), kind=kOutput, calls=%fused_computation.12 | convolution fusion | flops 201916416 | bytes 1703936 | tf_op jit(solution)/shard_map/dot_general | solution.py:36
  78.7 1.6 %all-to-all-done.5 = bf16[4,128,384]{2,1,0:T(8,128)(2,1)} async-done(((bf16[4,128,384]{2,1,0:T(8,128)(2,1)}), bf16[4,128,384]{2,1,0:T(8,128)(2,1)}, u32[]{:S(2)}, u32[]{:S(2)}) %all-to-all-start.5) | async-done | bytes 393248 | tf_op jit(solution)/shard_map/all_to_all | solution.py:70
  80.3 5.6 %all-to-all-start.4 = ((bf16[4,128,384]{2,1,0:T(8,128)(2,1)}), bf16[4,128,384]{2,1,0:T(8,128)(2,1)}, u32[]{:S(2)}, u32[]{:S(2)}) async-start(bf16[4,128,384]{2,1,0:T(8,128)(2,1)} %bitcast.13), calls=%async_computation.4 | async-start | bytes 786432 | tf_op jit(solution)/shard_map/all_to_all | solution.py:70
  86.0 1.2 constant_dynamic-slice_fusion.3
  87.2 0.3 copy-done.6
  87.5 1.7 %convolution_convert_fusion = bf16[512,512]{0,1:T(8,128)(2,1)} fusion(bf16[512,1152]{1,0:T(8,128)(2,1)S(1)} %bitcast.52, bf16[512,384]{1,0:T(8,128)(2,1)S(1)} %bitcast.48, bf16[512,384]{1,0:T(8,128)(2,1)S(1)} %bitcast.41, bf16[512,384]{1,0:T(8,128)(2,1)S(1)} %bitcast.45), kind=kOutput, calls=%fused_computation.1 | convolution fusion | flops 607780864 | bytes 2883584 | tf_op jit(solution)/shard_map/dot_general | solution.py:30
  89.2 2.0 %collective-permute-start.1 = (bf16[512,512]{0,1:T(8,128)(2,1)}, bf16[512,512]{0,1:T(8,128)(2,1)}, u32[]{:S(2)}, u32[]{:S(2)}) collective-permute-start(bf16[512,512]{0,1:T(8,128)(2,1)} %convolution_convert_fusion), channel_id=1, source_target_pairs={{0,8},{8,0},{1,9},{9,1},{2,10},{10,2},{3,11},{11,3},{4,12},{12,4},... | collective-permute-start | bytes 1572872 | tf_op jit(solution)/shard_map/ppermute | solution.py:83
  91.2 0.0 collective-permute-done.4
  91.2 2.2 %add_convert_fusion.1 = bf16[512,384]{1,0:T(8,128)(2,1)} fusion(bf16[512,384]{1,0:T(8,128)(2,1)} %collective-permute-done.4, bf16[512,512]{1,0:T(8,128)(2,1)S(1)} %bitcast.34, bf16[512,384]{1,0:T(8,128)(2,1)S(1)} %bitcast.49), kind=kOutput, calls=%fused_computation.8 | convolution fusion | flops 201916416 | bytes 1703936 | tf_op jit(solution)/shard_map/dot_general | solution.py:36
  93.4 3.1 %all-to-all-done.4 = bf16[4,128,384]{2,1,0:T(8,128)(2,1)} async-done(((bf16[4,128,384]{2,1,0:T(8,128)(2,1)}), bf16[4,128,384]{2,1,0:T(8,128)(2,1)}, u32[]{:S(2)}, u32[]{:S(2)}) %all-to-all-start.4) | async-done | bytes 393248 | tf_op jit(solution)/shard_map/all_to_all | solution.py:70
  96.5 4.1 %all-to-all-start.6 = ((bf16[4,128,384]{2,1,0:T(8,128)(2,1)}), bf16[4,128,384]{2,1,0:T(8,128)(2,1)S(1)}, u32[]{:S(2)}, u32[]{:S(2)}) async-start(bf16[4,128,384]{2,1,0:T(8,128)(2,1)} %bitcast.15), calls=%async_computation.6 | async-start | bytes 786432 | tf_op jit(solution)/shard_map/all_to_all | solution.py:70
  100.7 0.0 collective-permute-done.1
  100.7 2.7 %add_convert_fusion = bf16[512,512]{0,1:T(8,128)(2,1)} fusion(bf16[512,512]{0,1:T(8,128)(2,1)} %collective-permute-done.1, bf16[512,1152]{1,0:T(8,128)(2,1)S(1)} %bitcast.51, bf16[512,384]{1,0:T(8,128)(2,1)S(1)} %bitcast.50, bf16[512,384]{1,0:T(8,128)(2,1)S(1)} %bitcast.42, bf16[512,384]{1,0:T(8,128)(2,1)S(1)} %bitcast.46), kind=kOutput, calls=%fused_computation.6 | convolution fusion | flops 608305152 | bytes 3407872 | tf_op jit(solution)/shard_map/dot_general | solution.py:30
  103.4 11.8 %all-to-all-done.6 = bf16[4,128,384]{2,1,0:T(8,128)(2,1)S(1)} async-done(((bf16[4,128,384]{2,1,0:T(8,128)(2,1)}), bf16[4,128,384]{2,1,0:T(8,128)(2,1)S(1)}, u32[]{:S(2)}, u32[]{:S(2)}) %all-to-all-start.6) | async-done | bytes 393248 | tf_op jit(solution)/shard_map/all_to_all | solution.py:70
  115.2 7.5 %all-to-all-start.3 = ((bf16[4,512,128]{1,2,0:T(8,128)(2,1)}), bf16[4,512,128]{1,2,0:T(8,128)(2,1)S(1)}, u32[]{:S(2)}, u32[]{:S(2)}) async-start(bf16[4,512,128]{1,2,0:T(8,128)(2,1)} %bitcast.7), calls=%async_computation.3 | async-start | bytes 1048576 | tf_op jit(solution)/shard_map/all_to_all | solution.py:86
  122.7 1.1 convert_reduce_fusion.1
  123.8 1.1 convert_reduce_fusion.2
  125.0 0.6 slice.21
  125.6 0.8 pad_maximum_fusion.2
  126.4 9.2 %all-to-all-done.3 = bf16[4,512,128]{1,2,0:T(8,128)(2,1)S(1)} async-done(((bf16[4,512,128]{1,2,0:T(8,128)(2,1)}), bf16[4,512,128]{1,2,0:T(8,128)(2,1)S(1)}, u32[]{:S(2)}, u32[]{:S(2)}) %all-to-all-start.3) | async-done | bytes 524320 | tf_op jit(solution)/shard_map/all_to_all | solution.py:86
  135.7 0.1 reduce_sum.39
  135.8 0.8 copy.14
  (26 shorter events, 0.2 us)
Async XLA Ops:
  0.6 31.8 %copy-start.10 = (bf16[64,256]{1,0:T(8,128)(2,1)S(1)}, bf16[64,256]{1,0:T(8,128)(2,1)}, u32[]{:S(2)}) copy-start(bf16[64,256]{1,0:T(8,128)(2,1)} %param.7) | copy-start | bytes 98308
  0.6 33.7 %copy-start.9 = (bf16[512,1024]{1,0:T(8,128)(2,1)S(1)}, bf16[512,1024]{1,0:T(8,128)(2,1)}, u32[]{:S(2)}) copy-start(bf16[512,1024]{1,0:T(8,128)(2,1)} %param.5) | copy-start | bytes 3145732
  27.0 33.3 %copy-start = (bf16[8,64,384]{2,1,0:T(8,128)(2,1)}, bf16[8,64,384]{2,1,0:T(8,128)(2,1)S(1)}, u32[]{:S(2)}) copy-start(bf16[8,64,384]{2,1,0:T(8,128)(2,1)S(1)} %all_to_all.35) | copy-start | bytes 1179652
  27.8 16.5 %all-to-all-start = ((bf16[8,64,384]{2,1,0:T(8,128)(2,1)}), bf16[8,64,384]{2,1,0:T(8,128)(2,1)S(1)}, u32[]{:S(2)}, u32[]{:S(2)}) async-start(bf16[8,64,384]{2,1,0:T(8,128)(2,1)} %broadcast_in_dim.6), calls=%async_computation | async-start | bytes 786432 | tf_op jit(solution)/shard_map/all_to_all | solution.py:26
  32.5 3.1 %collective-permute-start = (bf16[64,128]{1,0:T(8,128)(2,1)S(1)}, bf16[64,128]{1,0:T(8,128)(2,1)S(1)}, u32[]{:S(2)}, u32[]{:S(2)}) collective-permute-start(bf16[64,128]{1,0:T(8,128)(2,1)S(1)} %constant_dynamic-slice_fusion.4), channel_id=1, source_target_pairs={{0,8},{8,0},{1,9},{9,1},{2,10},{10,2},{3,11},{11,3},{4,12},{12,4},... | collective-permute-start | bytes 49160 | tf_op jit(solution)/shard_map/ppermute | solution.py:48
  34.4 1.1 slice-start
  44.3 17.8 %copy-start.2 = (bf16[8,64,384]{2,1,0:T(8,128)(2,1)}, bf16[8,64,384]{2,1,0:T(8,128)(2,1)S(1)}, u32[]{:S(2)}) copy-start(bf16[8,64,384]{2,1,0:T(8,128)(2,1)S(1)} %all-to-all-done) | copy-start | bytes 1179652
  45.2 16.9 %all-to-all-start.2 = ((bf16[8,64,384]{2,1,0:T(8,128)(2,1)}), bf16[8,64,384]{2,1,0:T(8,128)(2,1)S(1)}, u32[]{:S(2)}, u32[]{:S(2)}) async-start(bf16[8,64,384]{2,1,0:T(8,128)(2,1)} %broadcast_in_dim.8), calls=%async_computation.2 | async-start | bytes 786432 | tf_op jit(solution)/shard_map/all_to_all | solution.py:26
  50.6 9.7 %collective-permute-start.3 = (bf16[512,384]{1,0:T(8,128)(2,1)S(1)}, bf16[512,384]{1,0:T(8,128)(2,1)S(1)}, u32[]{:S(2)}, u32[]{:S(2)}) collective-permute-start(bf16[512,384]{1,0:T(8,128)(2,1)S(1)} %convolution_convert_fusion.2), channel_id=1, source_target_pairs={{0,64},{8,456},{64,0},{72,136},{128,192},{136,72},{192,128},{200,2... | collective-permute-start | bytes 1179656 | tf_op jit(solution)/shard_map/ppermute | solution.py:68
  54.1 22.3 %collective-permute-start.2 = (bf16[512,384]{1,0:T(8,128)(2,1)}, bf16[512,384]{1,0:T(8,128)(2,1)}, u32[]{:S(2)}, u32[]{:S(2)}) collective-permute-start(bf16[512,384]{1,0:T(8,128)(2,1)} %convolution_convert_fusion.3), channel_id=1, source_target_pairs={{0,64},{8,456},{64,0},{72,136},{128,192},{136,72},{192,128},{200,2... | collective-permute-start | bytes 1179656 | tf_op jit(solution)/shard_map/ppermute | solution.py:68
  62.1 0.8 copy-start.5
  62.9 17.4 %all-to-all-start.5 = ((bf16[4,128,384]{2,1,0:T(8,128)(2,1)}), bf16[4,128,384]{2,1,0:T(8,128)(2,1)}, u32[]{:S(2)}, u32[]{:S(2)}) async-start(bf16[4,128,384]{2,1,0:T(8,128)(2,1)} %bitcast.14), calls=%async_computation.5 | async-start | bytes 786432 | tf_op jit(solution)/shard_map/all_to_all | solution.py:70
  73.2 18.1 %collective-permute-start.4 = (bf16[512,384]{1,0:T(8,128)(2,1)}, bf16[512,384]{1,0:T(8,128)(2,1)}, u32[]{:S(2)}, u32[]{:S(2)}) collective-permute-start(bf16[512,384]{1,0:T(8,128)(2,1)} %convolution_convert_fusion.1), channel_id=1, source_target_pairs={{0,64},{8,456},{64,0},{72,136},{128,192},{136,72},{192,128},{200,2... | collective-permute-start | bytes 1179656 | tf_op jit(solution)/shard_map/ppermute | solution.py:68
  80.3 16.2 %all-to-all-start.4 = ((bf16[4,128,384]{2,1,0:T(8,128)(2,1)}), bf16[4,128,384]{2,1,0:T(8,128)(2,1)}, u32[]{:S(2)}, u32[]{:S(2)}) async-start(bf16[4,128,384]{2,1,0:T(8,128)(2,1)} %bitcast.13), calls=%async_computation.4 | async-start | bytes 786432 | tf_op jit(solution)/shard_map/all_to_all | solution.py:70
  85.9 1.2 copy-start.1
  85.9 1.2 copy-start.3
  86.0 1.6 %copy-start.6 = (bf16[8,64,384]{2,1,0:T(8,128)(2,1)S(1)}, bf16[8,64,384]{2,1,0:T(8,128)(2,1)}, u32[]{:S(2)}) copy-start(bf16[8,64,384]{2,1,0:T(8,128)(2,1)} %copy-done.5) | copy-start | bytes 1179652
  89.2 11.5 %copy-start.4 = (bf16[8,64,384]{2,1,0:T(8,128)(2,1)S(1)}, bf16[8,64,384]{2,1,0:T(8,128)(2,1)}, u32[]{:S(2)}) copy-start(bf16[8,64,384]{2,1,0:T(8,128)(2,1)} %copy-done.2) | copy-start | bytes 1179652
  89.2 11.5 %copy-start.7 = (bf16[8,64,384]{2,1,0:T(8,128)(2,1)S(1)}, bf16[8,64,384]{2,1,0:T(8,128)(2,1)}, u32[]{:S(2)}) copy-start(bf16[8,64,384]{2,1,0:T(8,128)(2,1)} %copy-done.5) | copy-start | bytes 1179652
  89.2 11.5 %copy-start.8 = (bf16[4,1,128,1152]{3,2,1,0:T(8,128)(2,1)S(1)}, bf16[4,1,128,1152]{3,2,1,0:T(8,128)(2,1)}, u32[]{:S(2)}) copy-start(bf16[4,1,128,1152]{3,2,1,0:T(8,128)(2,1)} %get-tuple-element.6) | copy-start | bytes 3538948
  89.2 11.5 %collective-permute-start.1 = (bf16[512,512]{0,1:T(8,128)(2,1)}, bf16[512,512]{0,1:T(8,128)(2,1)}, u32[]{:S(2)}, u32[]{:S(2)}) collective-permute-start(bf16[512,512]{0,1:T(8,128)(2,1)} %convolution_convert_fusion), channel_id=1, source_target_pairs={{0,8},{8,0},{1,9},{9,1},{2,10},{10,2},{3,11},{11,3},{4,12},{12,4},... | collective-permute-start | bytes 1572872 | tf_op jit(solution)/shard_map/ppermute | solution.py:83
  96.5 18.7 %all-to-all-start.6 = ((bf16[4,128,384]{2,1,0:T(8,128)(2,1)}), bf16[4,128,384]{2,1,0:T(8,128)(2,1)S(1)}, u32[]{:S(2)}, u32[]{:S(2)}) async-start(bf16[4,128,384]{2,1,0:T(8,128)(2,1)} %bitcast.15), calls=%async_computation.6 | async-start | bytes 786432 | tf_op jit(solution)/shard_map/all_to_all | solution.py:70
  115.2 20.5 %all-to-all-start.3 = ((bf16[4,512,128]{1,2,0:T(8,128)(2,1)}), bf16[4,512,128]{1,2,0:T(8,128)(2,1)S(1)}, u32[]{:S(2)}, u32[]{:S(2)}) async-start(bf16[4,512,128]{1,2,0:T(8,128)(2,1)} %bitcast.7), calls=%async_computation.3 | async-start | bytes 1048576 | tf_op jit(solution)/shard_map/all_to_all | solution.py:86

commit v3 on v2

v3 whole, which is shorter than its diff:
```python
import jax
import jax.numpy as jnp
from jax import lax
from jax.sharding import Mesh
from jax.sharding import PartitionSpec as P

SWAP = [(0, 1), (1, 0)]
WID = ("x", "zhi")
TOK = ("th", "tl")
HEAD = ("zlo", "core")


def neighbour(at):
    y, core = divmod(at, 2)
    other = y ^ 1 if core == 0 else (y + (1 if y % 2 else -1)) % 8
    return other * 2 + core


NEIGHBOUR = [(i, neighbour(i)) for i in range(16)]


def spread(rows):
    n = lax.axis_size("x")
    copies = jnp.broadcast_to(rows[None], (n, *rows.shape))
    return lax.all_to_all(copies, "x", 0, 0, tiled=True)


def contract_last(left, right):
    return lax.dot_general(
        left, right, (((1,), (1,)), ((), ())), preferred_element_type=jnp.float32
    )


def matmul(left, right):
    return jnp.dot(left, right, preferred_element_type=jnp.float32)


def halves(rows, which, n):
    pairs = rows.reshape(n, 2, rows.shape[0] // (2 * n), rows.shape[1])
    keep = lax.dynamic_index_in_dim(pairs, which, 1, keepdims=False)
    give = lax.dynamic_index_in_dim(pairs, 1 - which, 1, keepdims=False)
    return keep.reshape(-1, rows.shape[1]), give.reshape(-1, rows.shape[1])


def local(inputs, q_grad, key_value_share_gradient, q_weight, key_value_weight):
    head_dim = key_value_weight.shape[1]
    q_columns = q_grad.shape[1]
    core = lax.axis_index("core")
    tl = lax.axis_index("tl")
    zhi = lax.axis_index("zhi")
    n_zlo, n_th = lax.axis_size("zlo"), lax.axis_size("th")

    share = key_value_share_gradient
    outgoing = lax.dynamic_slice_in_dim(share, (1 - core) * head_dim, head_dim, 1)
    incoming = lax.ppermute(outgoing, "core", SWAP)
    own_part = lax.dynamic_slice_in_dim(share, core * head_dim, head_dim, 1)
    kv_rows = (own_part.astype(jnp.float32) + incoming.astype(jnp.float32)).astype(jnp.bfloat16)
    mine = jnp.concatenate([q_grad, kv_rows], axis=1)

    far = lax.ppermute(mine, "zhi", SWAP)
    near_all = spread(mine)
    far_all = spread(far)
    first = jnp.where(zhi == 0, near_all, far_all)
    second = jnp.where(zhi == 0, far_all, near_all)
    combined = jnp.stack([first, second], axis=1).reshape(-1, mine.shape[1])

    keep_in, give_in = halves(inputs.T, tl, n_th)
    given = matmul(give_in, combined).astype(jnp.bfloat16)
    got = lax.ppermute(given, (*TOK, "core"), NEIGHBOUR)

    keep_q, give_q = halves(q_weight, core, n_zlo)
    keep_kv, give_kv = halves(key_value_weight, core, n_zlo)
    q_rows, kv_rows = combined[:, :q_columns], combined[:, q_columns:]

    def terms(q_part, kv_part):
        return contract_last(q_part, q_rows) + contract_last(kv_part, kv_rows)

    core_got = lax.ppermute(terms(give_q, give_kv).astype(jnp.bfloat16), "core", SWAP)
    pair = (terms(keep_q, keep_kv) + core_got.astype(jnp.float32)).astype(jnp.bfloat16)
    pieces = lax.all_to_all(pair.reshape(n_zlo, -1, pair.shape[1]), "zlo", 0, 0, tiled=True)
    input_grad = jnp.sum(pieces.astype(jnp.float32), axis=0).T.astype(jnp.bfloat16)

    pair = (matmul(keep_in, combined) + got.astype(jnp.float32)).astype(jnp.bfloat16)
    pieces = lax.all_to_all(pair.reshape(n_th, -1, pair.shape[1]), "th", 0, 0, tiled=True)
    total = jnp.sum(pieces.astype(jnp.float32), axis=0)
    return (input_grad, total[:, :q_columns], total[:, q_columns:])


def solution(mesh):
    fine = Mesh(
        mesh.devices.reshape(4, 2, 4, 2, 4, 2), ("th", "tl", "zlo", "core", "x", "zhi")
    )
    return jax.shard_map(
        local,
        mesh=fine,
        in_specs=(
            P(TOK, WID),
            P((*TOK, *WID), HEAD),
            P((*TOK, *WID), HEAD),
            P(WID, HEAD),
            P(WID, HEAD),
        ),
        out_specs=(P(TOK, (*WID, *HEAD)), P((*WID, *TOK), HEAD), P((*WID, *TOK), HEAD)),
        check_vma=False,
    )
```

time: 138 us -> 113 us (0.82)
  the two profiles are of different devices: /device:TPU:8 before, /device:TPU:2 now
where the time goes in v3:
time: 113 us; the launch traced here: 112 us
  waiting for transfers between devices  52.1 us (46%)
  starting transfers between devices  40 us (35%)
  local copies, waits for them, and re-layouts  10.5 us (9%)
  matrix products  6.64 us (6%)
  other arithmetic  2.1 us (2%)
    all_to_all x1, waiting for transfers between devices, local(): lax.all_to_all(pair.reshape(n_th, -1, pair.shape[1]), 'th', 0, 0, tiled=T...  29.4 us
    all_to_all x2, starting transfers between devices, spread(): return lax.all_to_all(copies, 'x', 0, 0, tiled=True)  14.1 us
    all_to_all x1, starting transfers between devices, local(): lax.all_to_all(pair.reshape(n_zlo, -1, pair.shape[1]), 'zlo', 0, 0, tiled...  7.79 us
    ppermute x1, waiting for transfers between devices, local(): got = lax.ppermute(given, (*TOK, 'core'), NEIGHBOUR)  6.69 us
    ppermute x1, starting transfers between devices, local(): far = lax.ppermute(mine, 'zhi', SWAP)  6.51 us
    all_to_all x1, waiting for transfers between devices, local(): lax.all_to_all(pair.reshape(n_zlo, -1, pair.shape[1]), 'zlo', 0, 0, tiled...  6.49 us
    all_to_all x1, starting transfers between devices, local(): lax.all_to_all(pair.reshape(n_th, -1, pair.shape[1]), 'th', 0, 0, tiled=T...  5.77 us
    ppermute x1, waiting for transfers between devices, local(): far = lax.ppermute(mine, 'zhi', SWAP)  5.14 us
  transfers between devices with their start and end apart: 8, of which 6 were waited for; matrix products, arithmetic and copies ran while one was open for 9% of the time, Pallas kernels for 0%

profile of v3, /device:TPU:2, one launch (start us, length us, event | category | flops | bytes accessed | tf_op | source)
XLA Modules:
  0.0 112.1 jit_solution(4091610853607588073)
XLA Ops:
  0.6 0.7 constant_dynamic-slice_fusion.5
  1.4 1.9 %collective-permute-start = (bf16[64,128]{1,0:T(8,128)(2,1)S(1)}, bf16[64,128]{1,0:T(8,128)(2,1)S(1)}, u32[]{:S(2)}, u32[]{:S(2)}) collective-permute-start(bf16[64,128]{1,0:T(8,128)(2,1)S(1)} %constant_dynamic-slice_fusion.5), channel_id=1, source_target_pairs={{0,8},{8,0},{1,9},{9,1},{2,10},{10,2},{3,11},{11,3},{4,12},{12,4},... | collective-permute-start | bytes 49160 | tf_op jit(solution)/shard_map/ppermute | solution.py:55
  3.3 1.1 %collective-permute-done = bf16[64,128]{1,0:T(8,128)(2,1)S(1)} collective-permute-done((bf16[64,128]{1,0:T(8,128)(2,1)S(1)}, bf16[64,128]{1,0:T(8,128)(2,1)S(1)}, u32[]{:S(2)}, u32[]{:S(2)}) %collective-permute-start) | collective-permute-done | bytes 16416 | tf_op jit(solution)/shard_map/ppermute | solution.py:55
  4.4 0.7 add_convert_fusion.2
  5.2 0.9 pad_maximum_fusion.1
  6.1 0.9 broadcast_in_dim.4
  6.9 9.4 %all-to-all-start = ((bf16[4,64,1152]{2,1,0:T(8,128)(2,1)}), bf16[4,64,1152]{2,1,0:T(8,128)(2,1)S(1)}, u32[]{:S(2)}, u32[]{:S(2)}) async-start(bf16[4,64,1152]{2,1,0:T(8,128)(2,1)} %broadcast_in_dim.4), calls=%async_computation | async-start | bytes 1179648 | tf_op jit(solution)/shard_map/all_to_all | solution.py:25
  16.3 0.0 copy-start.2
  16.3 6.5 %collective-permute-start.1 = (bf16[64,1152]{1,0:T(8,128)(2,1)S(1)}, bf16[64,1152]{1,0:T(8,128)(2,1)S(1)}, u32[]{:S(2)}, u32[]{:S(2)}) collective-permute-start(bf16[64,1152]{1,0:T(8,128)(2,1)S(1)} %pad_maximum_fusion.1), channel_id=1, source_target_pairs={{0,1},{1,0},{2,3},{3,2},{4,5},{5,4},{6,7},{7,6},{8,9},{9,8},{10,11... | collective-permute-start | bytes 442376 | tf_op jit(solution)/shard_map/ppermute | solution.py:60
  22.8 5.1 %collective-permute-done.1 = bf16[64,1152]{1,0:T(8,128)(2,1)S(1)} collective-permute-done((bf16[64,1152]{1,0:T(8,128)(2,1)S(1)}, bf16[64,1152]{1,0:T(8,128)(2,1)S(1)}, u32[]{:S(2)}, u32[]{:S(2)}) %collective-permute-start.1) | collective-permute-done | bytes 147488 | tf_op jit(solution)/shard_map/ppermute | solution.py:60
  27.9 0.0 all-to-all-done
  28.0 0.9 broadcast_in_dim.5
  28.8 4.8 %all-to-all-start.1 = ((bf16[4,64,1152]{2,1,0:T(8,128)(2,1)}), bf16[4,64,1152]{2,1,0:T(8,128)(2,1)S(1)}, u32[]{:S(2)}, u32[]{:S(2)}) async-start(bf16[4,64,1152]{2,1,0:T(8,128)(2,1)} %broadcast_in_dim.5), calls=%async_computation.1 | async-start | bytes 1179648 | tf_op jit(solution)/shard_map/all_to_all | solution.py:25
  33.6 0.0 copy-done.2
  33.6 0.5 copy.12
  34.2 1.0 constant_dynamic-slice_fusion.4
  35.2 0.0 copy-start
  35.2 1.1 %constant_dynamic-slice_fusion = (bf16[4,1,128,512]{3,2,1,0:T(8,128)(2,1)}, bf16[4,1,128,512]{3,2,1,0:T(8,128)(2,1)}) fusion(bf16[4,2,128,512]{3,2,1,0:T(8,128)(2,1)S(1)} %bitcast.29, s32[]{:T(128)S(6)} %select_n.43, s32[]{:T(128)S(6)} %select_n.42), kind=kLoop, calls=%fused_computation.18 | loop fusion | bytes 2097160 | tf_op jit(solution)/shard_map/jit(dynamic_index_in_dim)/dynamic_slice | solution.py:41
  36.3 0.8 copy-done
  37.2 1.1 %constant_dynamic-slice_fusion.6 = (bf16[4,1,128,1024]{3,2,1,0:T(8,128)(2,1)S(1)}, bf16[4,1,128,1024]{3,2,1,0:T(8,128)(2,1)}) fusion(bf16[4,2,128,1024]{3,2,1,0:T(8,128)(2,1)S(1)} %bitcast.30, s32[]{:T(128)S(6)} %select_n.35, s32[]{:T(128)S(6)} %select_n.41), kind=kLoop, calls=%fused_computation.24 | loop fusion | bytes 4194312 | tf_op jit(solution)/shard_map/jit(dynamic_index_in_dim)/dynamic_slice | solution.py:40
  38.3 3.2 %all-to-all-done.1 = bf16[4,64,1152]{2,1,0:T(8,128)(2,1)S(1)} async-done(((bf16[4,64,1152]{2,1,0:T(8,128)(2,1)}), bf16[4,64,1152]{2,1,0:T(8,128)(2,1)S(1)}, u32[]{:S(2)}, u32[]{:S(2)}) %all-to-all-start.1) | async-done | bytes 589856 | tf_op jit(solution)/shard_map/all_to_all | solution.py:25
  41.5 0.1 select_bitcast_fusion.1
  41.6 0.0 copy-start.1
  41.6 0.1 pad_maximum_fusion
  41.8 1.1 copy-done.1
  42.9 0.7 fusion.1
  43.6 0.0 copy-start.4
  43.6 0.3 fusion
  43.9 1.9 %collective-permute-start.2 = (bf16[512,512]{1,0:T(8,128)(2,1)S(1)}, bf16[512,512]{1,0:T(8,128)(2,1)S(1)}, u32[]{:S(2)}, u32[]{:S(2)}) collective-permute-start(bf16[512,512]{1,0:T(8,128)(2,1)S(1)} %fusion), channel_id=1, source_target_pairs={{0,8},{8,0},{1,9},{9,1},{2,10},{10,2},{3,11},{11,3},{4,12},{12,4},... | collective-permute-start | bytes 1572872 | tf_op jit(solution)/shard_map/ppermute | solution.py:78
  45.9 0.0 copy-done.4
  45.9 1.9 %convolution_convert_fusion = bf16[512,1152]{1,0:T(8,128)(2,1)} fusion(bf16[512,512]{1,0:T(8,128)(2,1)S(1)} %bitcast.43, bf16[512,1152]{1,0:T(8,128)(2,1)S(1)} %bitcast.33), kind=kOutput, calls=%fused_computation | convolution fusion | flops 604569600 | bytes 2883584 | tf_op jit(solution)/shard_map/dot_general | solution.py:35
  47.8 1.9 %collective-permute-start.3 = (bf16[512,1152]{1,0:T(8,128)(2,1)}, bf16[512,1152]{1,0:T(8,128)(2,1)S(1)}, u32[]{:S(2)}, u32[]{:S(2)}) collective-permute-start(bf16[512,1152]{1,0:T(8,128)(2,1)} %convolution_convert_fusion), channel_id=1, source_target_pairs={{0,64},{8,456},{64,0},{72,136},{128,192},{136,72},{192,128},{200,2... | collective-permute-start | bytes 3538952 | tf_op jit(solution)/shard_map/ppermute | solution.py:69
  49.7 0.7 fusion.3
  50.4 0.0 collective-permute-done.2
  50.5 0.0 copy-start.3
  50.5 1.1 add_convert_fusion.1
  51.6 7.8 %all-to-all-start.2 = ((bf16[4,128,512]{2,1,0:T(8,128)(2,1)}), bf16[4,128,512]{2,1,0:T(8,128)(2,1)S(1)}, u32[]{:S(2)}, u32[]{:S(2)}) async-start(bf16[4,128,512]{2,1,0:T(8,128)(2,1)} %bitcast.10), calls=%async_computation.2 | async-start | bytes 1048576 | tf_op jit(solution)/shard_map/all_to_all | solution.py:80
  59.4 6.7 %collective-permute-done.3 = bf16[512,1152]{1,0:T(8,128)(2,1)S(1)} collective-permute-done((bf16[512,1152]{1,0:T(8,128)(2,1)}, bf16[512,1152]{1,0:T(8,128)(2,1)S(1)}, u32[]{:S(2)}, u32[]{:S(2)}) %collective-permute-start.3) | collective-permute-done | bytes 1179680 | tf_op jit(solution)/shard_map/ppermute | solution.py:69
  66.0 0.0 copy-done.3
  66.0 1.9 %add_convert_fusion = bf16[512,1152]{1,0:T(8,128)(2,1)} fusion(bf16[512,1152]{1,0:T(8,128)(2,1)S(1)} %collective-permute-done.3, bf16[512,512]{1,0:T(8,128)(2,1)S(1)} %bitcast.42, bf16[512,1152]{1,0:T(8,128)(2,1)S(1)} %bitcast.36), kind=kOutput, calls=%fused_computation.2 | convolution fusion | flops 605749248 | bytes 4063232 | tf_op jit(solution)/shard_map/dot_general | solution.py:35
  67.9 6.5 %all-to-all-done.2 = bf16[4,128,512]{2,1,0:T(8,128)(2,1)S(1)} async-done(((bf16[4,128,512]{2,1,0:T(8,128)(2,1)}), bf16[4,128,512]{2,1,0:T(8,128)(2,1)S(1)}, u32[]{:S(2)}, u32[]{:S(2)}) %all-to-all-start.2) | async-done | bytes 524320 | tf_op jit(solution)/shard_map/all_to_all | solution.py:80
  74.4 5.8 %all-to-all-start.3 = ((bf16[4,128,1152]{2,1,0:T(8,128)(2,1)}), bf16[4,128,1152]{2,1,0:T(8,128)(2,1)S(1)}, u32[]{:S(2)}, u32[]{:S(2)}) async-start(bf16[4,128,1152]{2,1,0:T(8,128)(2,1)} %bitcast.17), calls=%async_computation.3 | async-start | bytes 2359296 | tf_op jit(solution)/shard_map/all_to_all | solution.py:84
  80.2 0.1 reduce_sum.21
  80.3 0.8 copy.13
  81.0 29.4 %all-to-all-done.3 = bf16[4,128,1152]{2,1,0:T(8,128)(2,1)S(1)} async-done(((bf16[4,128,1152]{2,1,0:T(8,128)(2,1)}), bf16[4,128,1152]{2,1,0:T(8,128)(2,1)S(1)}, u32[]{:S(2)}, u32[]{:S(2)}) %all-to-all-start.3) | async-done | bytes 1179680 | tf_op jit(solution)/shard_map/all_to_all | solution.py:84
  110.4 0.2 convert_reduce_fusion
  110.6 0.8 slice.18
  111.4 0.6 slice.19
Async XLA Ops:
  1.4 3.1 %collective-permute-start = (bf16[64,128]{1,0:T(8,128)(2,1)S(1)}, bf16[64,128]{1,0:T(8,128)(2,1)S(1)}, u32[]{:S(2)}, u32[]{:S(2)}) collective-permute-start(bf16[64,128]{1,0:T(8,128)(2,1)S(1)} %constant_dynamic-slice_fusion.5), channel_id=1, source_target_pairs={{0,8},{8,0},{1,9},{9,1},{2,10},{10,2},{3,11},{11,3},{4,12},{12,4},... | collective-permute-start | bytes 49160 | tf_op jit(solution)/shard_map/ppermute | solution.py:55
  6.9 21.0 %all-to-all-start = ((bf16[4,64,1152]{2,1,0:T(8,128)(2,1)}), bf16[4,64,1152]{2,1,0:T(8,128)(2,1)S(1)}, u32[]{:S(2)}, u32[]{:S(2)}) async-start(bf16[4,64,1152]{2,1,0:T(8,128)(2,1)} %broadcast_in_dim.4), calls=%async_computation | async-start | bytes 1179648 | tf_op jit(solution)/shard_map/all_to_all | solution.py:25
  16.3 17.4 %copy-start.2 = (bf16[512,1024]{1,0:T(8,128)(2,1)S(1)}, bf16[512,1024]{1,0:T(8,128)(2,1)}, u32[]{:S(2)}) copy-start(bf16[512,1024]{1,0:T(8,128)(2,1)} %param.5) | copy-start | bytes 3145732
  16.3 11.7 %collective-permute-start.1 = (bf16[64,1152]{1,0:T(8,128)(2,1)S(1)}, bf16[64,1152]{1,0:T(8,128)(2,1)S(1)}, u32[]{:S(2)}, u32[]{:S(2)}) collective-permute-start(bf16[64,1152]{1,0:T(8,128)(2,1)S(1)} %pad_maximum_fusion.1), channel_id=1, source_target_pairs={{0,1},{1,0},{2,3},{3,2},{4,5},{5,4},{6,7},{7,6},{8,9},{9,8},{10,11... | collective-permute-start | bytes 442376 | tf_op jit(solution)/shard_map/ppermute | solution.py:60
  28.8 12.7 %all-to-all-start.1 = ((bf16[4,64,1152]{2,1,0:T(8,128)(2,1)}), bf16[4,64,1152]{2,1,0:T(8,128)(2,1)S(1)}, u32[]{:S(2)}, u32[]{:S(2)}) async-start(bf16[4,64,1152]{2,1,0:T(8,128)(2,1)} %broadcast_in_dim.5), calls=%async_computation.1 | async-start | bytes 1179648 | tf_op jit(solution)/shard_map/all_to_all | solution.py:25
  35.2 2.0 %copy-start = (bf16[1024,1024]{1,0:T(8,128)(2,1)S(1)}, bf16[1024,1024]{1,0:T(8,128)(2,1)}, u32[]{:S(2)}) copy-start(bf16[1024,1024]{1,0:T(8,128)(2,1)} %param.8) | copy-start | bytes 6291460
  41.6 1.2 %copy-start.1 = (bf16[4,1,128,1024]{3,2,1,0:T(8,128)(2,1)S(1)}, bf16[4,1,128,1024]{3,2,1,0:T(8,128)(2,1)}, u32[]{:S(2)}) copy-start(bf16[4,1,128,1024]{3,2,1,0:T(8,128)(2,1)} %get-tuple-element.7) | copy-start | bytes 3145732
  43.6 2.2 %copy-start.4 = (bf16[4,1,128,512]{3,2,1,0:T(8,128)(2,1)S(1)}, bf16[4,1,128,512]{3,2,1,0:T(8,128)(2,1)}, u32[]{:S(2)}) copy-start(bf16[4,1,128,512]{3,2,1,0:T(8,128)(2,1)} %get-tuple-element.10) | copy-start | bytes 1572868
  43.9 6.5 %collective-permute-start.2 = (bf16[512,512]{1,0:T(8,128)(2,1)S(1)}, bf16[512,512]{1,0:T(8,128)(2,1)S(1)}, u32[]{:S(2)}, u32[]{:S(2)}) collective-permute-start(bf16[512,512]{1,0:T(8,128)(2,1)S(1)} %fusion), channel_id=1, source_target_pairs={{0,8},{8,0},{1,9},{9,1},{2,10},{10,2},{3,11},{11,3},{4,12},{12,4},... | collective-permute-start | bytes 1572872 | tf_op jit(solution)/shard_map/ppermute | solution.py:78
  47.8 18.3 %collective-permute-start.3 = (bf16[512,1152]{1,0:T(8,128)(2,1)}, bf16[512,1152]{1,0:T(8,128)(2,1)S(1)}, u32[]{:S(2)}, u32[]{:S(2)}) collective-permute-start(bf16[512,1152]{1,0:T(8,128)(2,1)} %convolution_convert_fusion), channel_id=1, source_target_pairs={{0,64},{8,456},{64,0},{72,136},{128,192},{136,72},{192,128},{200,2... | collective-permute-start | bytes 3538952 | tf_op jit(solution)/shard_map/ppermute | solution.py:69
  50.5 15.6 %copy-start.3 = (bf16[4,1,128,512]{3,2,1,0:T(8,128)(2,1)S(1)}, bf16[4,1,128,512]{3,2,1,0:T(8,128)(2,1)}, u32[]{:S(2)}) copy-start(bf16[4,1,128,512]{3,2,1,0:T(8,128)(2,1)} %get-tuple-element.11) | copy-start | bytes 1572868
  51.6 22.9 %all-to-all-start.2 = ((bf16[4,128,512]{2,1,0:T(8,128)(2,1)}), bf16[4,128,512]{2,1,0:T(8,128)(2,1)S(1)}, u32[]{:S(2)}, u32[]{:S(2)}) async-start(bf16[4,128,512]{2,1,0:T(8,128)(2,1)} %bitcast.10), calls=%async_computation.2 | async-start | bytes 1048576 | tf_op jit(solution)/shard_map/all_to_all | solution.py:80
  74.4 36.0 %all-to-all-start.3 = ((bf16[4,128,1152]{2,1,0:T(8,128)(2,1)}), bf16[4,128,1152]{2,1,0:T(8,128)(2,1)S(1)}, u32[]{:S(2)}, u32[]{:S(2)}) async-start(bf16[4,128,1152]{2,1,0:T(8,128)(2,1)} %bitcast.17), calls=%async_computation.3 | async-start | bytes 2359296 | tf_op jit(solution)/shard_map/all_to_all | solution.py:84

commit v4 on v3

v4 whole, which is shorter than its diff:
```python
import functools

import jax
import jax.numpy as jnp
from jax import lax
from jax.experimental import pallas as pl
from jax.experimental.pallas import tpu as pltpu
from jax.sharding import Mesh
from jax.sharding import PartitionSpec as P

SWAP = [(0, 1), (1, 0)]
WID = ("x", "zhi")
TOK = ("th", "tl")
HEAD = ("zlo", "core")
N_Y = 8
N_PAIRS = 4
VMEM_LIMIT = 48 * 2**20


def side(y, core):
    return 2 * ((y + core) % 2) - 1


def moved(step):
    return [
        (y * 2 + core, (y + step(y, core)) % N_Y * 2 + core)
        for y in range(N_Y)
        for core in range(2)
    ]


def spread(rows):
    n = lax.axis_size("x")
    copies = jnp.broadcast_to(rows[None], (n, *rows.shape))
    return lax.all_to_all(copies, "x", 0, 0, tiled=True)


def dot(left, right, dims):
    return lax.dot_general(left, right, ((dims[:1], dims[1:]), ((), ())), preferred_element_type=jnp.float32)


def weight_body(blocks, x_ref, g_ref, *refs):
    for r in range(N_PAIRS):
        columns = x_ref[:, pl.ds(pl.multiple_of(blocks[r] * 128, 128), 128)]
        term = dot(columns, g_ref[...], (0, 0))
        if len(refs) == 1:
            refs[0][r] = term.astype(jnp.bfloat16)
        else:
            refs[1 + r][...] = (term + refs[0][r].astype(jnp.float32)).astype(jnp.bfloat16)


def weight_terms(blocks, x, g, got=None):
    extra = () if got is None else (got,)
    vmem = pl.BlockSpec(memory_space=pltpu.VMEM)
    if got is None:
        shapes = [jax.ShapeDtypeStruct((N_PAIRS, 128, g.shape[1]), jnp.bfloat16)]
    else:
        shapes = [jax.ShapeDtypeStruct((128, g.shape[1]), jnp.bfloat16)] * N_PAIRS
    return pl.pallas_call(
        weight_body,
        out_shape=shapes,
        in_specs=[pl.BlockSpec(memory_space=pltpu.SMEM)] + [vmem] * (2 + len(extra)),
        out_specs=[vmem] * len(shapes),
        compiler_params=pltpu.CompilerParams(vmem_limit_bytes=VMEM_LIMIT),
        cost_estimate=pl.CostEstimate(
            flops=2 * 512 * 512 * g.shape[1], bytes_accessed=4 * 2**20, transcendentals=0
        ),
    )(blocks, x, g, *extra)


def input_body(which, g_ref, wq_ref, wkv_ref, *refs):
    out = refs[-1]
    n_q = wq_ref.shape[-1]
    term = dot(g_ref[:, :n_q], wq_ref[0], (1, 1))
    term = term + dot(g_ref[:, n_q:], wkv_ref[0], (1, 1))
    if len(refs) > 1:
        term = term + refs[0][0].astype(jnp.float32)
    out[0] = term.astype(out.dtype)


def input_terms(which, g, wq, wkv, got=None):
    n_q, n_kv = wq.shape[1], wkv.shape[1]
    n = wq.shape[0] // 256
    rows = g.shape[0]
    whole = lambda r, which: (0, 0)
    pick = lambda r, which: (2 * r + which[0], 0, 0)
    mine = lambda r, which: (r, 0, 0)
    extra = () if got is None else (got,)
    return pl.pallas_call(
        input_body,
        grid_spec=pltpu.PrefetchScalarGridSpec(
            num_scalar_prefetch=1,
            grid=(n,),
            in_specs=[
                pl.BlockSpec(g.shape, whole),
                pl.BlockSpec((1, 128, n_q), pick),
                pl.BlockSpec((1, 128, n_kv), pick),
            ]
            + [pl.BlockSpec((1, rows, 128), mine)] * len(extra),
            out_specs=pl.BlockSpec((1, rows, 128), mine),
        ),
        out_shape=jax.ShapeDtypeStruct((n, rows, 128), jnp.bfloat16),
        compiler_params=pltpu.CompilerParams(vmem_limit_bytes=VMEM_LIMIT),
        cost_estimate=pl.CostEstimate(
            flops=2 * 512 * 512 * 1152, bytes_accessed=4 * 2**20, transcendentals=0
        ),
    )(which, g, wq.reshape(-1, 128, n_q), wkv.reshape(-1, 128, n_kv), *extra)


def local(inputs, q_grad, key_value_share_gradient, q_weight, key_value_weight):
    head_dim = key_value_weight.shape[1]
    q_columns = q_grad.shape[1]
    core = lax.axis_index("core")
    zhi = lax.axis_index("zhi")
    y = lax.axis_index(TOK)

    share = key_value_share_gradient
    outgoing = lax.dynamic_slice_in_dim(share, (1 - core) * head_dim, head_dim, 1)
    incoming = lax.ppermute(outgoing, "core", SWAP)
    own_part = lax.dynamic_slice_in_dim(share, core * head_dim, head_dim, 1)
    kv_rows = (own_part.astype(jnp.float32) + incoming.astype(jnp.float32)).astype(jnp.bfloat16)
    mine = jnp.concatenate([q_grad, kv_rows], axis=1)

    sigma = side(y, core)
    steps = jnp.arange(N_PAIRS, dtype=jnp.int32)
    keep_blocks = (y + sigma * steps) % N_Y
    give_blocks = (y - sigma * (1 + steps)) % N_Y
    give_which = (1 - core).reshape(1)
    keep_which = core.reshape(1)

    far = lax.ppermute(mine, "zhi", SWAP)
    near_all = spread(mine)
    far, near_all, near_first, keep_blocks, give_blocks, keep_which, give_which = (
        lax.optimization_barrier(
            (far, near_all, zhi == 0, keep_blocks, give_blocks, keep_which, give_which)
        )
    )
    far_all = spread(far)
    first = jnp.where(near_first, near_all, far_all)
    second = jnp.where(near_first, far_all, near_all)
    combined = jnp.stack([first, second], axis=1).reshape(-1, mine.shape[1])

    (given,) = weight_terms(give_blocks, inputs, combined)
    got = lax.ppermute(given, (*TOK, "core"), moved(lambda y, core: -side(y, core)))

    core_got = lax.ppermute(input_terms(give_which, combined, q_weight, key_value_weight), "core", SWAP)
    pieces = input_terms(keep_which, combined, q_weight, key_value_weight, core_got)
    pieces = lax.all_to_all(pieces, "zlo", 0, 0, tiled=True)
    input_grad = jnp.sum(pieces.astype(jnp.float32), axis=0).astype(jnp.bfloat16)

    kept = weight_terms(keep_blocks, inputs, combined, got)
    pieces = [
        lax.ppermute(kept[r], (*TOK, "core"), moved(lambda y, core: r * side(y, core)))
        for r in range(N_PAIRS - 1, 0, -1)
    ]

    def total(columns):
        return sum(piece[:, columns].astype(jnp.float32) for piece in [kept[0], *pieces])

    return (input_grad, total(slice(0, q_columns)), total(slice(q_columns, None)))


def solution(mesh):
    fine = Mesh(
        mesh.devices.reshape(4, 2, 4, 2, 4, 2), ("th", "tl", "zlo", "core", "x", "zhi")
    )
    return jax.shard_map(
        local,
        mesh=fine,
        in_specs=(
            P(TOK, WID),
            P((*TOK, *WID), HEAD),
            P((*TOK, *WID), HEAD),
            P(WID, HEAD),
            P(WID, HEAD),
        ),
        out_specs=(P(TOK, (*WID, *HEAD)), P((*WID, *TOK), HEAD), P((*WID, *TOK), HEAD)),
        check_vma=False,
    )
```

time: 113 us -> 98.1 us (0.87)
  the two profiles are of different devices: /device:TPU:2 before, /device:TPU:144 now
where the time goes in v4:
time: 98.1 us; the launch traced here: 97.4 us
  starting transfers between devices  36.6 us (37%)
  waiting for transfers between devices  25.6 us (26%)
  blocking collectives  14.6 us (15%)
  Pallas kernels  9.35 us (10%)
  other arithmetic  6.97 us (7%)
  local copies, waits for them, and re-layouts  3.44 us (4%)
    all_to_all x1, blocking collectives, spread(): return lax.all_to_all(copies, 'x', 0, 0, tiled=True)  14.6 us
    ppermute x3, waiting for transfers between devices, local(): lax.ppermute(kept[r], (*TOK, 'core'), moved(lambda y, core: r * side(y, c...  13.4 us
    ppermute x3, starting transfers between devices, local(): lax.ppermute(kept[r], (*TOK, 'core'), moved(lambda y, core: r * side(y, c...  11.8 us
    ppermute x1, starting transfers between devices, local(): far = lax.ppermute(mine, 'zhi', SWAP)  9.11 us
    ppermute x1, waiting for transfers between devices, local(): far = lax.ppermute(mine, 'zhi', SWAP)  7.08 us
    pallas_call x2, Pallas kernels, input_terms(): pl.pallas_call(input_body, grid_spec=pltpu.PrefetchScalarGridSpec(num_sca...  4.7 us
    pallas_call x2, Pallas kernels, weight_terms(): pl.pallas_call(weight_body, out_shape=shapes, in_specs=[pl.BlockSpec(memo...  4.65 us
    all_to_all x1, starting transfers between devices, spread(): return lax.all_to_all(copies, 'x', 0, 0, tiled=True)  4.29 us
  transfers between devices with their start and end apart: 9, of which 7 were waited for; matrix products, arithmetic and copies ran while one was open for 2% of the time, Pallas kernels for 7%

profile of v4, /device:TPU:144, one launch (start us, length us, event | category | flops | bytes accessed | tf_op | source)
XLA Modules:
  0.0 97.4 jit_solution(6928172867053545604)
XLA Ops:
  0.6 0.7 constant_dynamic-slice_fusion
  1.4 1.9 %collective-permute-start = (bf16[64,128]{1,0:T(8,128)(2,1)S(1)}, bf16[64,128]{1,0:T(8,128)(2,1)S(1)}, u32[]{:S(2)}, u32[]{:S(2)}) collective-permute-start(bf16[64,128]{1,0:T(8,128)(2,1)S(1)} %constant_dynamic-slice_fusion), channel_id=1, source_target_pairs={{0,8},{8,0},{1,9},{9,1},{2,10},{10,2},{3,11},{11,3},{4,12},{12,4},... | collective-permute-start | bytes 49160 | tf_op jit(solution)/shard_map/ppermute | solution.py:119
  3.3 1.1 %collective-permute-done = bf16[64,128]{1,0:T(8,128)(2,1)S(1)} collective-permute-done((bf16[64,128]{1,0:T(8,128)(2,1)S(1)}, bf16[64,128]{1,0:T(8,128)(2,1)S(1)}, u32[]{:S(2)}, u32[]{:S(2)}) %collective-permute-start) | collective-permute-done | bytes 16416 | tf_op jit(solution)/shard_map/ppermute | solution.py:119
  4.4 0.7 add_convert_fusion
  5.2 0.9 pad_maximum_fusion.1
  6.1 0.9 broadcast_in_dim.4
  6.9 4.3 %all-to-all-start = ((bf16[4,64,1152]{2,1,0:T(8,128)(2,1)}), bf16[4,64,1152]{2,1,0:T(8,128)(2,1)S(1)}, u32[]{:S(2)}, u32[]{:S(2)}) async-start(bf16[4,64,1152]{2,1,0:T(8,128)(2,1)} %broadcast_in_dim.4), calls=%async_computation | async-start | bytes 1179648 | tf_op jit(solution)/shard_map/all_to_all | solution.py:35
  11.2 9.1 %collective-permute-start.1 = (bf16[64,1152]{1,0:T(8,128)(2,1)S(1)}, bf16[64,1152]{1,0:T(8,128)(2,1)S(1)}, u32[]{:S(2)}, u32[]{:S(2)}) collective-permute-start(bf16[64,1152]{1,0:T(8,128)(2,1)S(1)} %pad_maximum_fusion.1), channel_id=1, source_target_pairs={{0,1},{1,0},{2,3},{3,2},{4,5},{5,4},{6,7},{7,6},{8,9},{9,8},{10,11... | collective-permute-start | bytes 442376 | tf_op jit(solution)/shard_map/ppermute | solution.py:131
  20.4 7.1 %collective-permute-done.1 = bf16[64,1152]{1,0:T(8,128)(2,1)S(1)} collective-permute-done((bf16[64,1152]{1,0:T(8,128)(2,1)S(1)}, bf16[64,1152]{1,0:T(8,128)(2,1)S(1)}, u32[]{:S(2)}, u32[]{:S(2)}) %collective-permute-start.1) | collective-permute-done | bytes 147488 | tf_op jit(solution)/shard_map/ppermute | solution.py:131
  27.5 0.0 all-to-all-done
  27.5 14.6 %all_to_all.15 = bf16[4,64,1152]{2,1,0:T(8,128)(2,1)S(1)} all-to-all(bf16[4,64,1152]{2,1,0:T(8,128)(2,1)S(1)} %broadcast_in_dim.5), channel_id=1, replica_groups=mesh['th'=4,'tl'=2,'zlo'=4,'core'=2,'x'=4,'zhi'=2] {'x'}, dimensions={0} | all-to-all | bytes 1179648 | tf_op jit(solution)/shard_map/all_to_all | solution.py:35
  42.1 0.1 select_bitcast_fusion.1
  42.2 0.0 copy-start.1
  42.2 0.1 pad_maximum_fusion
  42.4 1.1 %copy-done.1 = bf16[512,1024]{1,0:T(8,128)(2,1)S(1)} copy-done((bf16[512,1024]{1,0:T(8,128)(2,1)S(1)}, bf16[512,1024]{1,0:T(8,128)(2,1)}, u32[]{:S(2)}) %copy-start.1) | copy-done | bytes 1048600
  43.4 0.0 copy-start
  43.4 0.0 copy-start.2
  43.4 2.5 %shard_map.78 = bf16[4,128,1152]{2,1,0:T(8,128)(2,1)} custom-call(s32[4]{0:T(128)S(1)} %get-tuple-element.20.blocks, bf16[512,1024]{1,0:T(8,128)(2,1)S(1)} %copy-done.1, bf16[512,1152]{1,0:T(8,128)(2,1)S(1)} %bitcast.11), custom_call_target="tpu_custom_call" | custom-call | flops 603979776 | bytes 4194304 | tf_op jit(solution)/shard_map/pallas_call | solution.py:59
  45.9 3.5 %collective-permute-start.3 = (bf16[4,128,1152]{2,1,0:T(8,128)(2,1)}, bf16[4,128,1152]{2,1,0:T(8,128)(2,1)S(1)}, u32[]{:S(2)}, u32[]{:S(2)}) collective-permute-start(bf16[4,128,1152]{2,1,0:T(8,128)(2,1)} %shard_map.78), channel_id=1, source_target_pairs={{0,64},{8,456},{64,0},{72,136},{128,192},{136,72},{192,128},{200,2... | collective-permute-start | bytes 3538952 | tf_op jit(solution)/shard_map/ppermute | solution.py:144
  49.4 0.0 copy-done
  49.4 0.0 copy-done.2
  49.4 1.9 %shard_map.76 = bf16[4,512,128]{2,1,0:T(8,128)(2,1)S(1)} custom-call(s32[1]{0:T(128)} %bitcast.1.which, bf16[512,1152]{1,0:T(8,128)(2,1)S(1)} %bitcast.12, bf16[8,128,1024]{2,1,0:T(8,128)(2,1)S(1)} %bitcast.15, bf16[8,128,128]{2,1,0:T(8,128)(2,1)S(1)} %bitcast.17), custom_call_target="tpu_custom_call" | custom-call | flops 603979776 | bytes 4194304 | tf_op jit(solution)/shard_map/pallas_call | solution.py:89
  51.4 1.9 %collective-permute-start.2 = (bf16[4,512,128]{2,1,0:T(8,128)(2,1)S(1)}, bf16[4,512,128]{2,1,0:T(8,128)(2,1)S(1)}, u32[]{:S(2)}, u32[]{:S(2)}) collective-permute-start(bf16[4,512,128]{2,1,0:T(8,128)(2,1)S(1)} %shard_map.76), channel_id=1, source_target_pairs={{0,8},{8,0},{1,9},{9,1},{2,10},{10,2},{3,11},{11,3},{4,12},{12,4},... | collective-permute-start | bytes 1572872 | tf_op jit(solution)/shard_map/ppermute | solution.py:146
  53.3 1.9 %collective-permute-done.2.refs_0_ = bf16[4,512,128]{2,1,0:T(8,128)(2,1)S(1)} collective-permute-done((bf16[4,512,128]{2,1,0:T(8,128)(2,1)S(1)}, bf16[4,512,128]{2,1,0:T(8,128)(2,1)S(1)}, u32[]{:S(2)}, u32[]{:S(2)}) %collective-permute-start.2) | collective-permute-done | bytes 524320 | tf_op jit(solution)/shard_map/ppermute | solution.py:146
  55.2 2.8 %shard_map.77 = bf16[4,512,128]{2,1,0:T(8,128)(2,1)} custom-call(s32[1]{0:T(128)} %bitcast.which, bf16[512,1152]{1,0:T(8,128)(2,1)S(1)} %bitcast.13, bf16[8,128,1024]{2,1,0:T(8,128)(2,1)S(1)} %bitcast.16, bf16[8,128,128]{2,1,0:T(8,128)(2,1)S(1)} %bitcast.18, bf16[4,512,128]{2,1,0:T(8,128)(2,1)S(1)} %collective-permute-done.2.refs_0_), custom_call_target="tpu_custom_call" | custom-call | flops 603979776 | bytes 4194304 | tf_op jit(solution)/shard_map/pallas_call | solution.py:89
  57.9 4.2 %all-to-all-start.2 = ((bf16[4,512,128]{2,1,0:T(8,128)(2,1)}), bf16[4,512,128]{2,1,0:T(8,128)(2,1)}, u32[]{:S(2)}, u32[]{:S(2)}) async-start(bf16[4,512,128]{2,1,0:T(8,128)(2,1)} %shard_map.77), calls=%async_computation.2 | async-start | bytes 1048576 | tf_op jit(solution)/shard_map/all_to_all | solution.py:148
  62.1 2.1 %collective-permute-done.3.refs_0_ = bf16[4,128,1152]{2,1,0:T(8,128)(2,1)S(1)} collective-permute-done((bf16[4,128,1152]{2,1,0:T(8,128)(2,1)}, bf16[4,128,1152]{2,1,0:T(8,128)(2,1)S(1)}, u32[]{:S(2)}, u32[]{:S(2)}) %collective-permute-start.3) | collective-permute-done | bytes 1179680 | tf_op jit(solution)/shard_map/ppermute | solution.py:144
  64.2 2.2 %shard_map.79 = (bf16[128,1152]{1,0:T(8,128)(2,1)S(1)}, bf16[128,1152]{1,0:T(8,128)(2,1)}, bf16[128,1152]{1,0:T(8,128)(2,1)}, bf16[128,1152]{1,0:T(8,128)(2,1)}) custom-call(s32[4]{0:T(128)S(1)} %get-tuple-element.19.blocks, bf16[512,1024]{1,0:T(8,128)(2,1)S(1)} %copy-done.1, bf16[512,1152]{1,0:T(8,128)(2,1)S(1)} %bitcast.14, ...), custom_call_target="tpu_custom_call" | custom-call | flops 603979776 | bytes 4194304 | tf_op jit(solution)/shard_map/pallas_call | solution.py:59
  66.4 0.0 copy-start.3
  66.4 0.7 copy-done.3
  67.1 5.1 %collective-permute-start.4 = (bf16[128,1152]{1,0:T(8,128)(2,1)}, bf16[128,1152]{1,0:T(8,128)(2,1)S(1)}, u32[]{:S(2)}, u32[]{:S(2)}) collective-permute-start(bf16[128,1152]{1,0:T(8,128)(2,1)} %get-tuple-element.22), channel_id=1, source_target_pairs={{0,320},{8,200},{64,256},{72,392},{128,448},{136,328},{192,384},{2... | collective-permute-start | bytes 884744 | tf_op jit(solution)/shard_map/ppermute | solution.py:153
  72.2 4.0 %collective-permute-start.5 = (bf16[128,1152]{1,0:T(8,128)(2,1)}, bf16[128,1152]{1,0:T(8,128)(2,1)S(1)}, u32[]{:S(2)}, u32[]{:S(2)}) collective-permute-start(bf16[128,1152]{1,0:T(8,128)(2,1)} %get-tuple-element.23), channel_id=1, source_target_pairs={{0,384},{8,136},{64,192},{72,456},{128,0},{136,264},{192,320},{200... | collective-permute-start | bytes 884744 | tf_op jit(solution)/shard_map/ppermute | solution.py:153
  76.3 2.6 %collective-permute-start.6 = (bf16[128,1152]{1,0:T(8,128)(2,1)}, bf16[128,1152]{1,0:T(8,128)(2,1)S(1)}, u32[]{:S(2)}, u32[]{:S(2)}) collective-permute-start(bf16[128,1152]{1,0:T(8,128)(2,1)} %get-tuple-element.24), channel_id=1, source_target_pairs={{0,448},{8,72},{64,128},{72,8},{128,64},{136,200},{192,256},{200,1... | collective-permute-start | bytes 884744 | tf_op jit(solution)/shard_map/ppermute | solution.py:153
  78.9 0.0 all-to-all-done.2
  78.9 1.8 %reduce_sum.12 = bf16[512,128]{1,0:T(8,128)(2,1)} reduce(bf16[4,512,128]{2,1,0:T(8,128)(2,1)} %all-to-all-done.2, bf16[]{:T(256)} %constant.60.clone.1), dimensions={0}, to_apply=%region_0.1 | reduce | flops 196608 | bytes 655362 | tf_op jit(solution)/shard_map/reduce_sum | solution.py:149
  80.7 5.2 %collective-permute-done.4 = bf16[128,1152]{1,0:T(8,128)(2,1)S(1)} collective-permute-done((bf16[128,1152]{1,0:T(8,128)(2,1)}, bf16[128,1152]{1,0:T(8,128)(2,1)S(1)}, u32[]{:S(2)}, u32[]{:S(2)}) %collective-permute-start.4) | collective-permute-done | bytes 294944 | tf_op jit(solution)/shard_map/ppermute | solution.py:153
  85.9 2.8 %collective-permute-done.5 = bf16[128,1152]{1,0:T(8,128)(2,1)S(1)} collective-permute-done((bf16[128,1152]{1,0:T(8,128)(2,1)}, bf16[128,1152]{1,0:T(8,128)(2,1)S(1)}, u32[]{:S(2)}, u32[]{:S(2)}) %collective-permute-start.5) | collective-permute-done | bytes 294944 | tf_op jit(solution)/shard_map/ppermute | solution.py:153
  88.7 5.4 %collective-permute-done.6 = bf16[128,1152]{1,0:T(8,128)(2,1)S(1)} collective-permute-done((bf16[128,1152]{1,0:T(8,128)(2,1)}, bf16[128,1152]{1,0:T(8,128)(2,1)S(1)}, u32[]{:S(2)}, u32[]{:S(2)}) %collective-permute-start.6) | collective-permute-done | bytes 294944 | tf_op jit(solution)/shard_map/ppermute | solution.py:153
  94.1 1.4 %convert_add_fusion.1 = f32[128,128]{1,0:T(8,128)} fusion(bf16[128,1152]{1,0:T(8,128)(2,1)S(1)} %collective-permute-done.6, bf16[128,1152]{1,0:T(8,128)(2,1)S(1)} %collective-permute-done.5, bf16[128,1152]{1,0:T(8,128)(2,1)S(1)} %collective-permute-done.4, bf16[128,1152]{1,0:T(8,128)(2,1)} %copy-done.3), kind=kLoop, calls=%fused_computation.5 | loop fusion | flops 114688 | bytes 196608 | tf_op jit(solution)/shard_map/add | solution.py:158
  95.5 1.9 %convert_add_fusion = f32[128,1024]{1,0:T(8,128)} fusion(bf16[128,1152]{1,0:T(8,128)(2,1)S(1)} %collective-permute-done.6, bf16[128,1152]{1,0:T(8,128)(2,1)S(1)} %collective-permute-done.5, bf16[128,1152]{1,0:T(8,128)(2,1)S(1)} %collective-permute-done.4, bf16[128,1152]{1,0:T(8,128)(2,1)} %copy-done.3), kind=kLoop, calls=%fused_computation.3 | loop fusion | flops 917504 | bytes 1572864 | tf_op jit(solution)/shard_map/add | solution.py:158
  (2 shorter events, 0.1 us)
Async XLA Ops:
  1.4 3.1 %collective-permute-start = (bf16[64,128]{1,0:T(8,128)(2,1)S(1)}, bf16[64,128]{1,0:T(8,128)(2,1)S(1)}, u32[]{:S(2)}, u32[]{:S(2)}) collective-permute-start(bf16[64,128]{1,0:T(8,128)(2,1)S(1)} %constant_dynamic-slice_fusion), channel_id=1, source_target_pairs={{0,8},{8,0},{1,9},{9,1},{2,10},{10,2},{3,11},{11,3},{4,12},{12,4},... | collective-permute-start | bytes 49160 | tf_op jit(solution)/shard_map/ppermute | solution.py:119
  6.9 20.5 %all-to-all-start = ((bf16[4,64,1152]{2,1,0:T(8,128)(2,1)}), bf16[4,64,1152]{2,1,0:T(8,128)(2,1)S(1)}, u32[]{:S(2)}, u32[]{:S(2)}) async-start(bf16[4,64,1152]{2,1,0:T(8,128)(2,1)} %broadcast_in_dim.4), calls=%async_computation | async-start | bytes 1179648 | tf_op jit(solution)/shard_map/all_to_all | solution.py:35
  11.2 16.2 %collective-permute-start.1 = (bf16[64,1152]{1,0:T(8,128)(2,1)S(1)}, bf16[64,1152]{1,0:T(8,128)(2,1)S(1)}, u32[]{:S(2)}, u32[]{:S(2)}) collective-permute-start(bf16[64,1152]{1,0:T(8,128)(2,1)S(1)} %pad_maximum_fusion.1), channel_id=1, source_target_pairs={{0,1},{1,0},{2,3},{3,2},{4,5},{5,4},{6,7},{7,6},{8,9},{9,8},{10,11... | collective-permute-start | bytes 442376 | tf_op jit(solution)/shard_map/ppermute | solution.py:131
  42.2 1.2 %copy-start.1 = (bf16[512,1024]{1,0:T(8,128)(2,1)S(1)}, bf16[512,1024]{1,0:T(8,128)(2,1)}, u32[]{:S(2)}) copy-start(bf16[512,1024]{1,0:T(8,128)(2,1)} %x_ref.3) | copy-start | bytes 3145732
  43.4 6.0 %copy-start = (bf16[1024,1024]{1,0:T(8,128)(2,1)S(1)}, bf16[1024,1024]{1,0:T(8,128)(2,1)}, u32[]{:S(2)}) copy-start(bf16[1024,1024]{1,0:T(8,128)(2,1)} %param.8) | copy-start | bytes 6291460
  43.4 6.0 %copy-start.2 = (bf16[1024,128]{1,0:T(8,128)(2,1)S(1)}, bf16[1024,128]{1,0:T(8,128)(2,1)}, u32[]{:S(2)}) copy-start(bf16[1024,128]{1,0:T(8,128)(2,1)} %param.9) | copy-start | bytes 786436
  45.9 18.3 %collective-permute-start.3 = (bf16[4,128,1152]{2,1,0:T(8,128)(2,1)}, bf16[4,128,1152]{2,1,0:T(8,128)(2,1)S(1)}, u32[]{:S(2)}, u32[]{:S(2)}) collective-permute-start(bf16[4,128,1152]{2,1,0:T(8,128)(2,1)} %shard_map.78), channel_id=1, source_target_pairs={{0,64},{8,456},{64,0},{72,136},{128,192},{136,72},{192,128},{200,2... | collective-permute-start | bytes 3538952 | tf_op jit(solution)/shard_map/ppermute | solution.py:144
  51.4 3.8 %collective-permute-start.2 = (bf16[4,512,128]{2,1,0:T(8,128)(2,1)S(1)}, bf16[4,512,128]{2,1,0:T(8,128)(2,1)S(1)}, u32[]{:S(2)}, u32[]{:S(2)}) collective-permute-start(bf16[4,512,128]{2,1,0:T(8,128)(2,1)S(1)} %shard_map.76), channel_id=1, source_target_pairs={{0,8},{8,0},{1,9},{9,1},{2,10},{10,2},{3,11},{11,3},{4,12},{12,4},... | collective-permute-start | bytes 1572872 | tf_op jit(solution)/shard_map/ppermute | solution.py:146
  57.9 21.0 %all-to-all-start.2 = ((bf16[4,512,128]{2,1,0:T(8,128)(2,1)}), bf16[4,512,128]{2,1,0:T(8,128)(2,1)}, u32[]{:S(2)}, u32[]{:S(2)}) async-start(bf16[4,512,128]{2,1,0:T(8,128)(2,1)} %shard_map.77), calls=%async_computation.2 | async-start | bytes 1048576 | tf_op jit(solution)/shard_map/all_to_all | solution.py:148
  66.4 0.7 copy-start.3
  67.1 18.8 %collective-permute-start.4 = (bf16[128,1152]{1,0:T(8,128)(2,1)}, bf16[128,1152]{1,0:T(8,128)(2,1)S(1)}, u32[]{:S(2)}, u32[]{:S(2)}) collective-permute-start(bf16[128,1152]{1,0:T(8,128)(2,1)} %get-tuple-element.22), channel_id=1, source_target_pairs={{0,320},{8,200},{64,256},{72,392},{128,448},{136,328},{192,384},{2... | collective-permute-start | bytes 884744 | tf_op jit(solution)/shard_map/ppermute | solution.py:153
  72.2 16.5 %collective-permute-start.5 = (bf16[128,1152]{1,0:T(8,128)(2,1)}, bf16[128,1152]{1,0:T(8,128)(2,1)S(1)}, u32[]{:S(2)}, u32[]{:S(2)}) collective-permute-start(bf16[128,1152]{1,0:T(8,128)(2,1)} %get-tuple-element.23), channel_id=1, source_target_pairs={{0,384},{8,136},{64,192},{72,456},{128,0},{136,264},{192,320},{200... | collective-permute-start | bytes 884744 | tf_op jit(solution)/shard_map/ppermute | solution.py:153
  76.3 17.8 %collective-permute-start.6 = (bf16[128,1152]{1,0:T(8,128)(2,1)}, bf16[128,1152]{1,0:T(8,128)(2,1)S(1)}, u32[]{:S(2)}, u32[]{:S(2)}) collective-permute-start(bf16[128,1152]{1,0:T(8,128)(2,1)} %get-tuple-element.24), channel_id=1, source_target_pairs={{0,448},{8,72},{64,128},{72,8},{128,64},{136,200},{192,256},{200,1... | collective-permute-start | bytes 884744 | tf_op jit(solution)/shard_map/ppermute | solution.py:153

commit v5 on v4

--- a/solution.py
+++ b/solution.py
@@ -9,6 +9,7 @@
 from jax.sharding import PartitionSpec as P
 
 SWAP = [(0, 1), (1, 0)]
+CROSS = [(0, 3), (1, 2), (2, 1), (3, 0)]
 WID = ("x", "zhi")
 TOK = ("th", "tl")
 HEAD = ("zlo", "core")
@@ -66,6 +67,33 @@
             flops=2 * 512 * 512 * g.shape[1], bytes_accessed=4 * 2**20, transcendentals=0
         ),
     )(blocks, x, g, *extra)
+
+
+def sum_body(*refs):
+    *pieces, q_ref, kv_ref = refs
+    n_q = q_ref.shape[1]
+    q_ref[...] = sum(piece[:, :n_q].astype(jnp.float32) for piece in pieces)
+    kv_ref[...] = sum(piece[:, n_q:].astype(jnp.float32) for piece in pieces)
+
+
+def last_sum(pieces, n_q):
+    rows, columns = pieces[0].shape
+    step = rows // 2
+    block = lambda width: pl.BlockSpec((step, width), lambda i: (i, 0))
+    return pl.pallas_call(
+        sum_body,
+        grid=(2,),
+        out_shape=[
+            jax.ShapeDtypeStruct((rows, n_q), jnp.float32),
+            jax.ShapeDtypeStruct((rows, columns - n_q), jnp.float32),
+        ],
+        in_specs=[block(columns)] * len(pieces),
+        out_specs=[block(n_q), block(columns - n_q)],
+        compiler_params=pltpu.CompilerParams(vmem_limit_bytes=VMEM_LIMIT),
+        cost_estimate=pl.CostEstimate(
+            flops=4 * rows * columns, bytes_accessed=12 * rows * columns, transcendentals=0
+        ),
+    )(*pieces)
 
 
 def input_body(which, g_ref, wq_ref, wkv_ref, *refs):
@@ -116,10 +144,12 @@
 
     share = key_value_share_gradient
     outgoing = lax.dynamic_slice_in_dim(share, (1 - core) * head_dim, head_dim, 1)
-    incoming = lax.ppermute(outgoing, "core", SWAP)
     own_part = lax.dynamic_slice_in_dim(share, core * head_dim, head_dim, 1)
-    kv_rows = (own_part.astype(jnp.float32) + incoming.astype(jnp.float32)).astype(jnp.bfloat16)
-    mine = jnp.concatenate([q_grad, kv_rows], axis=1)
+    mine = jnp.concatenate([q_grad, own_part], axis=1)
+    mine, outgoing = lax.optimization_barrier((mine, outgoing))
+    part = lax.ppermute(outgoing, "core", SWAP)
+    far_part = lax.ppermute(outgoing, ("core", "zhi"), CROSS)
+    far = lax.ppermute(mine, "zhi", SWAP)
 
     sigma = side(y, core)
     steps = jnp.arange(N_PAIRS, dtype=jnp.int32)
@@ -127,37 +157,38 @@
     give_blocks = (y - sigma * (1 + steps)) % N_Y
     give_which = (1 - core).reshape(1)
     keep_which = core.reshape(1)
-
-    far = lax.ppermute(mine, "zhi", SWAP)
-    near_all = spread(mine)
-    far, near_all, near_first, keep_blocks, give_blocks, keep_which, give_which = (
-        lax.optimization_barrier(
-            (far, near_all, zhi == 0, keep_blocks, give_blocks, keep_which, give_which)
+    near_first = zhi == 0
+    orders = (near_first, keep_blocks, give_blocks, keep_which, give_which)
+    far, far_part, part, mine, orders = lax.optimization_barrier((far, far_part, part, mine, orders))
+    near_first, keep_blocks, give_blocks, keep_which, give_which = orders
+
+    def with_sum(rows, more):
+        kv_rows = rows[:, q_columns:].astype(jnp.float32) + more.astype(jnp.float32)
+        return rows[:, :q_columns], kv_rows.astype(jnp.bfloat16)
+
+    def in_order(one, other):
+        return jnp.concatenate(
+            [jnp.where(near_first, one, other), jnp.where(near_first, other, one)]
         )
-    )
-    far_all = spread(far)
-    first = jnp.where(near_first, near_all, far_all)
-    second = jnp.where(near_first, far_all, near_all)
-    combined = jnp.stack([first, second], axis=1).reshape(-1, mine.shape[1])
+
+    both = [in_order(one, other) for one, other in zip(with_sum(mine, part), with_sum(far, far_part))]
+    combined = spread(jnp.concatenate(both, axis=1))
+    combined = combined.reshape(-1, mine.shape[1])
 
     (given,) = weight_terms(give_blocks, inputs, combined)
     got = lax.ppermute(given, (*TOK, "core"), moved(lambda y, core: -side(y, core)))
+    kept = weight_terms(keep_blocks, inputs, combined, got)
 
     core_got = lax.ppermute(input_terms(give_which, combined, q_weight, key_value_weight), "core", SWAP)
-    pieces = input_terms(keep_which, combined, q_weight, key_value_weight, core_got)
-    pieces = lax.all_to_all(pieces, "zlo", 0, 0, tiled=True)
-    input_grad = jnp.sum(pieces.astype(jnp.float32), axis=0).astype(jnp.bfloat16)
-
-    kept = weight_terms(keep_blocks, inputs, combined, got)
-    pieces = [
-        lax.ppermute(kept[r], (*TOK, "core"), moved(lambda y, core: r * side(y, core)))
-        for r in range(N_PAIRS - 1, 0, -1)
-    ]
-
-    def total(columns):
-        return sum(piece[:, columns].astype(jnp.float32) for piece in [kept[0], *pieces])
-
-    return (input_grad, total(slice(0, q_columns)), total(slice(q_columns, None)))
+    terms = input_terms(keep_which, combined, q_weight, key_value_weight, core_got)
+
+    pieces = [kept[0]]
+    for r in range(N_PAIRS - 1, 0, -1):
+        piece = lax.ppermute(kept[r], (*TOK, "core"), moved(lambda y, core: r * side(y, core)))
+        pieces.append(piece)
+    terms = lax.all_to_all(terms, "zlo", 0, 0, tiled=True)
+    input_grad = jnp.sum(terms.astype(jnp.float32), axis=0).astype(jnp.bfloat16)
+    return (input_grad, *last_sum(pieces, q_columns))
 
 
 def solution(mesh):

time: 98.1 us -> 95.4 us (0.972)
  the two profiles are of different devices: /device:TPU:144 before, /device:TPU:16 now
where the time goes in v5:
time: 95.4 us; the launch traced here: 94.8 us
  starting transfers between devices  36.6 us (38%)
  waiting for transfers between devices  21.4 us (22%)
  blocking collectives  20.4 us (21%)
  Pallas kernels  10.2 us (11%)
  other arithmetic  2.8 us (3%)
  local copies, waits for them, and re-layouts  2.52 us (3%)
    all_to_all x1, blocking collectives, spread(): return lax.all_to_all(copies, 'x', 0, 0, tiled=True)  20.4 us
    ppermute x3, waiting for transfers between devices, local(): lax.ppermute(kept[r], (*TOK, 'core'), moved(lambda y, core: r * side(y, c...  12.8 us
    ppermute x3, starting transfers between devices, local(): lax.ppermute(kept[r], (*TOK, 'core'), moved(lambda y, core: r * side(y, c...  11.8 us
    ppermute x1, starting transfers between devices, local(): far = lax.ppermute(mine, 'zhi', SWAP)  10.9 us
    ppermute x1, waiting for transfers between devices, local(): far_part = lax.ppermute(outgoing, ('core', 'zhi'), CROSS)  4.98 us
    pallas_call x2, Pallas kernels, input_terms(): pl.pallas_call(input_body, grid_spec=pltpu.PrefetchScalarGridSpec(num_sca...  4.7 us
    pallas_call x2, Pallas kernels, weight_terms(): pl.pallas_call(weight_body, out_shape=shapes, in_specs=[pl.BlockSpec(memo...  4.66 us
    all_to_all x1, starting transfers between devices, local(): terms = lax.all_to_all(terms, 'zlo', 0, 0, tiled=True)  4.58 us
  transfers between devices with their start and end apart: 9, of which 6 were waited for; matrix products, arithmetic and copies ran while one was open for 2% of the time, Pallas kernels for 7%

profile of v5, /device:TPU:16, one launch (start us, length us, event | category | flops | bytes accessed | tf_op | source)
XLA Modules:
  0.0 94.8 jit_solution(688086649066582718)
XLA Ops:
  0.6 0.7 constant_dynamic-slice_fusion
  1.4 0.9 pad_maximum_fusion
  2.3 10.9 %collective-permute-start = (bf16[64,1152]{1,0:T(8,128)(2,1)S(1)}, bf16[64,1152]{1,0:T(8,128)(2,1)S(1)}, u32[]{:S(2)}, u32[]{:S(2)}) collective-permute-start(bf16[64,1152]{1,0:T(8,128)(2,1)S(1)} %pad_maximum_fusion), channel_id=1, source_target_pairs={{0,1},{1,0},{2,3},{3,2},{4,5},{5,4},{6,7},{7,6},{8,9},{9,8},{10,11... | collective-permute-start | bytes 442376 | tf_op jit(solution)/shard_map/ppermute | solution.py:152
  13.2 1.9 %collective-permute-start.1 = (bf16[64,128]{1,0:T(8,128)(2,1)S(1)}, bf16[64,128]{1,0:T(8,128)(2,1)S(1)}, u32[]{:S(2)}, u32[]{:S(2)}) collective-permute-start(bf16[64,128]{1,0:T(8,128)(2,1)S(1)} %get-tuple-element.21), channel_id=1, source_target_pairs={{0,9},{1,8},{8,1},{9,0},{2,11},{3,10},{10,3},{11,2},{4,13},{5,12},... | collective-permute-start | bytes 49160 | tf_op jit(solution)/shard_map/ppermute | solution.py:151
  15.2 2.0 %collective-permute-start.2 = (bf16[64,128]{1,0:T(8,128)(2,1)S(1)}, bf16[64,128]{1,0:T(8,128)(2,1)S(1)}, u32[]{:S(2)}, u32[]{:S(2)}) collective-permute-start(bf16[64,128]{1,0:T(8,128)(2,1)S(1)} %get-tuple-element.21), channel_id=1, source_target_pairs={{0,8},{8,0},{1,9},{9,1},{2,10},{10,2},{3,11},{11,3},{4,12},{12,4},... | collective-permute-start | bytes 49160 | tf_op jit(solution)/shard_map/ppermute | solution.py:150
  17.2 5.0 %collective-permute-done.1 = bf16[64,128]{1,0:T(8,128)(2,1)S(1)} collective-permute-done((bf16[64,128]{1,0:T(8,128)(2,1)S(1)}, bf16[64,128]{1,0:T(8,128)(2,1)S(1)}, u32[]{:S(2)}, u32[]{:S(2)}) %collective-permute-start.1) | collective-permute-done | bytes 16416 | tf_op jit(solution)/shard_map/ppermute | solution.py:151
  22.2 0.0 collective-permute-done.2
  22.2 0.0 collective-permute-done
  22.3 0.1 broadcast_in_dim.2
  22.4 0.0 copy-start.1
  22.4 20.4 %all_to_all.10 = bf16[4,128,1152]{2,1,0:T(8,128)(2,1)S(1)} all-to-all(bf16[4,128,1152]{2,1,0:T(8,128)(2,1)S(1)} %broadcast_in_dim.2), channel_id=1, replica_groups=mesh['th'=4,'tl'=2,'zlo'=4,'core'=2,'x'=4,'zhi'=2] {'x'}, dimensions={0} | all-to-all | bytes 2359296 | tf_op jit(solution)/shard_map/all_to_all | solution.py:36
  42.8 0.0 copy-done.1
  42.8 0.0 copy-start
  42.8 0.0 copy-start.2
  42.9 2.5 %shard_map.78 = bf16[4,128,1152]{2,1,0:T(8,128)(2,1)} custom-call(s32[4]{0:T(128)S(1)} %get-tuple-element.30.blocks, bf16[512,1024]{1,0:T(8,128)(2,1)S(1)} %copy-done.1, bf16[512,1152]{1,0:T(8,128)(2,1)S(1)} %bitcast.5), custom_call_target="tpu_custom_call" | custom-call | flops 603979776 | bytes 4194304 | tf_op jit(solution)/shard_map/pallas_call | solution.py:60
  45.4 3.5 %collective-permute-start.4 = (bf16[4,128,1152]{2,1,0:T(8,128)(2,1)}, bf16[4,128,1152]{2,1,0:T(8,128)(2,1)S(1)}, u32[]{:S(2)}, u32[]{:S(2)}) collective-permute-start(bf16[4,128,1152]{2,1,0:T(8,128)(2,1)} %shard_map.78), channel_id=1, source_target_pairs={{0,64},{8,456},{64,0},{72,136},{128,192},{136,72},{192,128},{200,2... | collective-permute-start | bytes 3538952 | tf_op jit(solution)/shard_map/ppermute | solution.py:179
  48.8 0.0 copy-done
  48.8 0.0 copy-done.2
  48.8 1.9 %shard_map.76 = bf16[4,512,128]{2,1,0:T(8,128)(2,1)S(1)} custom-call(s32[1]{0:T(128)} %bitcast.1.which, bf16[512,1152]{1,0:T(8,128)(2,1)S(1)} %bitcast.6, bf16[8,128,1024]{2,1,0:T(8,128)(2,1)S(1)} %bitcast.9, bf16[8,128,128]{2,1,0:T(8,128)(2,1)S(1)} %bitcast.11), custom_call_target="tpu_custom_call" | custom-call | flops 603979776 | bytes 4194304 | tf_op jit(solution)/shard_map/pallas_call | solution.py:117
  50.8 1.9 %collective-permute-start.3 = (bf16[4,512,128]{2,1,0:T(8,128)(2,1)S(1)}, bf16[4,512,128]{2,1,0:T(8,128)(2,1)S(1)}, u32[]{:S(2)}, u32[]{:S(2)}) collective-permute-start(bf16[4,512,128]{2,1,0:T(8,128)(2,1)S(1)} %shard_map.76), channel_id=1, source_target_pairs={{0,8},{8,0},{1,9},{9,1},{2,10},{10,2},{3,11},{11,3},{4,12},{12,4},... | collective-permute-start | bytes 1572872 | tf_op jit(solution)/shard_map/ppermute | solution.py:182
  52.7 1.9 %collective-permute-done.3.refs_0_ = bf16[4,512,128]{2,1,0:T(8,128)(2,1)S(1)} collective-permute-done((bf16[4,512,128]{2,1,0:T(8,128)(2,1)S(1)}, bf16[4,512,128]{2,1,0:T(8,128)(2,1)S(1)}, u32[]{:S(2)}, u32[]{:S(2)}) %collective-permute-start.3) | collective-permute-done | bytes 524320 | tf_op jit(solution)/shard_map/ppermute | solution.py:182
  54.6 2.8 %shard_map.77 = bf16[4,512,128]{2,1,0:T(8,128)(2,1)} custom-call(s32[1]{0:T(128)} %bitcast.which, bf16[512,1152]{1,0:T(8,128)(2,1)S(1)} %bitcast.7, bf16[8,128,1024]{2,1,0:T(8,128)(2,1)S(1)} %bitcast.10, bf16[8,128,128]{2,1,0:T(8,128)(2,1)S(1)} %bitcast.12, bf16[4,512,128]{2,1,0:T(8,128)(2,1)S(1)} %collective-permute-done.3.refs_0_), custom_call_target="tpu_custom_call" | custom-call | flops 603979776 | bytes 4194304 | tf_op jit(solution)/shard_map/pallas_call | solution.py:117
  57.4 4.6 %all-to-all-start.1 = ((bf16[4,512,128]{2,1,0:T(8,128)(2,1)}), bf16[4,512,128]{2,1,0:T(8,128)(2,1)}, u32[]{:S(2)}, u32[]{:S(2)}) async-start(bf16[4,512,128]{2,1,0:T(8,128)(2,1)} %shard_map.77), calls=%async_computation.1 | async-start | bytes 1048576 | tf_op jit(solution)/shard_map/all_to_all | solution.py:189
  61.9 1.7 %collective-permute-done.4.refs_0_ = bf16[4,128,1152]{2,1,0:T(8,128)(2,1)S(1)} collective-permute-done((bf16[4,128,1152]{2,1,0:T(8,128)(2,1)}, bf16[4,128,1152]{2,1,0:T(8,128)(2,1)S(1)}, u32[]{:S(2)}, u32[]{:S(2)}) %collective-permute-start.4) | collective-permute-done | bytes 1179680 | tf_op jit(solution)/shard_map/ppermute | solution.py:179
  63.7 2.2 %shard_map.79 = (bf16[128,1152]{1,0:T(8,128)(2,1)S(1)}, bf16[128,1152]{1,0:T(8,128)(2,1)}, bf16[128,1152]{1,0:T(8,128)(2,1)}, bf16[128,1152]{1,0:T(8,128)(2,1)}) custom-call(s32[4]{0:T(128)S(1)} %get-tuple-element.29.blocks, bf16[512,1024]{1,0:T(8,128)(2,1)S(1)} %copy-done.1, bf16[512,1152]{1,0:T(8,128)(2,1)S(1)} %bitcast.8, ...), custom_call_target="tpu_custom_call" | custom-call | flops 603979776 | bytes 4194304 | tf_op jit(solution)/shard_map/pallas_call | solution.py:60
  65.8 0.0 copy-start.3
  65.8 0.7 copy-done.3
  66.5 5.1 %collective-permute-start.5 = (bf16[128,1152]{1,0:T(8,128)(2,1)}, bf16[128,1152]{1,0:T(8,128)(2,1)S(1)}, u32[]{:S(2)}, u32[]{:S(2)}) collective-permute-start(bf16[128,1152]{1,0:T(8,128)(2,1)} %get-tuple-element.32), channel_id=1, source_target_pairs={{0,320},{8,200},{64,256},{72,392},{128,448},{136,328},{192,384},{2... | collective-permute-start | bytes 884744 | tf_op jit(solution)/shard_map/ppermute | solution.py:187
  71.7 4.0 %collective-permute-start.6 = (bf16[128,1152]{1,0:T(8,128)(2,1)}, bf16[128,1152]{1,0:T(8,128)(2,1)S(1)}, u32[]{:S(2)}, u32[]{:S(2)}) collective-permute-start(bf16[128,1152]{1,0:T(8,128)(2,1)} %get-tuple-element.33), channel_id=1, source_target_pairs={{0,384},{8,136},{64,192},{72,456},{128,0},{136,264},{192,320},{200... | collective-permute-start | bytes 884744 | tf_op jit(solution)/shard_map/ppermute | solution.py:187
  75.7 2.6 %collective-permute-start.7 = (bf16[128,1152]{1,0:T(8,128)(2,1)}, bf16[128,1152]{1,0:T(8,128)(2,1)S(1)}, u32[]{:S(2)}, u32[]{:S(2)}) collective-permute-start(bf16[128,1152]{1,0:T(8,128)(2,1)} %get-tuple-element.34), channel_id=1, source_target_pairs={{0,448},{8,72},{64,128},{72,8},{128,64},{136,200},{192,256},{200,1... | collective-permute-start | bytes 884744 | tf_op jit(solution)/shard_map/ppermute | solution.py:187
  78.3 0.0 all-to-all-done.1
  78.3 1.8 %reduce_sum.12 = bf16[512,128]{1,0:T(8,128)(2,1)} reduce(bf16[4,512,128]{2,1,0:T(8,128)(2,1)} %all-to-all-done.1, bf16[]{:T(256)} %constant.60.clone.1), dimensions={0}, to_apply=%region_0.1 | reduce | flops 196608 | bytes 655362 | tf_op jit(solution)/shard_map/reduce_sum | solution.py:190
  80.1 5.2 %collective-permute-done.5.refs_1_ = bf16[128,1152]{1,0:T(8,128)(2,1)S(1)} collective-permute-done((bf16[128,1152]{1,0:T(8,128)(2,1)}, bf16[128,1152]{1,0:T(8,128)(2,1)S(1)}, u32[]{:S(2)}, u32[]{:S(2)}) %collective-permute-start.5) | collective-permute-done | bytes 294944 | tf_op jit(solution)/shard_map/ppermute | solution.py:187
  85.3 3.0 %collective-permute-done.6.refs_2_ = bf16[128,1152]{1,0:T(8,128)(2,1)S(1)} collective-permute-done((bf16[128,1152]{1,0:T(8,128)(2,1)}, bf16[128,1152]{1,0:T(8,128)(2,1)S(1)}, u32[]{:S(2)}, u32[]{:S(2)}) %collective-permute-start.6) | collective-permute-done | bytes 294944 | tf_op jit(solution)/shard_map/ppermute | solution.py:187
  88.3 4.7 %collective-permute-done.7.refs_3_ = bf16[128,1152]{1,0:T(8,128)(2,1)S(1)} collective-permute-done((bf16[128,1152]{1,0:T(8,128)(2,1)}, bf16[128,1152]{1,0:T(8,128)(2,1)S(1)}, u32[]{:S(2)}, u32[]{:S(2)}) %collective-permute-start.7) | collective-permute-done | bytes 294944 | tf_op jit(solution)/shard_map/ppermute | solution.py:187
  93.0 0.0 copy-start.4
  93.0 1.0 %copy-done.4 = bf16[128,1152]{1,0:T(8,128)(2,1)S(1)} copy-done((bf16[128,1152]{1,0:T(8,128)(2,1)S(1)}, bf16[128,1152]{1,0:T(8,128)(2,1)}, u32[]{:S(2)}) %copy-start.4) | copy-done | bytes 294936
  93.9 0.9 shard_map.80
  (4 shorter events, 0.1 us)
Async XLA Ops:
  2.3 19.9 %collective-permute-start = (bf16[64,1152]{1,0:T(8,128)(2,1)S(1)}, bf16[64,1152]{1,0:T(8,128)(2,1)S(1)}, u32[]{:S(2)}, u32[]{:S(2)}) collective-permute-start(bf16[64,1152]{1,0:T(8,128)(2,1)S(1)} %pad_maximum_fusion), channel_id=1, source_target_pairs={{0,1},{1,0},{2,3},{3,2},{4,5},{5,4},{6,7},{7,6},{8,9},{9,8},{10,11... | collective-permute-start | bytes 442376 | tf_op jit(solution)/shard_map/ppermute | solution.py:152
  13.2 9.0 %collective-permute-start.1 = (bf16[64,128]{1,0:T(8,128)(2,1)S(1)}, bf16[64,128]{1,0:T(8,128)(2,1)S(1)}, u32[]{:S(2)}, u32[]{:S(2)}) collective-permute-start(bf16[64,128]{1,0:T(8,128)(2,1)S(1)} %get-tuple-element.21), channel_id=1, source_target_pairs={{0,9},{1,8},{8,1},{9,0},{2,11},{3,10},{10,3},{11,2},{4,13},{5,12},... | collective-permute-start | bytes 49160 | tf_op jit(solution)/shard_map/ppermute | solution.py:151
  15.2 7.1 %collective-permute-start.2 = (bf16[64,128]{1,0:T(8,128)(2,1)S(1)}, bf16[64,128]{1,0:T(8,128)(2,1)S(1)}, u32[]{:S(2)}, u32[]{:S(2)}) collective-permute-start(bf16[64,128]{1,0:T(8,128)(2,1)S(1)} %get-tuple-element.21), channel_id=1, source_target_pairs={{0,8},{8,0},{1,9},{9,1},{2,10},{10,2},{3,11},{11,3},{4,12},{12,4},... | collective-permute-start | bytes 49160 | tf_op jit(solution)/shard_map/ppermute | solution.py:150
  22.4 20.5 %copy-start.1 = (bf16[512,1024]{1,0:T(8,128)(2,1)S(1)}, bf16[512,1024]{1,0:T(8,128)(2,1)}, u32[]{:S(2)}) copy-start(bf16[512,1024]{1,0:T(8,128)(2,1)} %x_ref.3) | copy-start | bytes 3145732
  42.8 6.0 %copy-start = (bf16[1024,1024]{1,0:T(8,128)(2,1)S(1)}, bf16[1024,1024]{1,0:T(8,128)(2,1)}, u32[]{:S(2)}) copy-start(bf16[1024,1024]{1,0:T(8,128)(2,1)} %param.8) | copy-start | bytes 6291460
  42.8 6.0 %copy-start.2 = (bf16[1024,128]{1,0:T(8,128)(2,1)S(1)}, bf16[1024,128]{1,0:T(8,128)(2,1)}, u32[]{:S(2)}) copy-start(bf16[1024,128]{1,0:T(8,128)(2,1)} %param.9) | copy-start | bytes 786436
  45.4 18.3 %collective-permute-start.4 = (bf16[4,128,1152]{2,1,0:T(8,128)(2,1)}, bf16[4,128,1152]{2,1,0:T(8,128)(2,1)S(1)}, u32[]{:S(2)}, u32[]{:S(2)}) collective-permute-start(bf16[4,128,1152]{2,1,0:T(8,128)(2,1)} %shard_map.78), channel_id=1, source_target_pairs={{0,64},{8,456},{64,0},{72,136},{128,192},{136,72},{192,128},{200,2... | collective-permute-start | bytes 3538952 | tf_op jit(solution)/shard_map/ppermute | solution.py:179
  50.8 3.8 %collective-permute-start.3 = (bf16[4,512,128]{2,1,0:T(8,128)(2,1)S(1)}, bf16[4,512,128]{2,1,0:T(8,128)(2,1)S(1)}, u32[]{:S(2)}, u32[]{:S(2)}) collective-permute-start(bf16[4,512,128]{2,1,0:T(8,128)(2,1)S(1)} %shard_map.76), channel_id=1, source_target_pairs={{0,8},{8,0},{1,9},{9,1},{2,10},{10,2},{3,11},{11,3},{4,12},{12,4},... | collective-permute-start | bytes 1572872 | tf_op jit(solution)/shard_map/ppermute | solution.py:182
  57.4 21.0 %all-to-all-start.1 = ((bf16[4,512,128]{2,1,0:T(8,128)(2,1)}), bf16[4,512,128]{2,1,0:T(8,128)(2,1)}, u32[]{:S(2)}, u32[]{:S(2)}) async-start(bf16[4,512,128]{2,1,0:T(8,128)(2,1)} %shard_map.77), calls=%async_computation.1 | async-start | bytes 1048576 | tf_op jit(solution)/shard_map/all_to_all | solution.py:189
  65.8 0.7 copy-start.3
  66.5 18.8 %collective-permute-start.5 = (bf16[128,1152]{1,0:T(8,128)(2,1)}, bf16[128,1152]{1,0:T(8,128)(2,1)S(1)}, u32[]{:S(2)}, u32[]{:S(2)}) collective-permute-start(bf16[128,1152]{1,0:T(8,128)(2,1)} %get-tuple-element.32), channel_id=1, source_target_pairs={{0,320},{8,200},{64,256},{72,392},{128,448},{136,328},{192,384},{2... | collective-permute-start | bytes 884744 | tf_op jit(solution)/shard_map/ppermute | solution.py:187
  71.7 16.6 %collective-permute-start.6 = (bf16[128,1152]{1,0:T(8,128)(2,1)}, bf16[128,1152]{1,0:T(8,128)(2,1)S(1)}, u32[]{:S(2)}, u32[]{:S(2)}) collective-permute-start(bf16[128,1152]{1,0:T(8,128)(2,1)} %get-tuple-element.33), channel_id=1, source_target_pairs={{0,384},{8,136},{64,192},{72,456},{128,0},{136,264},{192,320},{200... | collective-permute-start | bytes 884744 | tf_op jit(solution)/shard_map/ppermute | solution.py:187
  75.7 17.2 %collective-permute-start.7 = (bf16[128,1152]{1,0:T(8,128)(2,1)}, bf16[128,1152]{1,0:T(8,128)(2,1)S(1)}, u32[]{:S(2)}, u32[]{:S(2)}) collective-permute-start(bf16[128,1152]{1,0:T(8,128)(2,1)} %get-tuple-element.34), channel_id=1, source_target_pairs={{0,448},{8,72},{64,128},{72,8},{128,64},{136,200},{192,256},{200,1... | collective-permute-start | bytes 884744 | tf_op jit(solution)/shard_map/ppermute | solution.py:187
  93.0 1.0 %copy-start.4 = (bf16[128,1152]{1,0:T(8,128)(2,1)S(1)}, bf16[128,1152]{1,0:T(8,128)(2,1)}, u32[]{:S(2)}) copy-start(bf16[128,1152]{1,0:T(8,128)(2,1)} %copy-done.3) | copy-start | bytes 884740

commit v6 on v3

v6 whole, which is shorter than its diff:
```python
import functools

import jax
import jax.numpy as jnp
from jax import lax
from jax.experimental import pallas as pl
from jax.experimental.pallas import tpu as pltpu
from jax.sharding import Mesh
from jax.sharding import PartitionSpec as P

SWAP = [(0, 1), (1, 0)]
WID = ("x", "zhi")
TOK = ("th", "tl")
HEAD = ("zlo", "core")
N_Y = 8
N_PAIRS = 4
VMEM_LIMIT = 32 * 2**20
COST = pl.CostEstimate(flops=1, bytes_accessed=1, transcendentals=0)
LONG = pl.CostEstimate(flops=5 * 10**10, bytes_accessed=1, transcendentals=0)


def inner(v, where):
    return where((v % 4 == 1) | (v % 4 == 2), True, False)


def second(v, where):
    return where(inner(v, where), (3 - v) % N_Y, (7 - v) % N_Y)


def third(v, where):
    return where(inner(v, where), (7 - v) % N_Y, (3 - v) % N_Y)


def select(condition, one, other):
    return one if condition else other


def swapped(partner):
    return [
        ((v + core) % N_Y * 2 + core, (partner(v) + core) % N_Y * 2 + core)
        for v in range(N_Y)
        for core in range(2)
    ]


FIRST = swapped(lambda v: v ^ 1)
SECOND = swapped(lambda v: second(v, select))
THIRD = swapped(lambda v: third(v, select))
PARTS = (640, 512)


VMEM = pl.BlockSpec(memory_space=pltpu.VMEM)
SMEM = pl.BlockSpec(memory_space=pltpu.SMEM)
PARAMS = pltpu.CompilerParams(vmem_limit_bytes=VMEM_LIMIT)


def own_body(core, q_hbm, share_hbm, more_ref, out_ref, share_ref, sems):
    n_q = q_hbm.shape[1]
    q_copy = pltpu.make_async_copy(q_hbm, out_ref.at[:, pl.ds(0, n_q)], sems.at[0])
    share_copy = pltpu.make_async_copy(share_hbm, share_ref, sems.at[1])
    q_copy.start()
    share_copy.start()
    share_copy.wait()
    columns = pl.ds(pl.multiple_of(core[0] * 128, 128), 128)
    kv = share_ref[:, columns].astype(jnp.float32) + more_ref[:, columns].astype(jnp.float32)
    out_ref[:, n_q:] = kv.astype(out_ref.dtype)
    q_copy.wait()


def own_rows(core, q, share, more):
    hbm = pl.BlockSpec(memory_space=pltpu.HBM)
    return pl.pallas_call(
        own_body,
        out_shape=jax.ShapeDtypeStruct((q.shape[0], q.shape[1] + 128), q.dtype),
        in_specs=[SMEM, hbm, hbm, VMEM],
        out_specs=VMEM,
        scratch_shapes=[pltpu.VMEM(share.shape, share.dtype), pltpu.SemaphoreType.DMA((2,))],
        compiler_params=PARAMS,
        cost_estimate=COST,
    )(core, q, share, more)


def again_body(rows_ref, out_ref):
    out_ref[...] = rows_ref[...]


def again(rows):
    return pl.pallas_call(
        again_body,
        out_shape=jax.ShapeDtypeStruct(rows.shape, rows.dtype),
        in_specs=[VMEM],
        out_specs=VMEM,
        compiler_params=PARAMS,
        cost_estimate=LONG,
    )(rows)


def shifted(rows, by):
    n = lax.axis_size("x")
    return lax.ppermute(rows, "x", [(i, (i + by) % n) for i in range(n)])


def all_along_x(rows):
    moved_rows = {by: shifted(rows, by) for by in (1, 3, 2)}
    return [rows] + [moved_rows[by] for by in (1, 2, 3)]


def order_body(place, *refs):
    *parts, out_ref = refs
    n = len(parts) // 2
    x, zhi = place[0], place[1]
    for by in range(n):
        at = 2 * ((x + n - by) % n)
        out_ref[at + zhi] = parts[by][...]
        out_ref[at + 1 - zhi] = parts[n + by][...]


def in_order(place, near, far):
    rows, columns = near[0].shape
    parts = [*near, *far]
    return pl.pallas_call(
        order_body,
        out_shape=jax.ShapeDtypeStruct((len(parts), rows, columns), near[0].dtype),
        in_specs=[SMEM] + [VMEM] * len(parts),
        out_specs=VMEM,
        compiler_params=PARAMS,
        cost_estimate=COST,
    )(place, *parts).reshape(-1, columns)


def dot(left, right, dims):
    return lax.dot_general(left, right, ((dims[:1], dims[1:]), ((), ())), preferred_element_type=jnp.float32)


def give_body(blocks, x_ref, g_ref, *outs):
    for r in range(N_PAIRS):
        columns = x_ref[:, pl.ds(pl.multiple_of(blocks[r] * 128, 128), 128)]
        at = 0
        for out in outs:
            width = out.shape[-1]
            out[r] = dot(columns, g_ref[:, at : at + width], (0, 0)).astype(out.dtype)
            at += width


def give_terms(blocks, x, g):
    return pl.pallas_call(
        give_body,
        out_shape=[jax.ShapeDtypeStruct((N_PAIRS, 128, width), jnp.bfloat16) for width in PARTS],
        in_specs=[SMEM] + [VMEM] * 2,
        out_specs=[VMEM] * len(PARTS),
        compiler_params=PARAMS,
        cost_estimate=COST,
    )(blocks, x, g)


def keep_body(at, blocks, x_ref, g_ref, got_ref, give_ref, keep_ref):
    width = got_ref.shape[-1]
    for r in range(N_PAIRS):
        columns = x_ref[:, pl.ds(pl.multiple_of(blocks[r] * 128, 128), 128)]
        term = dot(columns, g_ref[:, at : at + width], (0, 0)) + got_ref[r].astype(jnp.float32)
        out = give_ref if r < 2 else keep_ref
        out[r % 2] = term.astype(out.dtype)


def keep_terms(blocks, x, g, got, at):
    return pl.pallas_call(
        functools.partial(keep_body, at),
        out_shape=[jax.ShapeDtypeStruct((2, *got.shape[1:]), jnp.bfloat16)] * 2,
        in_specs=[SMEM] + [VMEM] * 3,
        out_specs=[VMEM] * 2,
        compiler_params=PARAMS,
        cost_estimate=COST,
    )(blocks, x, g, got)


def add_body(*refs):
    *parts, keep_ref, give_ref = refs
    at = 0
    for kept, got in zip(parts[::2], parts[1::2]):
        width = kept.shape[-1]
        for r, out in enumerate((keep_ref, give_ref)):
            total = kept[r].astype(jnp.float32) + got[r].astype(jnp.float32)
            out[:, at : at + width] = total.astype(out.dtype)
        at += width


def add_terms(*parts):
    columns = sum(part.shape[-1] for part in parts[::2])
    return pl.pallas_call(
        add_body,
        out_shape=[jax.ShapeDtypeStruct((parts[0].shape[1], columns), jnp.bfloat16)] * 2,
        in_specs=[VMEM] * len(parts),
        out_specs=[VMEM] * 2,
        compiler_params=PARAMS,
        cost_estimate=COST,
    )(*parts)


def sum_body(input_kept, input_got, kept, got, input_out, q_ref, kv_ref):
    n_q = q_ref.shape[1]
    total = input_kept[...].astype(jnp.float32) + input_got[...].astype(jnp.float32)
    input_out[...] = total.astype(input_out.dtype)
    q_ref[...] = kept[:, :n_q].astype(jnp.float32) + got[:, :n_q].astype(jnp.float32)
    kv_ref[...] = kept[:, n_q:].astype(jnp.float32) + got[:, n_q:].astype(jnp.float32)


def last_sums(input_kept, input_got, kept, got, n_q):
    rows, columns = kept.shape
    outs = [
        jax.ShapeDtypeStruct(input_kept.shape, jnp.bfloat16),
        jax.ShapeDtypeStruct((rows, n_q), jnp.float32),
        jax.ShapeDtypeStruct((rows, columns - n_q), jnp.float32),
    ]
    block = lambda array: pl.BlockSpec(array.shape, lambda i: (0, 0))
    arrays = [input_kept, input_got, kept, got]
    return pl.pallas_call(
        sum_body,
        grid=(1,),
        out_shape=outs,
        in_specs=[block(array) for array in arrays],
        out_specs=[block(out) for out in outs],
        compiler_params=PARAMS,
        cost_estimate=COST,
    )(*arrays)


def input_body(blocks, g_ref, wq_ref, wkv_ref, *refs):
    n_q = wq_ref.shape[-1]
    term = dot(g_ref[:, :n_q], wq_ref[0], (1, 1))
    term = term + dot(g_ref[:, n_q:], wkv_ref[0], (1, 1))
    if len(refs) == 1:
        refs[0][0] = term.astype(jnp.bfloat16)
        return
    got_ref, *outs = refs
    term = (term + got_ref[0].astype(jnp.float32)).astype(jnp.bfloat16)
    for half, out in enumerate(outs):

        @pl.when(pl.program_id(0) // 2 == half)
        def _():
            out[0] = term


def input_terms(blocks, g, wq, wkv, *got):
    n_q, n_kv = wq.shape[1], wkv.shape[1]
    rows = g.shape[0]
    n = blocks.shape[0]
    pick = lambda r, blocks: (blocks[r], 0, 0)
    mine = lambda r, blocks: (r, 0, 0)
    block = (1, rows, 128)
    if got:
        places = [
            lambda r, blocks: (jnp.minimum(r, 1), 0, 0),
            lambda r, blocks: (jnp.maximum(r - 2, 0), 0, 0),
        ]
    else:
        places = [mine]
    return pl.pallas_call(
        input_body,
        grid_spec=pltpu.PrefetchScalarGridSpec(
            num_scalar_prefetch=1,
            grid=(n,),
            in_specs=[
                pl.BlockSpec(g.shape, lambda r, blocks: (0, 0)),
                pl.BlockSpec((1, 128, n_q), pick),
                pl.BlockSpec((1, 128, n_kv), pick),
            ]
            + [pl.BlockSpec(block, mine)] * len(got),
            out_specs=[pl.BlockSpec(block, place) for place in places],
        ),
        out_shape=[jax.ShapeDtypeStruct((n // len(places), rows, 128), jnp.bfloat16) for _ in places],
        compiler_params=PARAMS,
        cost_estimate=COST,
    )(blocks, g, wq.reshape(-1, 128, n_q), wkv.reshape(-1, 128, n_kv), *got)


def local(inputs, q_grad, key_value_share_gradient, q_weight, key_value_weight):
    q_columns = q_grad.shape[1]
    core = lax.axis_index("core")
    zhi = lax.axis_index("zhi")
    y = lax.axis_index(TOK)

    more = lax.ppermute(key_value_share_gradient, "core", SWAP)
    mine = own_rows(core.reshape(1), q_grad, key_value_share_gradient, more)
    far = lax.ppermute(mine, "zhi", SWAP)

    v = (y - core) % N_Y
    blocks_of = lambda at: jnp.stack(
        [second(at, jnp.where), third(second(at, jnp.where), jnp.where), at, third(at, jnp.where)]
    )
    keep_blocks = (blocks_of(v) + core) % N_Y
    give_blocks = (blocks_of(v + 1 - 2 * (v % 2)) + core) % N_Y
    zlo = lax.axis_index("zlo")
    heads = 2 * jnp.stack([zlo ^ 1, zlo ^ 3, zlo, zlo ^ 2])
    give_heads, keep_heads = heads + 1 - core, heads + core
    place = jnp.stack([lax.axis_index("x"), zhi])
    orders = (place, keep_blocks, give_blocks, give_heads, keep_heads)
    near = all_along_x(again(mine))
    far, orders = lax.optimization_barrier((far, orders))
    place, keep_blocks, give_blocks, give_heads, keep_heads = orders
    combined = in_order(place, near, all_along_x(far))

    def along_y(terms, pairs):
        return lax.ppermute(terms, (*TOK, "core"), pairs)

    given = give_terms(give_blocks, inputs, combined)
    first, for_input = lax.optimization_barrier((given[0], combined))
    got = [along_y(part, FIRST) for part in (first, *given[1:])]
    (give,) = input_terms(give_heads, for_input, q_weight, key_value_weight)
    core_got = lax.ppermute(give, "core", SWAP)
    give, input_keep = input_terms(keep_heads, for_input, q_weight, key_value_weight, core_got)
    input_got = lax.ppermute(give, "zlo", [(i, i ^ 1) for i in range(4)])

    after = input_keep
    parts = []
    at = 0
    for part in got:
        part, _ = lax.optimization_barrier((part, after))
        give, after = keep_terms(keep_blocks, inputs, combined, part, at)
        parts += [after, along_y(give, SECOND)]
        at += part.shape[-1]
    keep, give = add_terms(*parts)
    got = along_y(give, THIRD)

    input_keep, give = add_terms(input_keep, input_got)
    input_got = lax.ppermute(give, "zlo", [(i, i ^ 2) for i in range(4)])
    return last_sums(input_keep, input_got, keep, got, q_columns)


def solution(mesh):
    fine = Mesh(
        mesh.devices.reshape(4, 2, 4, 2, 4, 2), ("th", "tl", "zlo", "core", "x", "zhi")
    )
    return jax.shard_map(
        local,
        mesh=fine,
        in_specs=(
            P(TOK, WID),
            P((*TOK, *WID), HEAD),
            P((*TOK, *WID), HEAD),
            P(WID, HEAD),
            P(WID, HEAD),
        ),
        out_specs=(P(TOK, (*WID, *HEAD)), P((*WID, *TOK), HEAD), P((*WID, *TOK), HEAD)),
        check_vma=False,
    )
```

time: 113 us -> 93.8 us (0.83)
  the two profiles are of different devices: /device:TPU:2 before, /device:TPU:1 now
where the time goes in v6:
time: 93.8 us; the launch traced here: 93.1 us
  starting transfers between devices  61.4 us (65%)
  waiting for transfers between devices  18.2 us (19%)
  Pallas kernels  10.5 us (11%)
  local copies, waits for them, and re-layouts  1.68 us (2%)
  between operations  1.15 us (1%)
    ppermute x5, starting transfers between devices, along_y(): return lax.ppermute(terms, (*TOK, 'core'), pairs)  19.6 us
    ppermute x6, starting transfers between devices, shifted(): return lax.ppermute(rows, 'x', [(i, (i + by) % n) for i in range(n)])  18.5 us
    ppermute x1, starting transfers between devices, local(): more = lax.ppermute(key_value_share_gradient, 'core', SWAP)  8.79 us
    ppermute x6, waiting for transfers between devices, shifted(): return lax.ppermute(rows, 'x', [(i, (i + by) % n) for i in range(n)])  6.96 us
    ppermute x5, waiting for transfers between devices, along_y(): return lax.ppermute(terms, (*TOK, 'core'), pairs)  5.64 us
    ppermute x1, starting transfers between devices, local(): far = lax.ppermute(mine, 'zhi', SWAP)  5.39 us
    pallas_call x2, Pallas kernels, input_terms(): pl.pallas_call(input_body, grid_spec=pltpu.PrefetchScalarGridSpec(num_sca...  4.99 us
    ppermute x1, waiting for transfers between devices, local(): input_got = lax.ppermute(give, 'zlo', [(i, i ^ 2) for i in range(4)])  4.61 us
  transfers between devices with their start and end apart: 16, of which 7 were waited for; matrix products, arithmetic and copies ran while one was open for 0% of the time, Pallas kernels for 8%

profile of v6, /device:TPU:1, one launch (start us, length us, event | category | flops | bytes accessed | tf_op | source)
XLA Modules:
  0.0 93.1 jit_solution(14857096525952683069)
XLA Ops:
  0.6 8.8 %collective-permute-start = (bf16[64,256]{1,0:T(8,128)(2,1)}, bf16[64,256]{1,0:T(8,128)(2,1)S(1)}, u32[]{:S(2)}, u32[]{:S(2)}) collective-permute-start(bf16[64,256]{1,0:T(8,128)(2,1)} %share_hbm.1), channel_id=1, source_target_pairs={{0,8},{8,0},{1,9},{9,1},{2,10},{10,2},{3,11},{11,3},{4,12},{12,4},... | collective-permute-start | bytes 98312 | tf_op jit(solution)/shard_map/ppermute | solution.py:282
  9.4 0.1 broadcast_add_fusion
  9.5 1.0 %collective-permute-done.more_ref = bf16[64,256]{1,0:T(8,128)(2,1)S(1)} collective-permute-done((bf16[64,256]{1,0:T(8,128)(2,1)}, bf16[64,256]{1,0:T(8,128)(2,1)S(1)}, u32[]{:S(2)}, u32[]{:S(2)}) %collective-permute-start) | collective-permute-done | bytes 32800 | tf_op jit(solution)/shard_map/ppermute | solution.py:282
  10.5 0.9 copy-done.3
  11.4 0.8 copy-done.4
  12.1 0.1 shard_map.76.rows_ref
  12.3 0.0 copy-start
  12.3 5.4 %collective-permute-start.1 = (bf16[64,1152]{1,0:T(8,128)(2,1)S(1)}, bf16[64,1152]{1,0:T(8,128)(2,1)S(1)}, u32[]{:S(2)}, u32[]{:S(2)}) collective-permute-start(bf16[64,1152]{1,0:T(8,128)(2,1)S(1)} %shard_map.76.rows_ref), channel_id=1, source_target_pairs={{0,1},{1,0},{2,3},{3,2},{4,5},{5,4},{6,7},{7,6},{8,9},{9,8},{10,11... | collective-permute-start | bytes 442376 | tf_op jit(solution)/shard_map/ppermute | solution.py:284
  17.7 4.4 %collective-permute-start.4 = (bf16[64,1152]{1,0:T(8,128)(2,1)S(1)}, bf16[64,1152]{1,0:T(8,128)(2,1)S(1)}, u32[]{:S(2)}, u32[]{:S(2)}) collective-permute-start(bf16[64,1152]{1,0:T(8,128)(2,1)S(1)} %shard_map.77.refs_0_), channel_id=1, source_target_pairs={{0,6},{2,0},{4,2},{6,4},{1,7},{3,1},{5,3},{7,5},{8,14},{10,8},{12,... | collective-permute-start | bytes 442376 | tf_op jit(solution)/shard_map/ppermute | solution.py:100
  22.1 0.1 pad_add_fusion.place
  22.3 0.1 and_select_fusion
  22.4 2.4 %collective-permute-start.3 = (bf16[64,1152]{1,0:T(8,128)(2,1)S(1)}, bf16[64,1152]{1,0:T(8,128)(2,1)S(1)}, u32[]{:S(2)}, u32[]{:S(2)}) collective-permute-start(bf16[64,1152]{1,0:T(8,128)(2,1)S(1)} %shard_map.77.refs_0_), channel_id=1, source_target_pairs={{0,4},{2,6},{4,0},{6,2},{1,5},{3,7},{5,1},{7,3},{8,12},{10,14},{12... | collective-permute-start | bytes 442376 | tf_op jit(solution)/shard_map/ppermute | solution.py:100
  24.9 2.5 %collective-permute-start.2 = (bf16[64,1152]{1,0:T(8,128)(2,1)S(1)}, bf16[64,1152]{1,0:T(8,128)(2,1)S(1)}, u32[]{:S(2)}, u32[]{:S(2)}) collective-permute-start(bf16[64,1152]{1,0:T(8,128)(2,1)S(1)} %shard_map.77.refs_0_), channel_id=1, source_target_pairs={{0,2},{2,4},{4,6},{6,0},{1,3},{3,5},{5,7},{7,1},{8,10},{10,12},{12... | collective-permute-start | bytes 442376 | tf_op jit(solution)/shard_map/ppermute | solution.py:100
  27.4 0.0 collective-permute-done.1.refs_4_
  27.4 0.0 copy-start.1
  27.4 0.0 copy-start.2
  27.4 4.1 %collective-permute-start.7 = (bf16[64,1152]{1,0:T(8,128)(2,1)S(1)}, bf16[64,1152]{1,0:T(8,128)(2,1)S(1)}, u32[]{:S(2)}, u32[]{:S(2)}) collective-permute-start(bf16[64,1152]{1,0:T(8,128)(2,1)S(1)} %collective-permute-done.1.refs_4_), channel_id=1, source_target_pairs={{0,6},{2,0},{4,2},{6,4},{1,7},{3,1},{5,3},{7,5},{8,14},{10,8},{12,... | collective-permute-start | bytes 442376 | tf_op jit(solution)/shard_map/ppermute | solution.py:100
  31.5 3.1 %collective-permute-start.6 = (bf16[64,1152]{1,0:T(8,128)(2,1)S(1)}, bf16[64,1152]{1,0:T(8,128)(2,1)S(1)}, u32[]{:S(2)}, u32[]{:S(2)}) collective-permute-start(bf16[64,1152]{1,0:T(8,128)(2,1)S(1)} %collective-permute-done.1.refs_4_), channel_id=1, source_target_pairs={{0,4},{2,6},{4,0},{6,2},{1,5},{3,7},{5,1},{7,3},{8,12},{10,14},{12... | collective-permute-start | bytes 442376 | tf_op jit(solution)/shard_map/ppermute | solution.py:100
  34.7 0.0 collective-permute-done.4.refs_3_
  34.7 1.9 %collective-permute-start.5 = (bf16[64,1152]{1,0:T(8,128)(2,1)S(1)}, bf16[64,1152]{1,0:T(8,128)(2,1)S(1)}, u32[]{:S(2)}, u32[]{:S(2)}) collective-permute-start(bf16[64,1152]{1,0:T(8,128)(2,1)S(1)} %collective-permute-done.1.refs_4_), channel_id=1, source_target_pairs={{0,2},{2,4},{4,6},{6,0},{1,3},{3,5},{5,7},{7,1},{8,10},{10,12},{12... | collective-permute-start | bytes 442376 | tf_op jit(solution)/shard_map/ppermute | solution.py:100
  36.6 0.0 collective-permute-done.3.refs_2_
  36.6 0.0 collective-permute-done.2.refs_1_
  36.7 0.0 collective-permute-done.7.refs_7_
  36.7 2.3 %collective-permute-done.6.refs_6_ = bf16[64,1152]{1,0:T(8,128)(2,1)S(1)} collective-permute-done((bf16[64,1152]{1,0:T(8,128)(2,1)S(1)}, bf16[64,1152]{1,0:T(8,128)(2,1)S(1)}, u32[]{:S(2)}, u32[]{:S(2)}) %collective-permute-start.6) | collective-permute-done | bytes 147488 | tf_op jit(solution)/shard_map/ppermute | solution.py:100
  38.9 4.7 %collective-permute-done.5.refs_5_ = bf16[64,1152]{1,0:T(8,128)(2,1)S(1)} collective-permute-done((bf16[64,1152]{1,0:T(8,128)(2,1)S(1)}, bf16[64,1152]{1,0:T(8,128)(2,1)S(1)}, u32[]{:S(2)}, u32[]{:S(2)}) %collective-permute-start.5) | collective-permute-done | bytes 147488 | tf_op jit(solution)/shard_map/ppermute | solution.py:100
  43.6 0.6 shard_map.78
  44.3 1.4 %shard_map.79 = (bf16[4,128,640]{2,1,0:T(8,128)(2,1)S(1)}, bf16[4,128,512]{2,1,0:T(8,128)(2,1)S(1)}) custom-call(s32[4]{0:T(128)S(1)} %get-tuple-element.26.blocks, bf16[512,1024]{1,0:T(8,128)(2,1)S(1)} %copy-done, bf16[512,1152]{1,0:T(8,128)(2,1)S(1)} %bitcast.18), custom_call_target="tpu_custom_call" | custom-call | flops 1 | bytes 1 | tf_op jit(solution)/shard_map/pallas_call | solution.py:146
  45.7 5.1 %collective-permute-start.11 = (bf16[4,128,640]{2,1,0:T(8,128)(2,1)S(1)}, bf16[4,128,640]{2,1,0:T(8,128)(2,1)S(1)}, u32[]{:S(2)}, u32[]{:S(2)}) collective-permute-start(bf16[4,128,640]{2,1,0:T(8,128)(2,1)S(1)} %get-tuple-element.37), channel_id=1, source_target_pairs={{0,64},{72,136},{64,0},{136,72},{128,192},{200,264},{192,128},{264... | collective-permute-start | bytes 1966088 | tf_op jit(solution)/shard_map/ppermute | solution.py:303
  50.8 2.5 %shard_map.80 = bf16[4,512,128]{2,1,0:T(8,128)(2,1)S(1)} custom-call(s32[4]{0:T(128)S(1)} %add_subtract_fusion.blocks, bf16[512,1152]{1,0:T(8,128)(2,1)S(1)} %bitcast.19, bf16[8,128,1024]{2,1,0:T(8,128)(2,1)S(1)} %bitcast.23, bf16[8,128,128]{2,1,0:T(8,128)(2,1)S(1)} %bitcast.25), custom_call_target="tpu_custom_call" | custom-call | flops 1 | bytes 1 | tf_op jit(solution)/shard_map/pallas_call | solution.py:257
  53.3 2.0 %collective-permute-start.8 = (bf16[4,512,128]{2,1,0:T(8,128)(2,1)S(1)}, bf16[4,512,128]{2,1,0:T(8,128)(2,1)S(1)}, u32[]{:S(2)}, u32[]{:S(2)}) collective-permute-start(bf16[4,512,128]{2,1,0:T(8,128)(2,1)S(1)} %shard_map.80), channel_id=1, source_target_pairs={{0,8},{8,0},{1,9},{9,1},{2,10},{10,2},{3,11},{11,3},{4,12},{12,4},... | collective-permute-start | bytes 1572872 | tf_op jit(solution)/shard_map/ppermute | solution.py:309
  55.3 4.9 %collective-permute-start.13 = (bf16[4,128,512]{2,1,0:T(8,128)(2,1)S(1)}, bf16[4,128,512]{2,1,0:T(8,128)(2,1)S(1)}, u32[]{:S(2)}, u32[]{:S(2)}) collective-permute-start(bf16[4,128,512]{2,1,0:T(8,128)(2,1)S(1)} %get-tuple-element.41), channel_id=1, source_target_pairs={{0,64},{72,136},{64,0},{136,72},{128,192},{200,264},{192,128},{264... | collective-permute-start | bytes 1572872 | tf_op jit(solution)/shard_map/ppermute | solution.py:303
  60.2 0.0 collective-permute-done.8.refs_0_
  60.2 2.5 %shard_map.81 = (bf16[2,512,128]{2,1,0:T(8,128)(2,1)S(1)}, bf16[2,512,128]{2,1,0:T(8,128)(2,1)S(1)}) custom-call(s32[4]{0:T(128)S(1)} %get-tuple-element.25.blocks, bf16[512,1152]{1,0:T(8,128)(2,1)S(1)} %bitcast.20, bf16[8,128,1024]{2,1,0:T(8,128)(2,1)S(1)} %bitcast.24, bf16[8,128,128]{2,1,0:T(8,128)(2,1)S(1)} %bitcast.26, ...), custom_call_target="tpu_custom_call" | custom-call | flops 1 | bytes 1 | tf_op jit(solution)/shard_map/pallas_call | solution.py:257
  62.8 1.2 %shard_map.83 = (bf16[2,128,640]{2,1,0:T(8,128)(2,1)S(1)}, bf16[2,128,640]{2,1,0:T(8,128)(2,1)S(1)}) custom-call(s32[4]{0:T(128)S(1)} %get-tuple-element.36.blocks, bf16[512,1024]{1,0:T(8,128)(2,1)S(1)} %copy-done, bf16[512,1152]{1,0:T(8,128)(2,1)S(1)} %bitcast.21, bf16[4,128,640]{2,1,0:T(8,128)(2,1)S(1)} %collective-permute-done.11.got_ref), custom_call_target="tpu_custom_call" | custom-call | flops 1 | bytes 1 | tf_op jit(solution)/shard_map/pallas_call | solution.py:166
  63.9 1.9 %collective-permute-start.12 = (bf16[2,128,640]{2,1,0:T(8,128)(2,1)S(1)}, bf16[2,128,640]{2,1,0:T(8,128)(2,1)S(1)}, u32[]{:S(2)}, u32[]{:S(2)}) collective-permute-start(bf16[2,128,640]{2,1,0:T(8,128)(2,1)S(1)} %get-tuple-element.40), channel_id=1, source_target_pairs={{0,448},{72,8},{64,128},{136,200},{128,64},{200,136},{192,256},{26... | collective-permute-start | bytes 983048 | tf_op jit(solution)/shard_map/ppermute | solution.py:303
  65.9 0.9 collective-permute-done.13.got_ref
  66.8 1.0 %shard_map.84 = (bf16[2,128,512]{2,1,0:T(8,128)(2,1)S(1)}, bf16[2,128,512]{2,1,0:T(8,128)(2,1)S(1)}) custom-call(s32[4]{0:T(128)S(1)} %get-tuple-element.36.blocks, bf16[512,1024]{1,0:T(8,128)(2,1)S(1)} %copy-done, bf16[512,1152]{1,0:T(8,128)(2,1)S(1)} %bitcast.22, bf16[4,128,512]{2,1,0:T(8,128)(2,1)S(1)} %collective-permute-done.13.got_ref), custom_call_target="tpu_custom_call" | custom-call | flops 1 | bytes 1 | tf_op jit(solution)/shard_map/pallas_call | solution.py:166
  67.8 2.5 %collective-permute-start.14 = (bf16[2,128,512]{2,1,0:T(8,128)(2,1)S(1)}, bf16[2,128,512]{2,1,0:T(8,128)(2,1)S(1)}, u32[]{:S(2)}, u32[]{:S(2)}) collective-permute-start(bf16[2,128,512]{2,1,0:T(8,128)(2,1)S(1)} %get-tuple-element.44), channel_id=1, source_target_pairs={{0,448},{72,8},{64,128},{136,200},{128,64},{200,136},{192,256},{26... | collective-permute-start | bytes 786440 | tf_op jit(solution)/shard_map/ppermute | solution.py:303
  70.3 3.1 %collective-permute-start.9 = (bf16[2,512,128]{2,1,0:T(8,128)(2,1)S(1)}, bf16[2,512,128]{2,1,0:T(8,128)(2,1)S(1)}, u32[]{:S(2)}, u32[]{:S(2)}) collective-permute-start(bf16[2,512,128]{2,1,0:T(8,128)(2,1)S(1)} %get-tuple-element.33), channel_id=1, source_target_pairs={{0,16},{16,0},{32,48},{48,32},{1,17},{17,1},{33,49},{49,33},{2,18}... | collective-permute-start | bytes 786440 | tf_op jit(solution)/shard_map/ppermute | solution.py:311
  73.4 1.8 %collective-permute-done.14.refs_3_ = bf16[2,128,512]{2,1,0:T(8,128)(2,1)S(1)} collective-permute-done((bf16[2,128,512]{2,1,0:T(8,128)(2,1)S(1)}, bf16[2,128,512]{2,1,0:T(8,128)(2,1)S(1)}, u32[]{:S(2)}, u32[]{:S(2)}) %collective-permute-start.14) | collective-permute-done | bytes 262176 | tf_op jit(solution)/shard_map/ppermute | solution.py:303
  75.2 0.1 shard_map.85
  75.4 5.2 %collective-permute-start.15 = (bf16[128,1152]{1,0:T(8,128)(2,1)S(1)}, bf16[128,1152]{1,0:T(8,128)(2,1)S(1)}, u32[]{:S(2)}, u32[]{:S(2)}) collective-permute-start(bf16[128,1152]{1,0:T(8,128)(2,1)S(1)} %get-tuple-element.46), channel_id=1, source_target_pairs={{0,192},{72,264},{64,384},{136,456},{128,320},{200,392},{192,0},{2... | collective-permute-start | bytes 884744 | tf_op jit(solution)/shard_map/ppermute | solution.py:303
  80.6 0.0 collective-permute-done.9.refs_1_
  80.6 0.1 shard_map.82
  80.7 4.0 %collective-permute-start.10 = (bf16[512,128]{1,0:T(8,128)(2,1)S(1)}, bf16[512,128]{1,0:T(8,128)(2,1)S(1)}, u32[]{:S(2)}, u32[]{:S(2)}) collective-permute-start(bf16[512,128]{1,0:T(8,128)(2,1)S(1)} %get-tuple-element.35), channel_id=1, source_target_pairs={{0,32},{16,48},{32,0},{48,16},{1,33},{17,49},{33,1},{49,17},{2,34}... | collective-permute-start | bytes 393224 | tf_op jit(solution)/shard_map/ppermute | solution.py:325
  84.7 4.6 %collective-permute-done.10.input_got = bf16[512,128]{1,0:T(8,128)(2,1)S(1)} collective-permute-done((bf16[512,128]{1,0:T(8,128)(2,1)S(1)}, bf16[512,128]{1,0:T(8,128)(2,1)S(1)}, u32[]{:S(2)}, u32[]{:S(2)}) %collective-permute-start.10) | collective-permute-done | bytes 131104 | tf_op jit(solution)/shard_map/ppermute | solution.py:325
  89.3 2.9 %collective-permute-done.15.got = bf16[128,1152]{1,0:T(8,128)(2,1)S(1)} collective-permute-done((bf16[128,1152]{1,0:T(8,128)(2,1)S(1)}, bf16[128,1152]{1,0:T(8,128)(2,1)S(1)}, u32[]{:S(2)}, u32[]{:S(2)}) %collective-permute-start.15) | collective-permute-done | bytes 294944 | tf_op jit(solution)/shard_map/ppermute | solution.py:303
  92.2 0.9 shard_map.86
  (9 shorter events, 0.0 us)
Async XLA Ops:
  0.6 9.8 %collective-permute-start = (bf16[64,256]{1,0:T(8,128)(2,1)}, bf16[64,256]{1,0:T(8,128)(2,1)S(1)}, u32[]{:S(2)}, u32[]{:S(2)}) collective-permute-start(bf16[64,256]{1,0:T(8,128)(2,1)} %share_hbm.1), channel_id=1, source_target_pairs={{0,8},{8,0},{1,9},{9,1},{2,10},{10,2},{3,11},{11,3},{4,12},{12,4},... | collective-permute-start | bytes 98312 | tf_op jit(solution)/shard_map/ppermute | solution.py:282
  10.5 0.9 copy-start.3
  11.4 0.8 copy-start.4
  12.3 32.0 %copy-start = (bf16[512,1024]{1,0:T(8,128)(2,1)S(1)}, bf16[512,1024]{1,0:T(8,128)(2,1)}, u32[]{:S(2)}) copy-start(bf16[512,1024]{1,0:T(8,128)(2,1)} %x_ref.5) | copy-start | bytes 3145732
  12.3 15.1 %collective-permute-start.1 = (bf16[64,1152]{1,0:T(8,128)(2,1)S(1)}, bf16[64,1152]{1,0:T(8,128)(2,1)S(1)}, u32[]{:S(2)}, u32[]{:S(2)}) collective-permute-start(bf16[64,1152]{1,0:T(8,128)(2,1)S(1)} %shard_map.76.rows_ref), channel_id=1, source_target_pairs={{0,1},{1,0},{2,3},{3,2},{4,5},{5,4},{6,7},{7,6},{8,9},{9,8},{10,11... | collective-permute-start | bytes 442376 | tf_op jit(solution)/shard_map/ppermute | solution.py:284
  17.7 17.0 %collective-permute-start.4 = (bf16[64,1152]{1,0:T(8,128)(2,1)S(1)}, bf16[64,1152]{1,0:T(8,128)(2,1)S(1)}, u32[]{:S(2)}, u32[]{:S(2)}) collective-permute-start(bf16[64,1152]{1,0:T(8,128)(2,1)S(1)} %shard_map.77.refs_0_), channel_id=1, source_target_pairs={{0,6},{2,0},{4,2},{6,4},{1,7},{3,1},{5,3},{7,5},{8,14},{10,8},{12,... | collective-permute-start | bytes 442376 | tf_op jit(solution)/shard_map/ppermute | solution.py:100
  22.4 14.2 %collective-permute-start.3 = (bf16[64,1152]{1,0:T(8,128)(2,1)S(1)}, bf16[64,1152]{1,0:T(8,128)(2,1)S(1)}, u32[]{:S(2)}, u32[]{:S(2)}) collective-permute-start(bf16[64,1152]{1,0:T(8,128)(2,1)S(1)} %shard_map.77.refs_0_), channel_id=1, source_target_pairs={{0,4},{2,6},{4,0},{6,2},{1,5},{3,7},{5,1},{7,3},{8,12},{10,14},{12... | collective-permute-start | bytes 442376 | tf_op jit(solution)/shard_map/ppermute | solution.py:100
  24.9 11.8 %collective-permute-start.2 = (bf16[64,1152]{1,0:T(8,128)(2,1)S(1)}, bf16[64,1152]{1,0:T(8,128)(2,1)S(1)}, u32[]{:S(2)}, u32[]{:S(2)}) collective-permute-start(bf16[64,1152]{1,0:T(8,128)(2,1)S(1)} %shard_map.77.refs_0_), channel_id=1, source_target_pairs={{0,2},{2,4},{4,6},{6,0},{1,3},{3,5},{5,7},{7,1},{8,10},{10,12},{12... | collective-permute-start | bytes 442376 | tf_op jit(solution)/shard_map/ppermute | solution.py:100
  27.4 23.4 %copy-start.1 = (bf16[1024,1024]{1,0:T(8,128)(2,1)S(1)}, bf16[1024,1024]{1,0:T(8,128)(2,1)}, u32[]{:S(2)}) copy-start(bf16[1024,1024]{1,0:T(8,128)(2,1)} %param.8) | copy-start | bytes 6291460
  27.4 23.4 %copy-start.2 = (bf16[1024,128]{1,0:T(8,128)(2,1)S(1)}, bf16[1024,128]{1,0:T(8,128)(2,1)}, u32[]{:S(2)}) copy-start(bf16[1024,128]{1,0:T(8,128)(2,1)} %param.9) | copy-start | bytes 786436
  27.4 9.2 %collective-permute-start.7 = (bf16[64,1152]{1,0:T(8,128)(2,1)S(1)}, bf16[64,1152]{1,0:T(8,128)(2,1)S(1)}, u32[]{:S(2)}, u32[]{:S(2)}) collective-permute-start(bf16[64,1152]{1,0:T(8,128)(2,1)S(1)} %collective-permute-done.1.refs_4_), channel_id=1, source_target_pairs={{0,6},{2,0},{4,2},{6,4},{1,7},{3,1},{5,3},{7,5},{8,14},{10,8},{12,... | collective-permute-start | bytes 442376 | tf_op jit(solution)/shard_map/ppermute | solution.py:100
  31.5 7.4 %collective-permute-start.6 = (bf16[64,1152]{1,0:T(8,128)(2,1)S(1)}, bf16[64,1152]{1,0:T(8,128)(2,1)S(1)}, u32[]{:S(2)}, u32[]{:S(2)}) collective-permute-start(bf16[64,1152]{1,0:T(8,128)(2,1)S(1)} %collective-permute-done.1.refs_4_), channel_id=1, source_target_pairs={{0,4},{2,6},{4,0},{6,2},{1,5},{3,7},{5,1},{7,3},{8,12},{10,14},{12... | collective-permute-start | bytes 442376 | tf_op jit(solution)/shard_map/ppermute | solution.py:100
  34.7 8.9 %collective-permute-start.5 = (bf16[64,1152]{1,0:T(8,128)(2,1)S(1)}, bf16[64,1152]{1,0:T(8,128)(2,1)S(1)}, u32[]{:S(2)}, u32[]{:S(2)}) collective-permute-start(bf16[64,1152]{1,0:T(8,128)(2,1)S(1)} %collective-permute-done.1.refs_4_), channel_id=1, source_target_pairs={{0,2},{2,4},{4,6},{6,0},{1,3},{3,5},{5,7},{7,1},{8,10},{10,12},{12... | collective-permute-start | bytes 442376 | tf_op jit(solution)/shard_map/ppermute | solution.py:100
  45.7 17.0 %collective-permute-start.11 = (bf16[4,128,640]{2,1,0:T(8,128)(2,1)S(1)}, bf16[4,128,640]{2,1,0:T(8,128)(2,1)S(1)}, u32[]{:S(2)}, u32[]{:S(2)}) collective-permute-start(bf16[4,128,640]{2,1,0:T(8,128)(2,1)S(1)} %get-tuple-element.37), channel_id=1, source_target_pairs={{0,64},{72,136},{64,0},{136,72},{128,192},{200,264},{192,128},{264... | collective-permute-start | bytes 1966088 | tf_op jit(solution)/shard_map/ppermute | solution.py:303
  53.3 6.9 %collective-permute-start.8 = (bf16[4,512,128]{2,1,0:T(8,128)(2,1)S(1)}, bf16[4,512,128]{2,1,0:T(8,128)(2,1)S(1)}, u32[]{:S(2)}, u32[]{:S(2)}) collective-permute-start(bf16[4,512,128]{2,1,0:T(8,128)(2,1)S(1)} %shard_map.80), channel_id=1, source_target_pairs={{0,8},{8,0},{1,9},{9,1},{2,10},{10,2},{3,11},{11,3},{4,12},{12,4},... | collective-permute-start | bytes 1572872 | tf_op jit(solution)/shard_map/ppermute | solution.py:309
  55.3 11.4 %collective-permute-start.13 = (bf16[4,128,512]{2,1,0:T(8,128)(2,1)S(1)}, bf16[4,128,512]{2,1,0:T(8,128)(2,1)S(1)}, u32[]{:S(2)}, u32[]{:S(2)}) collective-permute-start(bf16[4,128,512]{2,1,0:T(8,128)(2,1)S(1)} %get-tuple-element.41), channel_id=1, source_target_pairs={{0,64},{72,136},{64,0},{136,72},{128,192},{200,264},{192,128},{264... | collective-permute-start | bytes 1572872 | tf_op jit(solution)/shard_map/ppermute | solution.py:303
  63.9 11.3 %collective-permute-start.12 = (bf16[2,128,640]{2,1,0:T(8,128)(2,1)S(1)}, bf16[2,128,640]{2,1,0:T(8,128)(2,1)S(1)}, u32[]{:S(2)}, u32[]{:S(2)}) collective-permute-start(bf16[2,128,640]{2,1,0:T(8,128)(2,1)S(1)} %get-tuple-element.40), channel_id=1, source_target_pairs={{0,448},{72,8},{64,128},{136,200},{128,64},{200,136},{192,256},{26... | collective-permute-start | bytes 983048 | tf_op jit(solution)/shard_map/ppermute | solution.py:303
  67.8 7.4 %collective-permute-start.14 = (bf16[2,128,512]{2,1,0:T(8,128)(2,1)S(1)}, bf16[2,128,512]{2,1,0:T(8,128)(2,1)S(1)}, u32[]{:S(2)}, u32[]{:S(2)}) collective-permute-start(bf16[2,128,512]{2,1,0:T(8,128)(2,1)S(1)} %get-tuple-element.44), channel_id=1, source_target_pairs={{0,448},{72,8},{64,128},{136,200},{128,64},{200,136},{192,256},{26... | collective-permute-start | bytes 786440 | tf_op jit(solution)/shard_map/ppermute | solution.py:303
  70.3 10.3 %collective-permute-start.9 = (bf16[2,512,128]{2,1,0:T(8,128)(2,1)S(1)}, bf16[2,512,128]{2,1,0:T(8,128)(2,1)S(1)}, u32[]{:S(2)}, u32[]{:S(2)}) collective-permute-start(bf16[2,512,128]{2,1,0:T(8,128)(2,1)S(1)} %get-tuple-element.33), channel_id=1, source_target_pairs={{0,16},{16,0},{32,48},{48,32},{1,17},{17,1},{33,49},{49,33},{2,18}... | collective-permute-start | bytes 786440 | tf_op jit(solution)/shard_map/ppermute | solution.py:311
  75.4 16.9 %collective-permute-start.15 = (bf16[128,1152]{1,0:T(8,128)(2,1)S(1)}, bf16[128,1152]{1,0:T(8,128)(2,1)S(1)}, u32[]{:S(2)}, u32[]{:S(2)}) collective-permute-start(bf16[128,1152]{1,0:T(8,128)(2,1)S(1)} %get-tuple-element.46), channel_id=1, source_target_pairs={{0,192},{72,264},{64,384},{136,456},{128,320},{200,392},{192,0},{2... | collective-permute-start | bytes 884744 | tf_op jit(solution)/shard_map/ppermute | solution.py:303
  80.7 8.6 %collective-permute-start.10 = (bf16[512,128]{1,0:T(8,128)(2,1)S(1)}, bf16[512,128]{1,0:T(8,128)(2,1)S(1)}, u32[]{:S(2)}, u32[]{:S(2)}) collective-permute-start(bf16[512,128]{1,0:T(8,128)(2,1)S(1)} %get-tuple-element.35), channel_id=1, source_target_pairs={{0,32},{16,48},{32,0},{48,16},{1,33},{17,49},{33,1},{49,17},{2,34}... | collective-permute-start | bytes 393224 | tf_op jit(solution)/shard_map/ppermute | solution.py:325

commit v7 on v6

--- a/solution.py
+++ b/solution.py
@@ -95,37 +95,38 @@
     )(rows)
 
 
-def shifted(rows, by):
-    n = lax.axis_size("x")
-    return lax.ppermute(rows, "x", [(i, (i + by) % n) for i in range(n)])
+def x_swap(rows, partner):
+    pairs = [
+        (core * 4 + (u + core) % 4, core * 4 + (partner(u) + core) % 4)
+        for core in range(2)
+        for u in range(4)
+    ]
+    return lax.ppermute(rows, ("core", "x"), pairs)
 
 
 def all_along_x(rows):
-    moved_rows = {by: shifted(rows, by) for by in (1, 3, 2)}
-    return [rows] + [moved_rows[by] for by in (1, 2, 3)]
+    pair = jnp.stack([rows, x_swap(rows, lambda u: u ^ 1)])
+    return pair, x_swap(pair, lambda u: 3 - u)
 
 
 def order_body(place, *refs):
-    *parts, out_ref = refs
-    n = len(parts) // 2
-    x, zhi = place[0], place[1]
-    for by in range(n):
-        at = 2 * ((x + n - by) % n)
-        out_ref[at + zhi] = parts[by][...]
-        out_ref[at + 1 - zhi] = parts[n + by][...]
-
-
-def in_order(place, near, far):
-    rows, columns = near[0].shape
-    parts = [*near, *far]
+    *pairs, out_ref = refs
+    for i, pair in enumerate(pairs):
+        zhi = place[4] if i < 2 else 1 - place[4]
+        for j in range(2):
+            out_ref[2 * place[2 * (i % 2) + j] + zhi] = pair[j]
+
+
+def in_order(place, *pairs):
+    _, rows, columns = pairs[0].shape
     return pl.pallas_call(
         order_body,
-        out_shape=jax.ShapeDtypeStruct((len(parts), rows, columns), near[0].dtype),
-        in_specs=[SMEM] + [VMEM] * len(parts),
+        out_shape=jax.ShapeDtypeStruct((2 * len(pairs), rows, columns), pairs[0].dtype),
+        in_specs=[SMEM] + [VMEM] * len(pairs),
         out_specs=VMEM,
         compiler_params=PARAMS,
         cost_estimate=COST,
-    )(place, *parts).reshape(-1, columns)
+    )(place, *pairs).reshape(-1, columns)
 
 
 def dot(left, right, dims):
@@ -280,7 +281,7 @@
     y = lax.axis_index(TOK)
 
     more = lax.ppermute(key_value_share_gradient, "core", SWAP)
-    mine = own_rows(core.reshape(1), q_grad, key_value_share_gradient, more)
+    mine = own_rows(core.reshape(1), again(q_grad), key_value_share_gradient, more)
     far = lax.ppermute(mine, "zhi", SWAP)
 
     v = (y - core) % N_Y
@@ -292,12 +293,14 @@
     zlo = lax.axis_index("zlo")
     heads = 2 * jnp.stack([zlo ^ 1, zlo ^ 3, zlo, zlo ^ 2])
     give_heads, keep_heads = heads + 1 - core, heads + core
-    place = jnp.stack([lax.axis_index("x"), zhi])
+    u = (lax.axis_index("x") - core) % 4
+    place = jnp.stack([u, u ^ 1, 3 - u, (3 - u) ^ 1, zhi - core])
+    place = (place + core) % 4
     orders = (place, keep_blocks, give_blocks, give_heads, keep_heads)
     near = all_along_x(again(mine))
     far, orders = lax.optimization_barrier((far, orders))
     place, keep_blocks, give_blocks, give_heads, keep_heads = orders
-    combined = in_order(place, near, all_along_x(far))
+    combined = in_order(place, *near, *all_along_x(far))
 
     def along_y(terms, pairs):
         return lax.ppermute(terms, (*TOK, "core"), pairs)

time: 93.8 us -> 89.5 us (0.954)
  the two profiles are of different devices: /device:TPU:1 before, /device:TPU:6 now
where the time goes in v7:
time: 89.5 us; the launch traced here: 88.4 us
  starting transfers between devices  62 us (69%)
  waiting for transfers between devices  13 us (15%)
  Pallas kernels  10.5 us (12%)
  local copies, waits for them, and re-layouts  1.41 us (2%)
  between operations  1.23 us (1%)
    ppermute x5, starting transfers between devices, along_y(): return lax.ppermute(terms, (*TOK, 'core'), pairs)  20.5 us
    ppermute x4, starting transfers between devices, x_swap(): return lax.ppermute(rows, ('core', 'x'), pairs)  13.8 us
    ppermute x1, starting transfers between devices, local(): far = lax.ppermute(mine, 'zhi', SWAP)  11 us
    ppermute x1, starting transfers between devices, local(): input_got = lax.ppermute(give, 'zlo', [(i, i ^ 1) for i in range(4)])  7.2 us
    ppermute x4, waiting for transfers between devices, x_swap(): return lax.ppermute(rows, ('core', 'x'), pairs)  5.83 us
    ppermute x1, starting transfers between devices, local(): input_got = lax.ppermute(give, 'zlo', [(i, i ^ 2) for i in range(4)])  5.64 us
    ppermute x1, waiting for transfers between devices, local(): input_got = lax.ppermute(give, 'zlo', [(i, i ^ 2) for i in range(4)])  5.28 us
    pallas_call x2, Pallas kernels, input_terms(): pl.pallas_call(input_body, grid_spec=pltpu.PrefetchScalarGridSpec(num_sca...  5.01 us
  transfers between devices with their start and end apart: 14, of which 7 were waited for; matrix products, arithmetic and copies ran while one was open for 0% of the time, Pallas kernels for 8%

profile of v7, /device:TPU:6, one launch (start us, length us, event | category | flops | bytes accessed | tf_op | source)
XLA Modules:
  0.0 88.4 jit_solution(1586599202259569388)
XLA Ops:
  0.6 1.9 %collective-permute-start = (bf16[64,256]{1,0:T(8,128)(2,1)}, bf16[64,256]{1,0:T(8,128)(2,1)S(1)}, u32[]{:S(2)}, u32[]{:S(2)}) collective-permute-start(bf16[64,256]{1,0:T(8,128)(2,1)} %share_hbm.1), channel_id=1, source_target_pairs={{0,8},{8,0},{1,9},{9,1},{2,10},{10,2},{3,11},{11,3},{4,12},{12,4},... | collective-permute-start | bytes 98312 | tf_op jit(solution)/shard_map/ppermute | solution.py:283
  2.6 0.1 stack.86
  2.7 0.9 %copy-done.4 = bf16[64,1024]{1,0:T(8,128)(2,1)S(1)} copy-done((bf16[64,1024]{1,0:T(8,128)(2,1)S(1)}, bf16[64,1024]{1,0:T(8,128)(2,1)}, u32[]{:S(2)}) %copy-start.4) | copy-done | bytes 131096
  3.6 0.1 broadcast_add_fusion
  3.7 0.3 collective-permute-done.more_ref
  3.9 0.4 copy-done.3
  4.4 0.1 shard_map.77.rows_ref
  4.5 0.0 copy-start
  4.5 11.0 %collective-permute-start.1 = (bf16[64,1152]{1,0:T(8,128)(2,1)S(1)}, bf16[64,1152]{1,0:T(8,128)(2,1)S(1)}, u32[]{:S(2)}, u32[]{:S(2)}) collective-permute-start(bf16[64,1152]{1,0:T(8,128)(2,1)S(1)} %shard_map.77.rows_ref), channel_id=1, source_target_pairs={{0,1},{1,0},{2,3},{3,2},{4,5},{5,4},{6,7},{7,6},{8,9},{9,8},{10,11... | collective-permute-start | bytes 442376 | tf_op jit(solution)/shard_map/ppermute | solution.py:285
  15.5 2.7 %collective-permute-start.2 = (bf16[64,1152]{1,0:T(8,128)(2,1)S(1)}, bf16[64,1152]{1,0:T(8,128)(2,1)S(1)}, u32[]{:S(2)}, u32[]{:S(2)}) collective-permute-start(bf16[64,1152]{1,0:T(8,128)(2,1)S(1)} %shard_map.78), channel_id=1, source_target_pairs={{0,2},{2,0},{4,6},{6,4},{10,12},{12,10},{14,8},{8,14},{1,3},{3,1},... | collective-permute-start | bytes 442376 | tf_op jit(solution)/shard_map/ppermute | solution.py:104
  18.5 0.1 and_select_fusion
  18.6 1.5 %collective-permute-done.1 = bf16[64,1152]{1,0:T(8,128)(2,1)S(1)} collective-permute-done((bf16[64,1152]{1,0:T(8,128)(2,1)S(1)}, bf16[64,1152]{1,0:T(8,128)(2,1)S(1)}, u32[]{:S(2)}, u32[]{:S(2)}) %collective-permute-start.1) | collective-permute-done | bytes 147488 | tf_op jit(solution)/shard_map/ppermute | solution.py:285
  20.1 2.7 %collective-permute-start.4 = (bf16[64,1152]{1,0:T(8,128)(2,1)S(1)}, bf16[64,1152]{1,0:T(8,128)(2,1)S(1)}, u32[]{:S(2)}, u32[]{:S(2)}) collective-permute-start(bf16[64,1152]{1,0:T(8,128)(2,1)S(1)} %collective-permute-done.1), channel_id=1, source_target_pairs={{0,2},{2,0},{4,6},{6,4},{10,12},{12,10},{14,8},{8,14},{1,3},{3,1},... | collective-permute-start | bytes 442376 | tf_op jit(solution)/shard_map/ppermute | solution.py:104
  22.9 0.0 collective-permute-done.2
  22.9 3.6 %collective-permute-start.3 = (bf16[2,64,1152]{2,1,0:T(8,128)(2,1)S(1)}, bf16[2,64,1152]{2,1,0:T(8,128)(2,1)S(1)}, u32[]{:S(2)}, u32[]{:S(2)}) collective-permute-start(bf16[2,64,1152]{2,1,0:T(8,128)(2,1)S(1)} %pad_maximum_fusion.refs_0_), channel_id=1, source_target_pairs={{0,6},{2,4},{4,2},{6,0},{10,8},{12,14},{14,12},{8,10},{1,7},{3,5},... | collective-permute-start | bytes 884744 | tf_op jit(solution)/shard_map/ppermute | solution.py:104
  26.5 0.7 collective-permute-done.4
  27.2 0.0 copy-start.1
  27.2 0.0 copy-start.2
  27.2 4.8 %collective-permute-start.5 = (bf16[2,64,1152]{2,1,0:T(8,128)(2,1)S(1)}, bf16[2,64,1152]{2,1,0:T(8,128)(2,1)S(1)}, u32[]{:S(2)}, u32[]{:S(2)}) collective-permute-start(bf16[2,64,1152]{2,1,0:T(8,128)(2,1)S(1)} %pad_maximum_fusion.1.refs_2_), channel_id=1, source_target_pairs={{0,6},{2,4},{4,2},{6,0},{10,8},{12,14},{14,12},{8,10},{1,7},{3,5},... | collective-permute-start | bytes 884744 | tf_op jit(solution)/shard_map/ppermute | solution.py:104
  32.0 0.7 collective-permute-done.3.refs_1_
  32.7 4.4 %collective-permute-done.5.refs_3_ = bf16[2,64,1152]{2,1,0:T(8,128)(2,1)S(1)} collective-permute-done((bf16[2,64,1152]{2,1,0:T(8,128)(2,1)S(1)}, bf16[2,64,1152]{2,1,0:T(8,128)(2,1)S(1)}, u32[]{:S(2)}, u32[]{:S(2)}) %collective-permute-start.5) | collective-permute-done | bytes 294944 | tf_op jit(solution)/shard_map/ppermute | solution.py:104
  37.2 0.6 shard_map.79
  37.8 0.0 copy-done
  37.8 1.4 %shard_map.80 = (bf16[4,128,640]{2,1,0:T(8,128)(2,1)S(1)}, bf16[4,128,512]{2,1,0:T(8,128)(2,1)S(1)}) custom-call(s32[4]{0:T(128)S(1)} %get-tuple-element.26.blocks, bf16[512,1024]{1,0:T(8,128)(2,1)S(1)} %copy-done, bf16[512,1152]{1,0:T(8,128)(2,1)S(1)} %bitcast.25), custom_call_target="tpu_custom_call" | custom-call | flops 1 | bytes 1 | tf_op jit(solution)/shard_map/pallas_call | solution.py:147
  39.3 3.5 %collective-permute-start.9 = (bf16[4,128,640]{2,1,0:T(8,128)(2,1)S(1)}, bf16[4,128,640]{2,1,0:T(8,128)(2,1)S(1)}, u32[]{:S(2)}, u32[]{:S(2)}) collective-permute-start(bf16[4,128,640]{2,1,0:T(8,128)(2,1)S(1)} %get-tuple-element.37), channel_id=1, source_target_pairs={{0,64},{72,136},{64,0},{136,72},{128,192},{200,264},{192,128},{264... | collective-permute-start | bytes 1966088 | tf_op jit(solution)/shard_map/ppermute | solution.py:306
  42.8 0.0 copy-done.1
  42.8 2.5 %shard_map.81 = bf16[4,512,128]{2,1,0:T(8,128)(2,1)S(1)} custom-call(s32[4]{0:T(128)S(1)} %add_subtract_fusion.blocks, bf16[512,1152]{1,0:T(8,128)(2,1)S(1)} %bitcast.26, bf16[8,128,1024]{2,1,0:T(8,128)(2,1)S(1)} %bitcast.30, bf16[8,128,128]{2,1,0:T(8,128)(2,1)S(1)} %bitcast.32), custom_call_target="tpu_custom_call" | custom-call | flops 1 | bytes 1 | tf_op jit(solution)/shard_map/pallas_call | solution.py:258
  45.3 1.9 %collective-permute-start.6 = (bf16[4,512,128]{2,1,0:T(8,128)(2,1)S(1)}, bf16[4,512,128]{2,1,0:T(8,128)(2,1)S(1)}, u32[]{:S(2)}, u32[]{:S(2)}) collective-permute-start(bf16[4,512,128]{2,1,0:T(8,128)(2,1)S(1)} %shard_map.81), channel_id=1, source_target_pairs={{0,8},{8,0},{1,9},{9,1},{2,10},{10,2},{3,11},{11,3},{4,12},{12,4},... | collective-permute-start | bytes 1572872 | tf_op jit(solution)/shard_map/ppermute | solution.py:312
  47.2 2.4 %collective-permute-start.11 = (bf16[4,128,512]{2,1,0:T(8,128)(2,1)S(1)}, bf16[4,128,512]{2,1,0:T(8,128)(2,1)S(1)}, u32[]{:S(2)}, u32[]{:S(2)}) collective-permute-start(bf16[4,128,512]{2,1,0:T(8,128)(2,1)S(1)} %get-tuple-element.41), channel_id=1, source_target_pairs={{0,64},{72,136},{64,0},{136,72},{128,192},{200,264},{192,128},{264... | collective-permute-start | bytes 1572872 | tf_op jit(solution)/shard_map/ppermute | solution.py:306
  49.6 0.0 collective-permute-done.6.refs_0_
  49.6 2.5 %shard_map.82 = (bf16[2,512,128]{2,1,0:T(8,128)(2,1)S(1)}, bf16[2,512,128]{2,1,0:T(8,128)(2,1)S(1)}) custom-call(s32[4]{0:T(128)S(1)} %get-tuple-element.25.blocks, bf16[512,1152]{1,0:T(8,128)(2,1)S(1)} %bitcast.27, bf16[8,128,1024]{2,1,0:T(8,128)(2,1)S(1)} %bitcast.31, bf16[8,128,128]{2,1,0:T(8,128)(2,1)S(1)} %bitcast.33, ...), custom_call_target="tpu_custom_call" | custom-call | flops 1 | bytes 1 | tf_op jit(solution)/shard_map/pallas_call | solution.py:258
  52.1 0.0 collective-permute-done.9.got_ref
  52.1 1.2 %shard_map.84 = (bf16[2,128,640]{2,1,0:T(8,128)(2,1)S(1)}, bf16[2,128,640]{2,1,0:T(8,128)(2,1)S(1)}) custom-call(s32[4]{0:T(128)S(1)} %get-tuple-element.36.blocks, bf16[512,1024]{1,0:T(8,128)(2,1)S(1)} %copy-done, bf16[512,1152]{1,0:T(8,128)(2,1)S(1)} %bitcast.28, bf16[4,128,640]{2,1,0:T(8,128)(2,1)S(1)} %collective-permute-done.9.got_ref), custom_call_target="tpu_custom_call" | custom-call | flops 1 | bytes 1 | tf_op jit(solution)/shard_map/pallas_call | solution.py:167
  53.3 5.4 %collective-permute-start.10 = (bf16[2,128,640]{2,1,0:T(8,128)(2,1)S(1)}, bf16[2,128,640]{2,1,0:T(8,128)(2,1)S(1)}, u32[]{:S(2)}, u32[]{:S(2)}) collective-permute-start(bf16[2,128,640]{2,1,0:T(8,128)(2,1)S(1)} %get-tuple-element.40), channel_id=1, source_target_pairs={{0,448},{72,8},{64,128},{136,200},{128,64},{200,136},{192,256},{26... | collective-permute-start | bytes 983048 | tf_op jit(solution)/shard_map/ppermute | solution.py:306
  58.7 0.0 collective-permute-done.11.got_ref
  58.7 1.0 %shard_map.85 = (bf16[2,128,512]{2,1,0:T(8,128)(2,1)S(1)}, bf16[2,128,512]{2,1,0:T(8,128)(2,1)S(1)}) custom-call(s32[4]{0:T(128)S(1)} %get-tuple-element.36.blocks, bf16[512,1024]{1,0:T(8,128)(2,1)S(1)} %copy-done, bf16[512,1152]{1,0:T(8,128)(2,1)S(1)} %bitcast.29, bf16[4,128,512]{2,1,0:T(8,128)(2,1)S(1)} %collective-permute-done.11.got_ref), custom_call_target="tpu_custom_call" | custom-call | flops 1 | bytes 1 | tf_op jit(solution)/shard_map/pallas_call | solution.py:167
  59.7 4.7 %collective-permute-start.12 = (bf16[2,128,512]{2,1,0:T(8,128)(2,1)S(1)}, bf16[2,128,512]{2,1,0:T(8,128)(2,1)S(1)}, u32[]{:S(2)}, u32[]{:S(2)}) collective-permute-start(bf16[2,128,512]{2,1,0:T(8,128)(2,1)S(1)} %get-tuple-element.44), channel_id=1, source_target_pairs={{0,448},{72,8},{64,128},{136,200},{128,64},{200,136},{192,256},{26... | collective-permute-start | bytes 786440 | tf_op jit(solution)/shard_map/ppermute | solution.py:306
  64.5 7.2 %collective-permute-start.7 = (bf16[2,512,128]{2,1,0:T(8,128)(2,1)S(1)}, bf16[2,512,128]{2,1,0:T(8,128)(2,1)S(1)}, u32[]{:S(2)}, u32[]{:S(2)}) collective-permute-start(bf16[2,512,128]{2,1,0:T(8,128)(2,1)S(1)} %get-tuple-element.33), channel_id=1, source_target_pairs={{0,16},{16,0},{32,48},{48,32},{1,17},{17,1},{33,49},{49,33},{2,18}... | collective-permute-start | bytes 786440 | tf_op jit(solution)/shard_map/ppermute | solution.py:314
  71.7 0.0 collective-permute-done.12.refs_3_
  71.7 0.0 collective-permute-done.10.refs_1_
  71.7 0.1 shard_map.86
  71.9 4.5 %collective-permute-start.13 = (bf16[128,1152]{1,0:T(8,128)(2,1)S(1)}, bf16[128,1152]{1,0:T(8,128)(2,1)S(1)}, u32[]{:S(2)}, u32[]{:S(2)}) collective-permute-start(bf16[128,1152]{1,0:T(8,128)(2,1)S(1)} %get-tuple-element.46), channel_id=1, source_target_pairs={{0,192},{72,264},{64,384},{136,456},{128,320},{200,392},{192,0},{2... | collective-permute-start | bytes 884744 | tf_op jit(solution)/shard_map/ppermute | solution.py:306
  76.4 0.0 collective-permute-done.7.refs_1_
  76.4 0.1 shard_map.83
  76.5 5.6 %collective-permute-start.8 = (bf16[512,128]{1,0:T(8,128)(2,1)S(1)}, bf16[512,128]{1,0:T(8,128)(2,1)S(1)}, u32[]{:S(2)}, u32[]{:S(2)}) collective-permute-start(bf16[512,128]{1,0:T(8,128)(2,1)S(1)} %get-tuple-element.35), channel_id=1, source_target_pairs={{0,32},{16,48},{32,0},{48,16},{1,33},{17,49},{33,1},{49,17},{2,34}... | collective-permute-start | bytes 393224 | tf_op jit(solution)/shard_map/ppermute | solution.py:328
  82.1 5.3 %collective-permute-done.8.input_got = bf16[512,128]{1,0:T(8,128)(2,1)S(1)} collective-permute-done((bf16[512,128]{1,0:T(8,128)(2,1)S(1)}, bf16[512,128]{1,0:T(8,128)(2,1)S(1)}, u32[]{:S(2)}, u32[]{:S(2)}) %collective-permute-start.8) | collective-permute-done | bytes 131104 | tf_op jit(solution)/shard_map/ppermute | solution.py:328
  87.4 0.1 collective-permute-done.13.got
  87.5 0.9 %shard_map.87 = (bf16[512,128]{1,0:T(8,128)(2,1)}, f32[128,1024]{1,0:T(8,128)}, f32[128,128]{1,0:T(8,128)}) custom-call(bf16[512,128]{1,0:T(8,128)(2,1)S(1)} %get-tuple-element.34.input_kept, bf16[512,128]{1,0:T(8,128)(2,1)S(1)} %collective-permute-done.8.input_got, bf16[128,1152]{1,0:T(8,128)(2,1)S(1)} %get-tuple-element.45.kept, ...), custom_call_target="tpu_custom_call" | custom-call | flops 1 | bytes 1 | tf_op jit(solution)/shard_map/pallas_call | solution.py:217
  (9 shorter events, 0.1 us)
Async XLA Ops:
  0.6 3.3 %collective-permute-start = (bf16[64,256]{1,0:T(8,128)(2,1)}, bf16[64,256]{1,0:T(8,128)(2,1)S(1)}, u32[]{:S(2)}, u32[]{:S(2)}) collective-permute-start(bf16[64,256]{1,0:T(8,128)(2,1)} %share_hbm.1), channel_id=1, source_target_pairs={{0,8},{8,0},{1,9},{9,1},{2,10},{10,2},{3,11},{11,3},{4,12},{12,4},... | collective-permute-start | bytes 98312 | tf_op jit(solution)/shard_map/ppermute | solution.py:283
  2.7 0.9 %copy-start.4 = (bf16[64,1024]{1,0:T(8,128)(2,1)S(1)}, bf16[64,1024]{1,0:T(8,128)(2,1)}, u32[]{:S(2)}) copy-start(bf16[64,1024]{1,0:T(8,128)(2,1)} %rows_ref.1) | copy-start | bytes 393220
  3.6 0.8 copy-start.3
  4.5 33.3 %copy-start = (bf16[512,1024]{1,0:T(8,128)(2,1)S(1)}, bf16[512,1024]{1,0:T(8,128)(2,1)}, u32[]{:S(2)}) copy-start(bf16[512,1024]{1,0:T(8,128)(2,1)} %x_ref.5) | copy-start | bytes 3145732
  4.5 15.6 %collective-permute-start.1 = (bf16[64,1152]{1,0:T(8,128)(2,1)S(1)}, bf16[64,1152]{1,0:T(8,128)(2,1)S(1)}, u32[]{:S(2)}, u32[]{:S(2)}) collective-permute-start(bf16[64,1152]{1,0:T(8,128)(2,1)S(1)} %shard_map.77.rows_ref), channel_id=1, source_target_pairs={{0,1},{1,0},{2,3},{3,2},{4,5},{5,4},{6,7},{7,6},{8,9},{9,8},{10,11... | collective-permute-start | bytes 442376 | tf_op jit(solution)/shard_map/ppermute | solution.py:285
  15.5 7.3 %collective-permute-start.2 = (bf16[64,1152]{1,0:T(8,128)(2,1)S(1)}, bf16[64,1152]{1,0:T(8,128)(2,1)S(1)}, u32[]{:S(2)}, u32[]{:S(2)}) collective-permute-start(bf16[64,1152]{1,0:T(8,128)(2,1)S(1)} %shard_map.78), channel_id=1, source_target_pairs={{0,2},{2,0},{4,6},{6,4},{10,12},{12,10},{14,8},{8,14},{1,3},{3,1},... | collective-permute-start | bytes 442376 | tf_op jit(solution)/shard_map/ppermute | solution.py:104
  20.1 7.0 %collective-permute-start.4 = (bf16[64,1152]{1,0:T(8,128)(2,1)S(1)}, bf16[64,1152]{1,0:T(8,128)(2,1)S(1)}, u32[]{:S(2)}, u32[]{:S(2)}) collective-permute-start(bf16[64,1152]{1,0:T(8,128)(2,1)S(1)} %collective-permute-done.1), channel_id=1, source_target_pairs={{0,2},{2,0},{4,6},{6,4},{10,12},{12,10},{14,8},{8,14},{1,3},{3,1},... | collective-permute-start | bytes 442376 | tf_op jit(solution)/shard_map/ppermute | solution.py:104
  22.9 9.8 %collective-permute-start.3 = (bf16[2,64,1152]{2,1,0:T(8,128)(2,1)S(1)}, bf16[2,64,1152]{2,1,0:T(8,128)(2,1)S(1)}, u32[]{:S(2)}, u32[]{:S(2)}) collective-permute-start(bf16[2,64,1152]{2,1,0:T(8,128)(2,1)S(1)} %pad_maximum_fusion.refs_0_), channel_id=1, source_target_pairs={{0,6},{2,4},{4,2},{6,0},{10,8},{12,14},{14,12},{8,10},{1,7},{3,5},... | collective-permute-start | bytes 884744 | tf_op jit(solution)/shard_map/ppermute | solution.py:104
  27.2 15.6 %copy-start.1 = (bf16[1024,1024]{1,0:T(8,128)(2,1)S(1)}, bf16[1024,1024]{1,0:T(8,128)(2,1)}, u32[]{:S(2)}) copy-start(bf16[1024,1024]{1,0:T(8,128)(2,1)} %param.8) | copy-start | bytes 6291460
  27.2 15.6 %copy-start.2 = (bf16[1024,128]{1,0:T(8,128)(2,1)S(1)}, bf16[1024,128]{1,0:T(8,128)(2,1)}, u32[]{:S(2)}) copy-start(bf16[1024,128]{1,0:T(8,128)(2,1)} %param.9) | copy-start | bytes 786436
  27.2 10.0 %collective-permute-start.5 = (bf16[2,64,1152]{2,1,0:T(8,128)(2,1)S(1)}, bf16[2,64,1152]{2,1,0:T(8,128)(2,1)S(1)}, u32[]{:S(2)}, u32[]{:S(2)}) collective-permute-start(bf16[2,64,1152]{2,1,0:T(8,128)(2,1)S(1)} %pad_maximum_fusion.1.refs_2_), channel_id=1, source_target_pairs={{0,6},{2,4},{4,2},{6,0},{10,8},{12,14},{14,12},{8,10},{1,7},{3,5},... | collective-permute-start | bytes 884744 | tf_op jit(solution)/shard_map/ppermute | solution.py:104
  39.3 12.8 %collective-permute-start.9 = (bf16[4,128,640]{2,1,0:T(8,128)(2,1)S(1)}, bf16[4,128,640]{2,1,0:T(8,128)(2,1)S(1)}, u32[]{:S(2)}, u32[]{:S(2)}) collective-permute-start(bf16[4,128,640]{2,1,0:T(8,128)(2,1)S(1)} %get-tuple-element.37), channel_id=1, source_target_pairs={{0,64},{72,136},{64,0},{136,72},{128,192},{200,264},{192,128},{264... | collective-permute-start | bytes 1966088 | tf_op jit(solution)/shard_map/ppermute | solution.py:306
  45.3 4.3 %collective-permute-start.6 = (bf16[4,512,128]{2,1,0:T(8,128)(2,1)S(1)}, bf16[4,512,128]{2,1,0:T(8,128)(2,1)S(1)}, u32[]{:S(2)}, u32[]{:S(2)}) collective-permute-start(bf16[4,512,128]{2,1,0:T(8,128)(2,1)S(1)} %shard_map.81), channel_id=1, source_target_pairs={{0,8},{8,0},{1,9},{9,1},{2,10},{10,2},{3,11},{11,3},{4,12},{12,4},... | collective-permute-start | bytes 1572872 | tf_op jit(solution)/shard_map/ppermute | solution.py:312
  47.2 11.5 %collective-permute-start.11 = (bf16[4,128,512]{2,1,0:T(8,128)(2,1)S(1)}, bf16[4,128,512]{2,1,0:T(8,128)(2,1)S(1)}, u32[]{:S(2)}, u32[]{:S(2)}) collective-permute-start(bf16[4,128,512]{2,1,0:T(8,128)(2,1)S(1)} %get-tuple-element.41), channel_id=1, source_target_pairs={{0,64},{72,136},{64,0},{136,72},{128,192},{200,264},{192,128},{264... | collective-permute-start | bytes 1572872 | tf_op jit(solution)/shard_map/ppermute | solution.py:306
  53.3 18.4 %collective-permute-start.10 = (bf16[2,128,640]{2,1,0:T(8,128)(2,1)S(1)}, bf16[2,128,640]{2,1,0:T(8,128)(2,1)S(1)}, u32[]{:S(2)}, u32[]{:S(2)}) collective-permute-start(bf16[2,128,640]{2,1,0:T(8,128)(2,1)S(1)} %get-tuple-element.40), channel_id=1, source_target_pairs={{0,448},{72,8},{64,128},{136,200},{128,64},{200,136},{192,256},{26... | collective-permute-start | bytes 983048 | tf_op jit(solution)/shard_map/ppermute | solution.py:306
  59.7 12.0 %collective-permute-start.12 = (bf16[2,128,512]{2,1,0:T(8,128)(2,1)S(1)}, bf16[2,128,512]{2,1,0:T(8,128)(2,1)S(1)}, u32[]{:S(2)}, u32[]{:S(2)}) collective-permute-start(bf16[2,128,512]{2,1,0:T(8,128)(2,1)S(1)} %get-tuple-element.44), channel_id=1, source_target_pairs={{0,448},{72,8},{64,128},{136,200},{128,64},{200,136},{192,256},{26... | collective-permute-start | bytes 786440 | tf_op jit(solution)/shard_map/ppermute | solution.py:306
  64.5 11.9 %collective-permute-start.7 = (bf16[2,512,128]{2,1,0:T(8,128)(2,1)S(1)}, bf16[2,512,128]{2,1,0:T(8,128)(2,1)S(1)}, u32[]{:S(2)}, u32[]{:S(2)}) collective-permute-start(bf16[2,512,128]{2,1,0:T(8,128)(2,1)S(1)} %get-tuple-element.33), channel_id=1, source_target_pairs={{0,16},{16,0},{32,48},{48,32},{1,17},{17,1},{33,49},{49,33},{2,18}... | collective-permute-start | bytes 786440 | tf_op jit(solution)/shard_map/ppermute | solution.py:314
  71.9 15.7 %collective-permute-start.13 = (bf16[128,1152]{1,0:T(8,128)(2,1)S(1)}, bf16[128,1152]{1,0:T(8,128)(2,1)S(1)}, u32[]{:S(2)}, u32[]{:S(2)}) collective-permute-start(bf16[128,1152]{1,0:T(8,128)(2,1)S(1)} %get-tuple-element.46), channel_id=1, source_target_pairs={{0,192},{72,264},{64,384},{136,456},{128,320},{200,392},{192,0},{2... | collective-permute-start | bytes 884744 | tf_op jit(solution)/shard_map/ppermute | solution.py:306
  76.5 10.9 %collective-permute-start.8 = (bf16[512,128]{1,0:T(8,128)(2,1)S(1)}, bf16[512,128]{1,0:T(8,128)(2,1)S(1)}, u32[]{:S(2)}, u32[]{:S(2)}) collective-permute-start(bf16[512,128]{1,0:T(8,128)(2,1)S(1)} %get-tuple-element.35), channel_id=1, source_target_pairs={{0,32},{16,48},{32,0},{48,16},{1,33},{17,49},{33,1},{49,17},{2,34}... | collective-permute-start | bytes 393224 | tf_op jit(solution)/shard_map/ppermute | solution.py:328

commit v8 on v7

--- a/solution.py
+++ b/solution.py
@@ -46,7 +46,7 @@
 FIRST = swapped(lambda v: v ^ 1)
 SECOND = swapped(lambda v: second(v, select))
 THIRD = swapped(lambda v: third(v, select))
-PARTS = (640, 512)
+PARTS = (768, 384)
 
 
 VMEM = pl.BlockSpec(memory_space=pltpu.VMEM)
@@ -225,45 +225,47 @@
     )(*arrays)
 
 
-def input_body(blocks, g_ref, wq_ref, wkv_ref, *refs):
-    n_q = wq_ref.shape[-1]
-    term = dot(g_ref[:, :n_q], wq_ref[0], (1, 1))
-    term = term + dot(g_ref[:, n_q:], wkv_ref[0], (1, 1))
+def input_body(blocks, g_ref, wq_one, wq_two, wkv_one, wkv_two, *refs):
+    n_q = wq_one.shape[-1]
+    wq = jnp.concatenate([wq_one[0], wq_two[0]])
+    wkv = jnp.concatenate([wkv_one[0], wkv_two[0]])
+    term = dot(g_ref[:, :n_q], wq, (1, 1)) + dot(g_ref[:, n_q:], wkv, (1, 1))
+    pair = [term[:, :128], term[:, 128:]]
     if len(refs) == 1:
-        refs[0][0] = term.astype(jnp.bfloat16)
+        for i in range(2):
+            refs[0][i] = pair[i].astype(jnp.bfloat16)
         return
     got_ref, *outs = refs
-    term = (term + got_ref[0].astype(jnp.float32)).astype(jnp.bfloat16)
     for half, out in enumerate(outs):
 
-        @pl.when(pl.program_id(0) // 2 == half)
+        @pl.when(pl.program_id(0) == half)
         def _():
-            out[0] = term
+            for i in range(2):
+                out[i] = (pair[i] + got_ref[i].astype(jnp.float32)).astype(jnp.bfloat16)
 
 
 def input_terms(blocks, g, wq, wkv, *got):
     n_q, n_kv = wq.shape[1], wkv.shape[1]
     rows = g.shape[0]
     n = blocks.shape[0]
-    pick = lambda r, blocks: (blocks[r], 0, 0)
+    one = lambda r, blocks: (blocks[2 * r], 0, 0)
+    two = lambda r, blocks: (blocks[2 * r + 1], 0, 0)
     mine = lambda r, blocks: (r, 0, 0)
-    block = (1, rows, 128)
-    if got:
-        places = [
-            lambda r, blocks: (jnp.minimum(r, 1), 0, 0),
-            lambda r, blocks: (jnp.maximum(r - 2, 0), 0, 0),
-        ]
-    else:
-        places = [mine]
+    fixed = lambda r, blocks: (0, 0, 0)
+    block = (2, rows, 128)
+    places = [fixed, fixed] if got else [mine]
+    wq, wkv = wq.reshape(-1, 128, n_q), wkv.reshape(-1, 128, n_kv)
     return pl.pallas_call(
         input_body,
         grid_spec=pltpu.PrefetchScalarGridSpec(
             num_scalar_prefetch=1,
-            grid=(n,),
+            grid=(n // 2,),
             in_specs=[
                 pl.BlockSpec(g.shape, lambda r, blocks: (0, 0)),
-                pl.BlockSpec((1, 128, n_q), pick),
-                pl.BlockSpec((1, 128, n_kv), pick),
+                pl.BlockSpec((1, 128, n_q), one),
+                pl.BlockSpec((1, 128, n_q), two),
+                pl.BlockSpec((1, 128, n_kv), one),
+                pl.BlockSpec((1, 128, n_kv), two),
             ]
             + [pl.BlockSpec(block, mine)] * len(got),
             out_specs=[pl.BlockSpec(block, place) for place in places],
@@ -271,7 +273,7 @@
         out_shape=[jax.ShapeDtypeStruct((n // len(places), rows, 128), jnp.bfloat16) for _ in places],
         compiler_params=PARAMS,
         cost_estimate=COST,
-    )(blocks, g, wq.reshape(-1, 128, n_q), wkv.reshape(-1, 128, n_kv), *got)
+    )(blocks, g, wq, wq, wkv, wkv, *got)
 
 
 def local(inputs, q_grad, key_value_share_gradient, q_weight, key_value_weight):

time: 89.5 us -> 89 us (level)
  waiting for transfers between devices: 13 us -> 14.8 us
  Pallas kernels: 10.5 us -> 8.83 us
    ppermute x5, waiting for transfers between devices: 0.16 us -> 4.24 us  [along_y(): return lax.ppermute(terms, (*TOK, 'core'), pairs)]
    ppermute x1, waiting for transfers between devices: 5.28 us -> 2.93 us  [local(): input_got = lax.ppermute(give, 'zlo', [(i, i ^ 2) for i in range(4)])]
    pallas_call x2, Pallas kernels: 5.01 us -> 3.31 us  [input_terms(): pl.pallas_call(input_body, grid_spec=pltpu.PrefetchScalarGridSpec(num_sca...]
  transfers between devices with their start and end apart: 14 -> 14, of which waited for: 7 -> 8; matrix products, arithmetic and copies ran while one was open for 0% -> 0% of each run, Pallas kernels for 8% -> 7%
where the time goes in v8:
time: 89 us; the launch traced here: 87.7 us
  starting transfers between devices  61.3 us (69%)
  waiting for transfers between devices  14.8 us (17%)
  Pallas kernels  8.83 us (10%)
  local copies, waits for them, and re-layouts  1.41 us (2%)
  between operations  1.22 us (1%)
    ppermute x5, starting transfers between devices, along_y(): return lax.ppermute(terms, (*TOK, 'core'), pairs)  20.2 us
    ppermute x4, starting transfers between devices, x_swap(): return lax.ppermute(rows, ('core', 'x'), pairs)  13.8 us
    ppermute x1, starting transfers between devices, local(): far = lax.ppermute(mine, 'zhi', SWAP)  11 us
    ppermute x1, starting transfers between devices, local(): input_got = lax.ppermute(give, 'zlo', [(i, i ^ 1) for i in range(4)])  7.33 us
    ppermute x4, waiting for transfers between devices, x_swap(): return lax.ppermute(rows, ('core', 'x'), pairs)  5.83 us
    ppermute x1, starting transfers between devices, local(): input_got = lax.ppermute(give, 'zlo', [(i, i ^ 2) for i in range(4)])  5.05 us
    ppermute x5, waiting for transfers between devices, along_y(): return lax.ppermute(terms, (*TOK, 'core'), pairs)  4.24 us
    pallas_call x2, Pallas kernels, input_terms(): pl.pallas_call(input_body, grid_spec=pltpu.PrefetchScalarGridSpec(num_sca...  3.31 us
  transfers between devices with their start and end apart: 14, of which 8 were waited for; matrix products, arithmetic and copies ran while one was open for 0% of the time, Pallas kernels for 7%

profile of v8, /device:TPU:6, one launch (start us, length us, event | category | flops | bytes accessed | tf_op | source)
XLA Modules:
  0.0 87.7 jit_solution(2896978914011999676)
XLA Ops:
  0.6 1.9 %collective-permute-start = (bf16[64,256]{1,0:T(8,128)(2,1)}, bf16[64,256]{1,0:T(8,128)(2,1)S(1)}, u32[]{:S(2)}, u32[]{:S(2)}) collective-permute-start(bf16[64,256]{1,0:T(8,128)(2,1)} %share_hbm.1), channel_id=1, source_target_pairs={{0,8},{8,0},{1,9},{9,1},{2,10},{10,2},{3,11},{11,3},{4,12},{12,4},... | collective-permute-start | bytes 98312 | tf_op jit(solution)/shard_map/ppermute | solution.py:285
  2.6 0.1 stack.86
  2.7 0.9 %copy-done.4 = bf16[64,1024]{1,0:T(8,128)(2,1)S(1)} copy-done((bf16[64,1024]{1,0:T(8,128)(2,1)S(1)}, bf16[64,1024]{1,0:T(8,128)(2,1)}, u32[]{:S(2)}) %copy-start.4) | copy-done | bytes 131096
  3.6 0.1 broadcast_add_fusion
  3.7 0.3 collective-permute-done.more_ref
  3.9 0.4 copy-done.3
  4.4 0.1 shard_map.77.rows_ref
  4.5 0.0 copy-start.1
  4.5 11.0 %collective-permute-start.1 = (bf16[64,1152]{1,0:T(8,128)(2,1)S(1)}, bf16[64,1152]{1,0:T(8,128)(2,1)S(1)}, u32[]{:S(2)}, u32[]{:S(2)}) collective-permute-start(bf16[64,1152]{1,0:T(8,128)(2,1)S(1)} %shard_map.77.rows_ref), channel_id=1, source_target_pairs={{0,1},{1,0},{2,3},{3,2},{4,5},{5,4},{6,7},{7,6},{8,9},{9,8},{10,11... | collective-permute-start | bytes 442376 | tf_op jit(solution)/shard_map/ppermute | solution.py:287
  15.5 2.7 %collective-permute-start.2 = (bf16[64,1152]{1,0:T(8,128)(2,1)S(1)}, bf16[64,1152]{1,0:T(8,128)(2,1)S(1)}, u32[]{:S(2)}, u32[]{:S(2)}) collective-permute-start(bf16[64,1152]{1,0:T(8,128)(2,1)S(1)} %shard_map.78), channel_id=1, source_target_pairs={{0,2},{2,0},{4,6},{6,4},{10,12},{12,10},{14,8},{8,14},{1,3},{3,1},... | collective-permute-start | bytes 442376 | tf_op jit(solution)/shard_map/ppermute | solution.py:104
  18.5 0.1 and_select_fusion
  18.6 1.5 %collective-permute-done.1 = bf16[64,1152]{1,0:T(8,128)(2,1)S(1)} collective-permute-done((bf16[64,1152]{1,0:T(8,128)(2,1)S(1)}, bf16[64,1152]{1,0:T(8,128)(2,1)S(1)}, u32[]{:S(2)}, u32[]{:S(2)}) %collective-permute-start.1) | collective-permute-done | bytes 147488 | tf_op jit(solution)/shard_map/ppermute | solution.py:287
  20.1 2.7 %collective-permute-start.4 = (bf16[64,1152]{1,0:T(8,128)(2,1)S(1)}, bf16[64,1152]{1,0:T(8,128)(2,1)S(1)}, u32[]{:S(2)}, u32[]{:S(2)}) collective-permute-start(bf16[64,1152]{1,0:T(8,128)(2,1)S(1)} %collective-permute-done.1), channel_id=1, source_target_pairs={{0,2},{2,0},{4,6},{6,4},{10,12},{12,10},{14,8},{8,14},{1,3},{3,1},... | collective-permute-start | bytes 442376 | tf_op jit(solution)/shard_map/ppermute | solution.py:104
  22.9 0.0 collective-permute-done.2
  22.9 3.6 %collective-permute-start.3 = (bf16[2,64,1152]{2,1,0:T(8,128)(2,1)S(1)}, bf16[2,64,1152]{2,1,0:T(8,128)(2,1)S(1)}, u32[]{:S(2)}, u32[]{:S(2)}) collective-permute-start(bf16[2,64,1152]{2,1,0:T(8,128)(2,1)S(1)} %pad_maximum_fusion.refs_0_), channel_id=1, source_target_pairs={{0,6},{2,4},{4,2},{6,0},{10,8},{12,14},{14,12},{8,10},{1,7},{3,5},... | collective-permute-start | bytes 884744 | tf_op jit(solution)/shard_map/ppermute | solution.py:104
  26.5 0.7 collective-permute-done.4
  27.2 0.0 copy-start
  27.2 0.0 copy-start.2
  27.2 4.8 %collective-permute-start.5 = (bf16[2,64,1152]{2,1,0:T(8,128)(2,1)S(1)}, bf16[2,64,1152]{2,1,0:T(8,128)(2,1)S(1)}, u32[]{:S(2)}, u32[]{:S(2)}) collective-permute-start(bf16[2,64,1152]{2,1,0:T(8,128)(2,1)S(1)} %pad_maximum_fusion.1.refs_2_), channel_id=1, source_target_pairs={{0,6},{2,4},{4,2},{6,0},{10,8},{12,14},{14,12},{8,10},{1,7},{3,5},... | collective-permute-start | bytes 884744 | tf_op jit(solution)/shard_map/ppermute | solution.py:104
  32.0 0.7 collective-permute-done.3.refs_1_
  32.7 4.4 %collective-permute-done.5.refs_3_ = bf16[2,64,1152]{2,1,0:T(8,128)(2,1)S(1)} collective-permute-done((bf16[2,64,1152]{2,1,0:T(8,128)(2,1)S(1)}, bf16[2,64,1152]{2,1,0:T(8,128)(2,1)S(1)}, u32[]{:S(2)}, u32[]{:S(2)}) %collective-permute-start.5) | collective-permute-done | bytes 294944 | tf_op jit(solution)/shard_map/ppermute | solution.py:104
  37.2 0.6 shard_map.79
  37.8 0.0 copy-done.1
  37.8 1.4 %shard_map.80 = (bf16[4,128,768]{2,1,0:T(8,128)(2,1)S(1)}, bf16[4,128,384]{2,1,0:T(8,128)(2,1)S(1)}) custom-call(s32[4]{0:T(128)S(1)} %get-tuple-element.26.blocks, bf16[512,1024]{1,0:T(8,128)(2,1)S(1)} %copy-done.1, bf16[512,1152]{1,0:T(8,128)(2,1)S(1)} %bitcast.25), custom_call_target="tpu_custom_call" | custom-call | flops 1 | bytes 1 | tf_op jit(solution)/shard_map/pallas_call | solution.py:147
  39.3 3.5 %collective-permute-start.9 = (bf16[4,128,768]{2,1,0:T(8,128)(2,1)S(1)}, bf16[4,128,768]{2,1,0:T(8,128)(2,1)S(1)}, u32[]{:S(2)}, u32[]{:S(2)}) collective-permute-start(bf16[4,128,768]{2,1,0:T(8,128)(2,1)S(1)} %get-tuple-element.37), channel_id=1, source_target_pairs={{0,64},{72,136},{64,0},{136,72},{128,192},{200,264},{192,128},{264... | collective-permute-start | bytes 2359304 | tf_op jit(solution)/shard_map/ppermute | solution.py:308
  42.8 0.0 copy-done
  42.8 1.6 %shard_map.81 = bf16[4,512,128]{2,1,0:T(8,128)(2,1)S(1)} custom-call(s32[4]{0:T(128)S(1)} %add_subtract_fusion.blocks, bf16[512,1152]{1,0:T(8,128)(2,1)S(1)} %bitcast.26, bf16[8,128,1024]{2,1,0:T(8,128)(2,1)S(1)} %bitcast.30, bf16[8,128,1024]{2,1,0:T(8,128)(2,1)S(1)} %bitcast.31, bf16[8,128,128]{2,1,0:T(8,128)(2,1)S(1)} %bitcast.34, ...), custom_call_target="tpu_custom_call" | custom-call | flops 1 | bytes 1 | tf_op jit(solution)/shard_map/pallas_call | solution.py:258
  44.4 1.9 %collective-permute-start.6 = (bf16[4,512,128]{2,1,0:T(8,128)(2,1)S(1)}, bf16[4,512,128]{2,1,0:T(8,128)(2,1)S(1)}, u32[]{:S(2)}, u32[]{:S(2)}) collective-permute-start(bf16[4,512,128]{2,1,0:T(8,128)(2,1)S(1)} %shard_map.81), channel_id=1, source_target_pairs={{0,8},{8,0},{1,9},{9,1},{2,10},{10,2},{3,11},{11,3},{4,12},{12,4},... | collective-permute-start | bytes 1572872 | tf_op jit(solution)/shard_map/ppermute | solution.py:314
  46.3 2.3 %collective-permute-start.11 = (bf16[4,128,384]{2,1,0:T(8,128)(2,1)S(1)}, bf16[4,128,384]{2,1,0:T(8,128)(2,1)S(1)}, u32[]{:S(2)}, u32[]{:S(2)}) collective-permute-start(bf16[4,128,384]{2,1,0:T(8,128)(2,1)S(1)} %get-tuple-element.41), channel_id=1, source_target_pairs={{0,64},{72,136},{64,0},{136,72},{128,192},{200,264},{192,128},{264... | collective-permute-start | bytes 1179656 | tf_op jit(solution)/shard_map/ppermute | solution.py:308
  48.7 0.0 collective-permute-done.6.refs_0_
  48.7 1.7 %shard_map.82 = (bf16[2,512,128]{2,1,0:T(8,128)(2,1)S(1)}, bf16[2,512,128]{2,1,0:T(8,128)(2,1)S(1)}) custom-call(s32[4]{0:T(128)S(1)} %get-tuple-element.25.blocks, bf16[512,1152]{1,0:T(8,128)(2,1)S(1)} %bitcast.27, bf16[8,128,1024]{2,1,0:T(8,128)(2,1)S(1)} %bitcast.32, bf16[8,128,1024]{2,1,0:T(8,128)(2,1)S(1)} %bitcast.33, ...), custom_call_target="tpu_custom_call" | custom-call | flops 1 | bytes 1 | tf_op jit(solution)/shard_map/pallas_call | solution.py:258
  50.4 2.7 %collective-permute-done.9.got_ref = bf16[4,128,768]{2,1,0:T(8,128)(2,1)S(1)} collective-permute-done((bf16[4,128,768]{2,1,0:T(8,128)(2,1)S(1)}, bf16[4,128,768]{2,1,0:T(8,128)(2,1)S(1)}, u32[]{:S(2)}, u32[]{:S(2)}) %collective-permute-start.9) | collective-permute-done | bytes 786464 | tf_op jit(solution)/shard_map/ppermute | solution.py:308
  53.2 1.2 %shard_map.84 = (bf16[2,128,768]{2,1,0:T(8,128)(2,1)S(1)}, bf16[2,128,768]{2,1,0:T(8,128)(2,1)S(1)}) custom-call(s32[4]{0:T(128)S(1)} %get-tuple-element.36.blocks, bf16[512,1024]{1,0:T(8,128)(2,1)S(1)} %copy-done.1, bf16[512,1152]{1,0:T(8,128)(2,1)S(1)} %bitcast.28, bf16[4,128,768]{2,1,0:T(8,128)(2,1)S(1)} %collective-permute-done.9.got_ref), custom_call_target="tpu_custom_call" | custom-call | flops 1 | bytes 1 | tf_op jit(solution)/shard_map/pallas_call | solution.py:167
  54.3 5.4 %collective-permute-start.10 = (bf16[2,128,768]{2,1,0:T(8,128)(2,1)S(1)}, bf16[2,128,768]{2,1,0:T(8,128)(2,1)S(1)}, u32[]{:S(2)}, u32[]{:S(2)}) collective-permute-start(bf16[2,128,768]{2,1,0:T(8,128)(2,1)S(1)} %get-tuple-element.40), channel_id=1, source_target_pairs={{0,448},{72,8},{64,128},{136,200},{128,64},{200,136},{192,256},{26... | collective-permute-start | bytes 1179656 | tf_op jit(solution)/shard_map/ppermute | solution.py:308
  59.7 0.0 collective-permute-done.11.got_ref
  59.7 1.1 %shard_map.85 = (bf16[2,128,384]{2,1,0:T(8,128)(2,1)S(1)}, bf16[2,128,384]{2,1,0:T(8,128)(2,1)S(1)}) custom-call(s32[4]{0:T(128)S(1)} %get-tuple-element.36.blocks, bf16[512,1024]{1,0:T(8,128)(2,1)S(1)} %copy-done.1, bf16[512,1152]{1,0:T(8,128)(2,1)S(1)} %bitcast.29, bf16[4,128,384]{2,1,0:T(8,128)(2,1)S(1)} %collective-permute-done.11.got_ref), custom_call_target="tpu_custom_call" | custom-call | flops 1 | bytes 1 | tf_op jit(solution)/shard_map/pallas_call | solution.py:167
  60.8 3.6 %collective-permute-start.12 = (bf16[2,128,384]{2,1,0:T(8,128)(2,1)S(1)}, bf16[2,128,384]{2,1,0:T(8,128)(2,1)S(1)}, u32[]{:S(2)}, u32[]{:S(2)}) collective-permute-start(bf16[2,128,384]{2,1,0:T(8,128)(2,1)S(1)} %get-tuple-element.44), channel_id=1, source_target_pairs={{0,448},{72,8},{64,128},{136,200},{128,64},{200,136},{192,256},{26... | collective-permute-start | bytes 589832 | tf_op jit(solution)/shard_map/ppermute | solution.py:308
  64.4 7.3 %collective-permute-start.7 = (bf16[2,512,128]{2,1,0:T(8,128)(2,1)S(1)}, bf16[2,512,128]{2,1,0:T(8,128)(2,1)S(1)}, u32[]{:S(2)}, u32[]{:S(2)}) collective-permute-start(bf16[2,512,128]{2,1,0:T(8,128)(2,1)S(1)} %get-tuple-element.33), channel_id=1, source_target_pairs={{0,16},{16,0},{32,48},{48,32},{1,17},{17,1},{33,49},{49,33},{2,18}... | collective-permute-start | bytes 786440 | tf_op jit(solution)/shard_map/ppermute | solution.py:316
  71.7 0.0 collective-permute-done.12.refs_3_
  71.7 0.0 collective-permute-done.10.refs_1_
  71.7 0.1 shard_map.86
  71.9 5.4 %collective-permute-start.13 = (bf16[128,1152]{1,0:T(8,128)(2,1)S(1)}, bf16[128,1152]{1,0:T(8,128)(2,1)S(1)}, u32[]{:S(2)}, u32[]{:S(2)}) collective-permute-start(bf16[128,1152]{1,0:T(8,128)(2,1)S(1)} %get-tuple-element.46), channel_id=1, source_target_pairs={{0,192},{72,264},{64,384},{136,456},{128,320},{200,392},{192,0},{2... | collective-permute-start | bytes 884744 | tf_op jit(solution)/shard_map/ppermute | solution.py:308
  77.3 0.0 collective-permute-done.7.refs_1_
  77.3 0.1 shard_map.83
  77.4 5.1 %collective-permute-start.8 = (bf16[512,128]{1,0:T(8,128)(2,1)S(1)}, bf16[512,128]{1,0:T(8,128)(2,1)S(1)}, u32[]{:S(2)}, u32[]{:S(2)}) collective-permute-start(bf16[512,128]{1,0:T(8,128)(2,1)S(1)} %get-tuple-element.35), channel_id=1, source_target_pairs={{0,32},{16,48},{32,0},{48,16},{1,33},{17,49},{33,1},{49,17},{2,34}... | collective-permute-start | bytes 393224 | tf_op jit(solution)/shard_map/ppermute | solution.py:330
  82.4 2.9 %collective-permute-done.8.input_got = bf16[512,128]{1,0:T(8,128)(2,1)S(1)} collective-permute-done((bf16[512,128]{1,0:T(8,128)(2,1)S(1)}, bf16[512,128]{1,0:T(8,128)(2,1)S(1)}, u32[]{:S(2)}, u32[]{:S(2)}) %collective-permute-start.8) | collective-permute-done | bytes 131104 | tf_op jit(solution)/shard_map/ppermute | solution.py:330
  85.4 1.5 %collective-permute-done.13.got = bf16[128,1152]{1,0:T(8,128)(2,1)S(1)} collective-permute-done((bf16[128,1152]{1,0:T(8,128)(2,1)S(1)}, bf16[128,1152]{1,0:T(8,128)(2,1)S(1)}, u32[]{:S(2)}, u32[]{:S(2)}) %collective-permute-start.13) | collective-permute-done | bytes 294944 | tf_op jit(solution)/shard_map/ppermute | solution.py:308
  86.8 0.9 %shard_map.87 = (bf16[512,128]{1,0:T(8,128)(2,1)}, f32[128,1024]{1,0:T(8,128)}, f32[128,128]{1,0:T(8,128)}) custom-call(bf16[512,128]{1,0:T(8,128)(2,1)S(1)} %get-tuple-element.34.input_kept, bf16[512,128]{1,0:T(8,128)(2,1)S(1)} %collective-permute-done.8.input_got, bf16[128,1152]{1,0:T(8,128)(2,1)S(1)} %get-tuple-element.45.kept, ...), custom_call_target="tpu_custom_call" | custom-call | flops 1 | bytes 1 | tf_op jit(solution)/shard_map/pallas_call | solution.py:217
  (9 shorter events, 0.1 us)
Async XLA Ops:
  0.6 3.3 %collective-permute-start = (bf16[64,256]{1,0:T(8,128)(2,1)}, bf16[64,256]{1,0:T(8,128)(2,1)S(1)}, u32[]{:S(2)}, u32[]{:S(2)}) collective-permute-start(bf16[64,256]{1,0:T(8,128)(2,1)} %share_hbm.1), channel_id=1, source_target_pairs={{0,8},{8,0},{1,9},{9,1},{2,10},{10,2},{3,11},{11,3},{4,12},{12,4},... | collective-permute-start | bytes 98312 | tf_op jit(solution)/shard_map/ppermute | solution.py:285
  2.7 0.9 %copy-start.4 = (bf16[64,1024]{1,0:T(8,128)(2,1)S(1)}, bf16[64,1024]{1,0:T(8,128)(2,1)}, u32[]{:S(2)}) copy-start(bf16[64,1024]{1,0:T(8,128)(2,1)} %rows_ref.1) | copy-start | bytes 393220
  3.6 0.8 copy-start.3
  4.5 33.3 %copy-start.1 = (bf16[512,1024]{1,0:T(8,128)(2,1)S(1)}, bf16[512,1024]{1,0:T(8,128)(2,1)}, u32[]{:S(2)}) copy-start(bf16[512,1024]{1,0:T(8,128)(2,1)} %x_ref.5) | copy-start | bytes 3145732
  4.5 15.6 %collective-permute-start.1 = (bf16[64,1152]{1,0:T(8,128)(2,1)S(1)}, bf16[64,1152]{1,0:T(8,128)(2,1)S(1)}, u32[]{:S(2)}, u32[]{:S(2)}) collective-permute-start(bf16[64,1152]{1,0:T(8,128)(2,1)S(1)} %shard_map.77.rows_ref), channel_id=1, source_target_pairs={{0,1},{1,0},{2,3},{3,2},{4,5},{5,4},{6,7},{7,6},{8,9},{9,8},{10,11... | collective-permute-start | bytes 442376 | tf_op jit(solution)/shard_map/ppermute | solution.py:287
  15.5 7.3 %collective-permute-start.2 = (bf16[64,1152]{1,0:T(8,128)(2,1)S(1)}, bf16[64,1152]{1,0:T(8,128)(2,1)S(1)}, u32[]{:S(2)}, u32[]{:S(2)}) collective-permute-start(bf16[64,1152]{1,0:T(8,128)(2,1)S(1)} %shard_map.78), channel_id=1, source_target_pairs={{0,2},{2,0},{4,6},{6,4},{10,12},{12,10},{14,8},{8,14},{1,3},{3,1},... | collective-permute-start | bytes 442376 | tf_op jit(solution)/shard_map/ppermute | solution.py:104
  20.1 7.0 %collective-permute-start.4 = (bf16[64,1152]{1,0:T(8,128)(2,1)S(1)}, bf16[64,1152]{1,0:T(8,128)(2,1)S(1)}, u32[]{:S(2)}, u32[]{:S(2)}) collective-permute-start(bf16[64,1152]{1,0:T(8,128)(2,1)S(1)} %collective-permute-done.1), channel_id=1, source_target_pairs={{0,2},{2,0},{4,6},{6,4},{10,12},{12,10},{14,8},{8,14},{1,3},{3,1},... | collective-permute-start | bytes 442376 | tf_op jit(solution)/shard_map/ppermute | solution.py:104
  22.9 9.8 %collective-permute-start.3 = (bf16[2,64,1152]{2,1,0:T(8,128)(2,1)S(1)}, bf16[2,64,1152]{2,1,0:T(8,128)(2,1)S(1)}, u32[]{:S(2)}, u32[]{:S(2)}) collective-permute-start(bf16[2,64,1152]{2,1,0:T(8,128)(2,1)S(1)} %pad_maximum_fusion.refs_0_), channel_id=1, source_target_pairs={{0,6},{2,4},{4,2},{6,0},{10,8},{12,14},{14,12},{8,10},{1,7},{3,5},... | collective-permute-start | bytes 884744 | tf_op jit(solution)/shard_map/ppermute | solution.py:104
  27.2 15.6 %copy-start = (bf16[1024,1024]{1,0:T(8,128)(2,1)S(1)}, bf16[1024,1024]{1,0:T(8,128)(2,1)}, u32[]{:S(2)}) copy-start(bf16[1024,1024]{1,0:T(8,128)(2,1)} %param.8) | copy-start | bytes 6291460
  27.2 15.6 %copy-start.2 = (bf16[1024,128]{1,0:T(8,128)(2,1)S(1)}, bf16[1024,128]{1,0:T(8,128)(2,1)}, u32[]{:S(2)}) copy-start(bf16[1024,128]{1,0:T(8,128)(2,1)} %param.9) | copy-start | bytes 786436
  27.2 10.0 %collective-permute-start.5 = (bf16[2,64,1152]{2,1,0:T(8,128)(2,1)S(1)}, bf16[2,64,1152]{2,1,0:T(8,128)(2,1)S(1)}, u32[]{:S(2)}, u32[]{:S(2)}) collective-permute-start(bf16[2,64,1152]{2,1,0:T(8,128)(2,1)S(1)} %pad_maximum_fusion.1.refs_2_), channel_id=1, source_target_pairs={{0,6},{2,4},{4,2},{6,0},{10,8},{12,14},{14,12},{8,10},{1,7},{3,5},... | collective-permute-start | bytes 884744 | tf_op jit(solution)/shard_map/ppermute | solution.py:104
  39.3 13.9 %collective-permute-start.9 = (bf16[4,128,768]{2,1,0:T(8,128)(2,1)S(1)}, bf16[4,128,768]{2,1,0:T(8,128)(2,1)S(1)}, u32[]{:S(2)}, u32[]{:S(2)}) collective-permute-start(bf16[4,128,768]{2,1,0:T(8,128)(2,1)S(1)} %get-tuple-element.37), channel_id=1, source_target_pairs={{0,64},{72,136},{64,0},{136,72},{128,192},{200,264},{192,128},{264... | collective-permute-start | bytes 2359304 | tf_op jit(solution)/shard_map/ppermute | solution.py:308
  44.4 4.3 %collective-permute-start.6 = (bf16[4,512,128]{2,1,0:T(8,128)(2,1)S(1)}, bf16[4,512,128]{2,1,0:T(8,128)(2,1)S(1)}, u32[]{:S(2)}, u32[]{:S(2)}) collective-permute-start(bf16[4,512,128]{2,1,0:T(8,128)(2,1)S(1)} %shard_map.81), channel_id=1, source_target_pairs={{0,8},{8,0},{1,9},{9,1},{2,10},{10,2},{3,11},{11,3},{4,12},{12,4},... | collective-permute-start | bytes 1572872 | tf_op jit(solution)/shard_map/ppermute | solution.py:314
  46.3 13.4 %collective-permute-start.11 = (bf16[4,128,384]{2,1,0:T(8,128)(2,1)S(1)}, bf16[4,128,384]{2,1,0:T(8,128)(2,1)S(1)}, u32[]{:S(2)}, u32[]{:S(2)}) collective-permute-start(bf16[4,128,384]{2,1,0:T(8,128)(2,1)S(1)} %get-tuple-element.41), channel_id=1, source_target_pairs={{0,64},{72,136},{64,0},{136,72},{128,192},{200,264},{192,128},{264... | collective-permute-start | bytes 1179656 | tf_op jit(solution)/shard_map/ppermute | solution.py:308
  54.3 17.4 %collective-permute-start.10 = (bf16[2,128,768]{2,1,0:T(8,128)(2,1)S(1)}, bf16[2,128,768]{2,1,0:T(8,128)(2,1)S(1)}, u32[]{:S(2)}, u32[]{:S(2)}) collective-permute-start(bf16[2,128,768]{2,1,0:T(8,128)(2,1)S(1)} %get-tuple-element.40), channel_id=1, source_target_pairs={{0,448},{72,8},{64,128},{136,200},{128,64},{200,136},{192,256},{26... | collective-permute-start | bytes 1179656 | tf_op jit(solution)/shard_map/ppermute | solution.py:308
  60.8 10.9 %collective-permute-start.12 = (bf16[2,128,384]{2,1,0:T(8,128)(2,1)S(1)}, bf16[2,128,384]{2,1,0:T(8,128)(2,1)S(1)}, u32[]{:S(2)}, u32[]{:S(2)}) collective-permute-start(bf16[2,128,384]{2,1,0:T(8,128)(2,1)S(1)} %get-tuple-element.44), channel_id=1, source_target_pairs={{0,448},{72,8},{64,128},{136,200},{128,64},{200,136},{192,256},{26... | collective-permute-start | bytes 589832 | tf_op jit(solution)/shard_map/ppermute | solution.py:308
  64.4 12.9 %collective-permute-start.7 = (bf16[2,512,128]{2,1,0:T(8,128)(2,1)S(1)}, bf16[2,512,128]{2,1,0:T(8,128)(2,1)S(1)}, u32[]{:S(2)}, u32[]{:S(2)}) collective-permute-start(bf16[2,512,128]{2,1,0:T(8,128)(2,1)S(1)} %get-tuple-element.33), channel_id=1, source_target_pairs={{0,16},{16,0},{32,48},{48,32},{1,17},{17,1},{33,49},{49,33},{2,18}... | collective-permute-start | bytes 786440 | tf_op jit(solution)/shard_map/ppermute | solution.py:316
  71.9 15.0 %collective-permute-start.13 = (bf16[128,1152]{1,0:T(8,128)(2,1)S(1)}, bf16[128,1152]{1,0:T(8,128)(2,1)S(1)}, u32[]{:S(2)}, u32[]{:S(2)}) collective-permute-start(bf16[128,1152]{1,0:T(8,128)(2,1)S(1)} %get-tuple-element.46), channel_id=1, source_target_pairs={{0,192},{72,264},{64,384},{136,456},{128,320},{200,392},{192,0},{2... | collective-permute-start | bytes 884744 | tf_op jit(solution)/shard_map/ppermute | solution.py:308
  77.4 8.0 %collective-permute-start.8 = (bf16[512,128]{1,0:T(8,128)(2,1)S(1)}, bf16[512,128]{1,0:T(8,128)(2,1)S(1)}, u32[]{:S(2)}, u32[]{:S(2)}) collective-permute-start(bf16[512,128]{1,0:T(8,128)(2,1)S(1)} %get-tuple-element.35), channel_id=1, source_target_pairs={{0,32},{16,48},{32,0},{48,16},{1,33},{17,49},{33,1},{49,17},{2,34}... | collective-permute-start | bytes 393224 | tf_op jit(solution)/shard_map/ppermute | solution.py:330

commit v9 on v8

--- a/solution.py
+++ b/solution.py
@@ -104,68 +104,68 @@
     return lax.ppermute(rows, ("core", "x"), pairs)
 
 
-def all_along_x(rows):
-    pair = jnp.stack([rows, x_swap(rows, lambda u: u ^ 1)])
-    return pair, x_swap(pair, lambda u: 3 - u)
-
-
-def order_body(place, *refs):
+def first_pair(rows):
+    return jnp.stack([rows, x_swap(rows, lambda u: u ^ 1)])
+
+
+def second_pair(pair):
+    return x_swap(pair, lambda u: 3 - u)
+
+
+def order_body(at, place, *refs):
     *pairs, out_ref = refs
+    width = out_ref.shape[-1]
     for i, pair in enumerate(pairs):
         zhi = place[4] if i < 2 else 1 - place[4]
         for j in range(2):
-            out_ref[2 * place[2 * (i % 2) + j] + zhi] = pair[j]
-
-
-def in_order(place, *pairs):
-    _, rows, columns = pairs[0].shape
-    return pl.pallas_call(
-        order_body,
-        out_shape=jax.ShapeDtypeStruct((2 * len(pairs), rows, columns), pairs[0].dtype),
+            rows = pair[j] if pair.shape[-1] == width else pair[j, :, at : at + width]
+            out_ref[2 * place[2 * (i % 2) + j] + zhi] = rows
+
+
+def in_order(at, place, *pairs):
+    _, rows, width = pairs[-1].shape
+    return pl.pallas_call(
+        functools.partial(order_body, at),
+        out_shape=jax.ShapeDtypeStruct((2 * len(pairs), rows, width), pairs[0].dtype),
         in_specs=[SMEM] + [VMEM] * len(pairs),
         out_specs=VMEM,
         compiler_params=PARAMS,
         cost_estimate=COST,
-    )(place, *pairs).reshape(-1, columns)
+    )(place, *pairs).reshape(-1, width)
 
 
 def dot(left, right, dims):
     return lax.dot_general(left, right, ((dims[:1], dims[1:]), ((), ())), preferred_element_type=jnp.float32)
 
 
-def give_body(blocks, x_ref, g_ref, *outs):
+def give_body(blocks, x_ref, g_ref, out_ref):
     for r in range(N_PAIRS):
         columns = x_ref[:, pl.ds(pl.multiple_of(blocks[r] * 128, 128), 128)]
-        at = 0
-        for out in outs:
-            width = out.shape[-1]
-            out[r] = dot(columns, g_ref[:, at : at + width], (0, 0)).astype(out.dtype)
-            at += width
+        out_ref[r] = dot(columns, g_ref[...], (0, 0)).astype(out_ref.dtype)
 
 
 def give_terms(blocks, x, g):
     return pl.pallas_call(
         give_body,
-        out_shape=[jax.ShapeDtypeStruct((N_PAIRS, 128, width), jnp.bfloat16) for width in PARTS],
+        out_shape=jax.ShapeDtypeStruct((N_PAIRS, 128, g.shape[1]), jnp.bfloat16),
         in_specs=[SMEM] + [VMEM] * 2,
-        out_specs=[VMEM] * len(PARTS),
+        out_specs=VMEM,
         compiler_params=PARAMS,
         cost_estimate=COST,
     )(blocks, x, g)
 
 
-def keep_body(at, blocks, x_ref, g_ref, got_ref, give_ref, keep_ref):
-    width = got_ref.shape[-1]
+def keep_body(blocks, x_ref, g_ref, got_ref, give_ref, keep_ref):
     for r in range(N_PAIRS):
         columns = x_ref[:, pl.ds(pl.multiple_of(blocks[r] * 128, 128), 128)]
-        term = dot(columns, g_ref[:, at : at + width], (0, 0)) + got_ref[r].astype(jnp.float32)
+        term = dot(columns, g_ref[...], (0, 0)) + got_ref[r].astype(jnp.float32)
         out = give_ref if r < 2 else keep_ref
         out[r % 2] = term.astype(out.dtype)
 
 
-def keep_terms(blocks, x, g, got, at):
-    return pl.pallas_call(
-        functools.partial(keep_body, at),
+def keep_terms(blocks, x, g, got):
+    return pl.pallas_call(
+        keep_body,
         out_shape=[jax.ShapeDtypeStruct((2, *got.shape[1:]), jnp.bfloat16)] * 2,
         in_specs=[SMEM] + [VMEM] * 3,
         out_specs=[VMEM] * 2,
@@ -225,11 +225,13 @@
     )(*arrays)
 
 
-def input_body(blocks, g_ref, wq_one, wq_two, wkv_one, wkv_two, *refs):
+def input_body(blocks, one_ref, two_ref, wq_one, wq_two, wkv_one, wkv_two, *refs):
     n_q = wq_one.shape[-1]
     wq = jnp.concatenate([wq_one[0], wq_two[0]])
     wkv = jnp.concatenate([wkv_one[0], wkv_two[0]])
-    term = dot(g_ref[:, :n_q], wq, (1, 1)) + dot(g_ref[:, n_q:], wkv, (1, 1))
+    split = one_ref.shape[1]
+    term = dot(one_ref[...], wq[:, :split], (1, 1)) + dot(two_ref[:, : n_q - split], wq[:, split:], (1, 1))
+    term = term + dot(two_ref[:, n_q - split :], wkv, (1, 1))
     pair = [term[:, :128], term[:, 128:]]
     if len(refs) == 1:
         for i in range(2):
@@ -244,9 +246,9 @@
                 out[i] = (pair[i] + got_ref[i].astype(jnp.float32)).astype(jnp.bfloat16)
 
 
-def input_terms(blocks, g, wq, wkv, *got):
+def input_terms(blocks, one_part, two_part, wq, wkv, *got):
     n_q, n_kv = wq.shape[1], wkv.shape[1]
-    rows = g.shape[0]
+    rows = one_part.shape[0]
     n = blocks.shape[0]
     one = lambda r, blocks: (blocks[2 * r], 0, 0)
     two = lambda r, blocks: (blocks[2 * r + 1], 0, 0)
@@ -261,7 +263,8 @@
             num_scalar_prefetch=1,
             grid=(n // 2,),
             in_specs=[
-                pl.BlockSpec(g.shape, lambda r, blocks: (0, 0)),
+                pl.BlockSpec(one_part.shape, lambda r, blocks: (0, 0)),
+                pl.BlockSpec(two_part.shape, lambda r, blocks: (0, 0)),
                 pl.BlockSpec((1, 128, n_q), one),
                 pl.BlockSpec((1, 128, n_q), two),
                 pl.BlockSpec((1, 128, n_kv), one),
@@ -273,7 +276,7 @@
         out_shape=[jax.ShapeDtypeStruct((n // len(places), rows, 128), jnp.bfloat16) for _ in places],
         compiler_params=PARAMS,
         cost_estimate=COST,
-    )(blocks, g, wq, wq, wkv, wkv, *got)
+    )(blocks, one_part, two_part, wq, wq, wkv, wkv, *got)
 
 
 def local(inputs, q_grad, key_value_share_gradient, q_weight, key_value_weight):
@@ -299,30 +302,37 @@
     place = jnp.stack([u, u ^ 1, 3 - u, (3 - u) ^ 1, zhi - core])
     place = (place + core) % 4
     orders = (place, keep_blocks, give_blocks, give_heads, keep_heads)
-    near = all_along_x(again(mine))
+    near = first_pair(again(mine))
+    near = [near, second_pair(near)]
     far, orders = lax.optimization_barrier((far, orders))
     place, keep_blocks, give_blocks, give_heads, keep_heads = orders
-    combined = in_order(place, *near, *all_along_x(far))
+    pair = first_pair(far)
+    others = []
+    at = 0
+    for width in PARTS:
+        others.append(second_pair(pair[:, :, at : at + width]))
+        at += width
 
     def along_y(terms, pairs):
         return lax.ppermute(terms, (*TOK, "core"), pairs)
 
-    given = give_terms(give_blocks, inputs, combined)
-    first, for_input = lax.optimization_barrier((given[0], combined))
-    got = [along_y(part, FIRST) for part in (first, *given[1:])]
-    (give,) = input_terms(give_heads, for_input, q_weight, key_value_weight)
+    combined = [in_order(0, place, *near, pair, others[0])]
+    given = [give_terms(give_blocks, inputs, combined[0])]
+    given[0], others[1] = lax.optimization_barrier((given[0], others[1]))
+    combined.append(in_order(PARTS[0], place, *near, pair, others[1]))
+    given.append(give_terms(give_blocks, inputs, combined[1]))
+    got = [along_y(part, FIRST) for part in given]
+    (give,) = input_terms(give_heads, *combined, q_weight, key_value_weight)
     core_got = lax.ppermute(give, "core", SWAP)
-    give, input_keep = input_terms(keep_heads, for_input, q_weight, key_value_weight, core_got)
+    give, input_keep = input_terms(keep_heads, *combined, q_weight, key_value_weight, core_got)
     input_got = lax.ppermute(give, "zlo", [(i, i ^ 1) for i in range(4)])
 
     after = input_keep
     parts = []
-    at = 0
-    for part in got:
+    for columns, part in zip(combined, got):
         part, _ = lax.optimization_barrier((part, after))
-        give, after = keep_terms(keep_blocks, inputs, combined, part, at)
+        give, after = keep_terms(keep_blocks, inputs, columns, part)
         parts += [after, along_y(give, SECOND)]
-        at += part.shape[-1]
     keep, give = add_terms(*parts)
     got = along_y(give, THIRD)
 

time: 89 us -> 89.4 us (level)
  the two profiles are of different devices: /device:TPU:6 before, /device:TPU:64 now
where the time goes in v9:
time: 89.4 us; the launch traced here: 88.8 us
  starting transfers between devices  54.7 us (61%)
  waiting for transfers between devices  20.9 us (23%)
  Pallas kernels  10.3 us (12%)
  local copies, waits for them, and re-layouts  1.31 us (1%)
  between operations  1.27 us (1%)
    ppermute x5, starting transfers between devices, along_y(): return lax.ppermute(terms, (*TOK, 'core'), pairs)  19.2 us
    ppermute x5, starting transfers between devices, x_swap(): return lax.ppermute(rows, ('core', 'x'), pairs)  17.8 us
    ppermute x1, starting transfers between devices, local(): far = lax.ppermute(mine, 'zhi', SWAP)  10 us
    ppermute x5, waiting for transfers between devices, along_y(): return lax.ppermute(terms, (*TOK, 'core'), pairs)  7.2 us
    ppermute x1, waiting for transfers between devices, local(): input_got = lax.ppermute(give, 'zlo', [(i, i ^ 2) for i in range(4)])  5.83 us
    ppermute x1, waiting for transfers between devices, local(): far = lax.ppermute(mine, 'zhi', SWAP)  4.01 us
    ppermute x5, waiting for transfers between devices, x_swap(): return lax.ppermute(rows, ('core', 'x'), pairs)  3.62 us
    pallas_call x2, Pallas kernels, input_terms(): pl.pallas_call(input_body, grid_spec=pltpu.PrefetchScalarGridSpec(num_sca...  3.45 us
  transfers between devices with their start and end apart: 15, of which 8 were waited for; matrix products, arithmetic and copies ran while one was open for 0% of the time, Pallas kernels for 10%

profile of v9, /device:TPU:64, one launch (start us, length us, event | category | flops | bytes accessed | tf_op | source)
XLA Modules:
  0.0 88.8 jit_solution(10041066496064997851)
XLA Ops:
  0.6 1.9 %collective-permute-start = (bf16[64,256]{1,0:T(8,128)(2,1)}, bf16[64,256]{1,0:T(8,128)(2,1)S(1)}, u32[]{:S(2)}, u32[]{:S(2)}) collective-permute-start(bf16[64,256]{1,0:T(8,128)(2,1)} %share_hbm.1), channel_id=1, source_target_pairs={{0,8},{8,0},{1,9},{9,1},{2,10},{10,2},{3,11},{11,3},{4,12},{12,4},... | collective-permute-start | bytes 98312 | tf_op jit(solution)/shard_map/ppermute | solution.py:288
  2.6 0.9 %copy-done.4 = bf16[64,1024]{1,0:T(8,128)(2,1)S(1)} copy-done((bf16[64,1024]{1,0:T(8,128)(2,1)S(1)}, bf16[64,1024]{1,0:T(8,128)(2,1)}, u32[]{:S(2)}) %copy-start.4) | copy-done | bytes 131096
  3.5 0.1 stack.86
  3.6 0.1 broadcast_add_fusion
  3.7 0.3 collective-permute-done.more_ref
  3.9 0.3 copy-done.3
  4.2 0.1 shard_map.77.rows_ref
  4.3 10.0 %collective-permute-start.1 = (bf16[64,1152]{1,0:T(8,128)(2,1)S(1)}, bf16[64,1152]{1,0:T(8,128)(2,1)S(1)}, u32[]{:S(2)}, u32[]{:S(2)}) collective-permute-start(bf16[64,1152]{1,0:T(8,128)(2,1)S(1)} %shard_map.77.rows_ref), channel_id=1, source_target_pairs={{0,1},{1,0},{2,3},{3,2},{4,5},{5,4},{6,7},{7,6},{8,9},{9,8},{10,11... | collective-permute-start | bytes 442376 | tf_op jit(solution)/shard_map/ppermute | solution.py:290
  14.4 3.4 %collective-permute-start.2 = (bf16[64,1152]{1,0:T(8,128)(2,1)S(1)}, bf16[64,1152]{1,0:T(8,128)(2,1)S(1)}, u32[]{:S(2)}, u32[]{:S(2)}) collective-permute-start(bf16[64,1152]{1,0:T(8,128)(2,1)S(1)} %shard_map.78), channel_id=1, source_target_pairs={{0,2},{2,0},{4,6},{6,4},{10,12},{12,10},{14,8},{8,14},{1,3},{3,1},... | collective-permute-start | bytes 442376 | tf_op jit(solution)/shard_map/ppermute | solution.py:104
  17.9 0.0 copy-start.1
  18.1 0.1 and_select_fusion
  18.2 4.0 %collective-permute-done.1 = bf16[64,1152]{1,0:T(8,128)(2,1)S(1)} collective-permute-done((bf16[64,1152]{1,0:T(8,128)(2,1)S(1)}, bf16[64,1152]{1,0:T(8,128)(2,1)S(1)}, u32[]{:S(2)}, u32[]{:S(2)}) %collective-permute-start.1) | collective-permute-done | bytes 147488 | tf_op jit(solution)/shard_map/ppermute | solution.py:290
  22.2 3.4 %collective-permute-start.4 = (bf16[64,1152]{1,0:T(8,128)(2,1)S(1)}, bf16[64,1152]{1,0:T(8,128)(2,1)S(1)}, u32[]{:S(2)}, u32[]{:S(2)}) collective-permute-start(bf16[64,1152]{1,0:T(8,128)(2,1)S(1)} %collective-permute-done.1), channel_id=1, source_target_pairs={{0,2},{2,0},{4,6},{6,4},{10,12},{12,10},{14,8},{8,14},{1,3},{3,1},... | collective-permute-start | bytes 442376 | tf_op jit(solution)/shard_map/ppermute | solution.py:104
  25.6 0.0 collective-permute-done.2
  25.6 4.0 %collective-permute-start.3 = (bf16[2,64,1152]{2,1,0:T(8,128)(2,1)S(1)}, bf16[2,64,1152]{2,1,0:T(8,128)(2,1)S(1)}, u32[]{:S(2)}, u32[]{:S(2)}) collective-permute-start(bf16[2,64,1152]{2,1,0:T(8,128)(2,1)S(1)} %pad_maximum_fusion.1.refs_0_), channel_id=1, source_target_pairs={{0,6},{2,4},{4,2},{6,0},{10,8},{12,14},{14,12},{8,10},{1,7},{3,5},... | collective-permute-start | bytes 884744 | tf_op jit(solution)/shard_map/ppermute | solution.py:104
  29.6 0.0 collective-permute-done.4
  29.7 4.8 %collective-permute-start.5 = (bf16[2,64,768]{2,1,0:T(8,128)(2,1)S(1)}, bf16[2,64,768]{2,1,0:T(8,128)(2,1)S(1)}, u32[]{:S(2)}, u32[]{:S(2)}) collective-permute-start(bf16[2,64,768]{2,1,0:T(8,128)(2,1)S(1)} %fusion), channel_id=1, source_target_pairs={{0,6},{2,4},{4,2},{6,0},{10,8},{12,14},{14,12},{8,10},{1,7},{3,5},... | collective-permute-start | bytes 589832 | tf_op jit(solution)/shard_map/ppermute | solution.py:104
  34.5 2.2 %collective-permute-start.6 = (bf16[2,64,384]{2,1,0:T(8,128)(2,1)S(1)}, bf16[2,64,384]{2,1,0:T(8,128)(2,1)S(1)}, u32[]{:S(2)}, u32[]{:S(2)}) collective-permute-start(bf16[2,64,384]{2,1,0:T(8,128)(2,1)S(1)} %fusion.1), channel_id=1, source_target_pairs={{0,6},{2,4},{4,2},{6,0},{10,8},{12,14},{14,12},{8,10},{1,7},{3,5},... | collective-permute-start | bytes 294920 | tf_op jit(solution)/shard_map/ppermute | solution.py:104
  36.8 0.0 collective-permute-done.3.refs_1_
  36.8 1.6 %collective-permute-done.5.refs_3_ = bf16[2,64,768]{2,1,0:T(8,128)(2,1)S(1)} collective-permute-done((bf16[2,64,768]{2,1,0:T(8,128)(2,1)S(1)}, bf16[2,64,768]{2,1,0:T(8,128)(2,1)S(1)}, u32[]{:S(2)}, u32[]{:S(2)}) %collective-permute-start.5) | collective-permute-done | bytes 196640 | tf_op jit(solution)/shard_map/ppermute | solution.py:104
  38.4 0.6 shard_map.79
  39.0 0.0 copy-start
  39.1 0.0 copy-start.2
  39.1 1.2 %shard_map.80 = bf16[4,128,768]{2,1,0:T(8,128)(2,1)S(1)} custom-call(s32[4]{0:T(128)S(1)} %get-tuple-element.26.blocks, bf16[512,1024]{1,0:T(8,128)(2,1)S(1)} %copy-done.1, bf16[512,768]{1,0:T(8,128)(2,1)S(1)} %bitcast.30), custom_call_target="tpu_custom_call" | custom-call | flops 1 | bytes 1 | tf_op jit(solution)/shard_map/pallas_call | solution.py:148
  40.3 2.0 %collective-permute-done.6.refs_3_ = bf16[2,64,384]{2,1,0:T(8,128)(2,1)S(1)} collective-permute-done((bf16[2,64,384]{2,1,0:T(8,128)(2,1)S(1)}, bf16[2,64,384]{2,1,0:T(8,128)(2,1)S(1)}, u32[]{:S(2)}, u32[]{:S(2)}) %collective-permute-start.6) | collective-permute-done | bytes 98336 | tf_op jit(solution)/shard_map/ppermute | solution.py:104
  42.3 3.5 %collective-permute-start.10 = (bf16[4,128,768]{2,1,0:T(8,128)(2,1)S(1)}, bf16[4,128,768]{2,1,0:T(8,128)(2,1)S(1)}, u32[]{:S(2)}, u32[]{:S(2)}) collective-permute-start(bf16[4,128,768]{2,1,0:T(8,128)(2,1)S(1)} %shard_map.80), channel_id=1, source_target_pairs={{0,64},{72,136},{64,0},{136,72},{128,192},{200,264},{192,128},{264... | collective-permute-start | bytes 2359304 | tf_op jit(solution)/shard_map/ppermute | solution.py:317
  45.7 0.6 shard_map.81
  46.3 1.7 %shard_map.82 = bf16[4,512,128]{2,1,0:T(8,128)(2,1)S(1)} custom-call(s32[4]{0:T(128)S(1)} %add_subtract_fusion.blocks, bf16[512,768]{1,0:T(8,128)(2,1)S(1)} %bitcast.31, bf16[512,384]{1,0:T(8,128)(2,1)S(1)} %bitcast.34, bf16[8,128,1024]{2,1,0:T(8,128)(2,1)S(1)} %bitcast.26, bf16[8,128,1024]{2,1,0:T(8,128)(2,1)S(1)} %bitcast.27, ...), custom_call_target="tpu_custom_call" | custom-call | flops 1 | bytes 1 | tf_op jit(solution)/shard_map/pallas_call | solution.py:260
  48.0 1.9 %collective-permute-start.7 = (bf16[4,512,128]{2,1,0:T(8,128)(2,1)S(1)}, bf16[4,512,128]{2,1,0:T(8,128)(2,1)S(1)}, u32[]{:S(2)}, u32[]{:S(2)}) collective-permute-start(bf16[4,512,128]{2,1,0:T(8,128)(2,1)S(1)} %shard_map.82), channel_id=1, source_target_pairs={{0,8},{8,0},{1,9},{9,1},{2,10},{10,2},{3,11},{11,3},{4,12},{12,4},... | collective-permute-start | bytes 1572872 | tf_op jit(solution)/shard_map/ppermute | solution.py:326
  50.0 1.0 %shard_map.86 = bf16[4,128,384]{2,1,0:T(8,128)(2,1)S(1)} custom-call(s32[4]{0:T(128)S(1)} %get-tuple-element.26.blocks, bf16[512,1024]{1,0:T(8,128)(2,1)S(1)} %copy-done.1, bf16[512,384]{1,0:T(8,128)(2,1)S(1)} %bitcast.35), custom_call_target="tpu_custom_call" | custom-call | flops 1 | bytes 1 | tf_op jit(solution)/shard_map/pallas_call | solution.py:148
  51.0 2.4 %collective-permute-start.12 = (bf16[4,128,384]{2,1,0:T(8,128)(2,1)S(1)}, bf16[4,128,384]{2,1,0:T(8,128)(2,1)S(1)}, u32[]{:S(2)}, u32[]{:S(2)}) collective-permute-start(bf16[4,128,384]{2,1,0:T(8,128)(2,1)S(1)} %shard_map.86), channel_id=1, source_target_pairs={{0,64},{72,136},{64,0},{136,72},{128,192},{200,264},{192,128},{264... | collective-permute-start | bytes 1179656 | tf_op jit(solution)/shard_map/ppermute | solution.py:317
  53.4 0.0 collective-permute-done.7.refs_0_
  53.4 1.8 %shard_map.83 = (bf16[2,512,128]{2,1,0:T(8,128)(2,1)S(1)}, bf16[2,512,128]{2,1,0:T(8,128)(2,1)S(1)}) custom-call(s32[4]{0:T(128)S(1)} %get-tuple-element.23.blocks, bf16[512,768]{1,0:T(8,128)(2,1)S(1)} %bitcast.32, bf16[512,384]{1,0:T(8,128)(2,1)S(1)} %bitcast.36, bf16[8,128,1024]{2,1,0:T(8,128)(2,1)S(1)} %bitcast.28, bf16[8,128,1024]{2,1,0:T(8,128)(2,1)S(1)} %bitcast.29, ...), custom_call_target="tpu_custom_call" | custom-call | flops 1 | bytes 1 | tf_op jit(solution)/shard_map/pallas_call | solution.py:260
  55.2 0.9 %collective-permute-done.10.got_ref = bf16[4,128,768]{2,1,0:T(8,128)(2,1)S(1)} collective-permute-done((bf16[4,128,768]{2,1,0:T(8,128)(2,1)S(1)}, bf16[4,128,768]{2,1,0:T(8,128)(2,1)S(1)}, u32[]{:S(2)}, u32[]{:S(2)}) %collective-permute-start.10) | collective-permute-done | bytes 786464 | tf_op jit(solution)/shard_map/ppermute | solution.py:317
  56.1 1.2 %shard_map.85 = (bf16[2,128,768]{2,1,0:T(8,128)(2,1)S(1)}, bf16[2,128,768]{2,1,0:T(8,128)(2,1)S(1)}) custom-call(s32[4]{0:T(128)S(1)} %get-tuple-element.33.blocks, bf16[512,1024]{1,0:T(8,128)(2,1)S(1)} %copy-done.1, bf16[512,768]{1,0:T(8,128)(2,1)S(1)} %bitcast.33, bf16[4,128,768]{2,1,0:T(8,128)(2,1)S(1)} %collective-permute-done.10.got_ref), custom_call_target="tpu_custom_call" | custom-call | flops 1 | bytes 1 | tf_op jit(solution)/shard_map/pallas_call | solution.py:167
  57.3 5.4 %collective-permute-start.11 = (bf16[2,128,768]{2,1,0:T(8,128)(2,1)S(1)}, bf16[2,128,768]{2,1,0:T(8,128)(2,1)S(1)}, u32[]{:S(2)}, u32[]{:S(2)}) collective-permute-start(bf16[2,128,768]{2,1,0:T(8,128)(2,1)S(1)} %get-tuple-element.37), channel_id=1, source_target_pairs={{0,448},{72,8},{64,128},{136,200},{128,64},{200,136},{192,256},{26... | collective-permute-start | bytes 1179656 | tf_op jit(solution)/shard_map/ppermute | solution.py:317
  62.7 1.0 %shard_map.87 = (bf16[2,128,384]{2,1,0:T(8,128)(2,1)S(1)}, bf16[2,128,384]{2,1,0:T(8,128)(2,1)S(1)}) custom-call(s32[4]{0:T(128)S(1)} %get-tuple-element.33.blocks, bf16[512,1024]{1,0:T(8,128)(2,1)S(1)} %copy-done.1, bf16[512,384]{1,0:T(8,128)(2,1)S(1)} %bitcast.37, bf16[4,128,384]{2,1,0:T(8,128)(2,1)S(1)} %collective-permute-done.12.got_ref), custom_call_target="tpu_custom_call" | custom-call | flops 1 | bytes 1 | tf_op jit(solution)/shard_map/pallas_call | solution.py:167
  63.8 3.1 %collective-permute-start.13 = (bf16[2,128,384]{2,1,0:T(8,128)(2,1)S(1)}, bf16[2,128,384]{2,1,0:T(8,128)(2,1)S(1)}, u32[]{:S(2)}, u32[]{:S(2)}) collective-permute-start(bf16[2,128,384]{2,1,0:T(8,128)(2,1)S(1)} %get-tuple-element.40), channel_id=1, source_target_pairs={{0,448},{72,8},{64,128},{136,200},{128,64},{200,136},{192,256},{26... | collective-permute-start | bytes 589832 | tf_op jit(solution)/shard_map/ppermute | solution.py:317
  66.9 1.9 %collective-permute-start.8 = (bf16[2,512,128]{2,1,0:T(8,128)(2,1)S(1)}, bf16[2,512,128]{2,1,0:T(8,128)(2,1)S(1)}, u32[]{:S(2)}, u32[]{:S(2)}) collective-permute-start(bf16[2,512,128]{2,1,0:T(8,128)(2,1)S(1)} %get-tuple-element.30), channel_id=1, source_target_pairs={{0,16},{16,0},{32,48},{48,32},{1,17},{17,1},{33,49},{49,33},{2,18}... | collective-permute-start | bytes 786440 | tf_op jit(solution)/shard_map/ppermute | solution.py:328
  68.8 3.7 %collective-permute-done.13.refs_3_ = bf16[2,128,384]{2,1,0:T(8,128)(2,1)S(1)} collective-permute-done((bf16[2,128,384]{2,1,0:T(8,128)(2,1)S(1)}, bf16[2,128,384]{2,1,0:T(8,128)(2,1)S(1)}, u32[]{:S(2)}, u32[]{:S(2)}) %collective-permute-start.13) | collective-permute-done | bytes 196640 | tf_op jit(solution)/shard_map/ppermute | solution.py:317
  72.5 0.0 collective-permute-done.11.refs_1_
  72.5 0.2 shard_map.88
  72.7 4.8 %collective-permute-start.14 = (bf16[128,1152]{1,0:T(8,128)(2,1)S(1)}, bf16[128,1152]{1,0:T(8,128)(2,1)S(1)}, u32[]{:S(2)}, u32[]{:S(2)}) collective-permute-start(bf16[128,1152]{1,0:T(8,128)(2,1)S(1)} %get-tuple-element.42), channel_id=1, source_target_pairs={{0,192},{72,264},{64,384},{136,456},{128,320},{200,392},{192,0},{2... | collective-permute-start | bytes 884744 | tf_op jit(solution)/shard_map/ppermute | solution.py:317
  77.5 0.1 shard_map.84
  77.6 1.9 %collective-permute-start.9 = (bf16[512,128]{1,0:T(8,128)(2,1)S(1)}, bf16[512,128]{1,0:T(8,128)(2,1)S(1)}, u32[]{:S(2)}, u32[]{:S(2)}) collective-permute-start(bf16[512,128]{1,0:T(8,128)(2,1)S(1)} %get-tuple-element.32), channel_id=1, source_target_pairs={{0,32},{16,48},{32,0},{48,16},{1,33},{17,49},{33,1},{49,17},{2,34}... | collective-permute-start | bytes 393224 | tf_op jit(solution)/shard_map/ppermute | solution.py:340
  79.5 5.8 %collective-permute-done.9.input_got = bf16[512,128]{1,0:T(8,128)(2,1)S(1)} collective-permute-done((bf16[512,128]{1,0:T(8,128)(2,1)S(1)}, bf16[512,128]{1,0:T(8,128)(2,1)S(1)}, u32[]{:S(2)}, u32[]{:S(2)}) %collective-permute-start.9) | collective-permute-done | bytes 131104 | tf_op jit(solution)/shard_map/ppermute | solution.py:340
  85.4 2.5 %collective-permute-done.14.got = bf16[128,1152]{1,0:T(8,128)(2,1)S(1)} collective-permute-done((bf16[128,1152]{1,0:T(8,128)(2,1)S(1)}, bf16[128,1152]{1,0:T(8,128)(2,1)S(1)}, u32[]{:S(2)}, u32[]{:S(2)}) %collective-permute-start.14) | collective-permute-done | bytes 294944 | tf_op jit(solution)/shard_map/ppermute | solution.py:317
  87.9 0.9 %shard_map.89 = (bf16[512,128]{1,0:T(8,128)(2,1)}, f32[128,1024]{1,0:T(8,128)}, f32[128,128]{1,0:T(8,128)}) custom-call(bf16[512,128]{1,0:T(8,128)(2,1)S(1)} %get-tuple-element.31.input_kept, bf16[512,128]{1,0:T(8,128)(2,1)S(1)} %collective-permute-done.9.input_got, bf16[128,1152]{1,0:T(8,128)(2,1)S(1)} %get-tuple-element.41.kept, ...), custom_call_target="tpu_custom_call" | custom-call | flops 1 | bytes 1 | tf_op jit(solution)/shard_map/pallas_call | solution.py:217
  (15 shorter events, 0.2 us)
Async XLA Ops:
  0.6 3.3 %collective-permute-start = (bf16[64,256]{1,0:T(8,128)(2,1)}, bf16[64,256]{1,0:T(8,128)(2,1)S(1)}, u32[]{:S(2)}, u32[]{:S(2)}) collective-permute-start(bf16[64,256]{1,0:T(8,128)(2,1)} %share_hbm.1), channel_id=1, source_target_pairs={{0,8},{8,0},{1,9},{9,1},{2,10},{10,2},{3,11},{11,3},{4,12},{12,4},... | collective-permute-start | bytes 98312 | tf_op jit(solution)/shard_map/ppermute | solution.py:288
  2.6 0.9 %copy-start.4 = (bf16[64,1024]{1,0:T(8,128)(2,1)S(1)}, bf16[64,1024]{1,0:T(8,128)(2,1)}, u32[]{:S(2)}) copy-start(bf16[64,1024]{1,0:T(8,128)(2,1)} %rows_ref.1) | copy-start | bytes 393220
  3.5 0.8 copy-start.3
  4.3 17.8 %collective-permute-start.1 = (bf16[64,1152]{1,0:T(8,128)(2,1)S(1)}, bf16[64,1152]{1,0:T(8,128)(2,1)S(1)}, u32[]{:S(2)}, u32[]{:S(2)}) collective-permute-start(bf16[64,1152]{1,0:T(8,128)(2,1)S(1)} %shard_map.77.rows_ref), channel_id=1, source_target_pairs={{0,1},{1,0},{2,3},{3,2},{4,5},{5,4},{6,7},{7,6},{8,9},{9,8},{10,11... | collective-permute-start | bytes 442376 | tf_op jit(solution)/shard_map/ppermute | solution.py:290
  14.4 11.2 %collective-permute-start.2 = (bf16[64,1152]{1,0:T(8,128)(2,1)S(1)}, bf16[64,1152]{1,0:T(8,128)(2,1)S(1)}, u32[]{:S(2)}, u32[]{:S(2)}) collective-permute-start(bf16[64,1152]{1,0:T(8,128)(2,1)S(1)} %shard_map.78), channel_id=1, source_target_pairs={{0,2},{2,0},{4,6},{6,4},{10,12},{12,10},{14,8},{8,14},{1,3},{3,1},... | collective-permute-start | bytes 442376 | tf_op jit(solution)/shard_map/ppermute | solution.py:104
  17.9 21.2 %copy-start.1 = (bf16[512,1024]{1,0:T(8,128)(2,1)S(1)}, bf16[512,1024]{1,0:T(8,128)(2,1)}, u32[]{:S(2)}) copy-start(bf16[512,1024]{1,0:T(8,128)(2,1)} %x_ref.7) | copy-start | bytes 3145732
  22.2 7.5 %collective-permute-start.4 = (bf16[64,1152]{1,0:T(8,128)(2,1)S(1)}, bf16[64,1152]{1,0:T(8,128)(2,1)S(1)}, u32[]{:S(2)}, u32[]{:S(2)}) collective-permute-start(bf16[64,1152]{1,0:T(8,128)(2,1)S(1)} %collective-permute-done.1), channel_id=1, source_target_pairs={{0,2},{2,0},{4,6},{6,4},{10,12},{12,10},{14,8},{8,14},{1,3},{3,1},... | collective-permute-start | bytes 442376 | tf_op jit(solution)/shard_map/ppermute | solution.py:104
  25.6 11.2 %collective-permute-start.3 = (bf16[2,64,1152]{2,1,0:T(8,128)(2,1)S(1)}, bf16[2,64,1152]{2,1,0:T(8,128)(2,1)S(1)}, u32[]{:S(2)}, u32[]{:S(2)}) collective-permute-start(bf16[2,64,1152]{2,1,0:T(8,128)(2,1)S(1)} %pad_maximum_fusion.1.refs_0_), channel_id=1, source_target_pairs={{0,6},{2,4},{4,2},{6,0},{10,8},{12,14},{14,12},{8,10},{1,7},{3,5},... | collective-permute-start | bytes 884744 | tf_op jit(solution)/shard_map/ppermute | solution.py:104
  29.7 8.8 %collective-permute-start.5 = (bf16[2,64,768]{2,1,0:T(8,128)(2,1)S(1)}, bf16[2,64,768]{2,1,0:T(8,128)(2,1)S(1)}, u32[]{:S(2)}, u32[]{:S(2)}) collective-permute-start(bf16[2,64,768]{2,1,0:T(8,128)(2,1)S(1)} %fusion), channel_id=1, source_target_pairs={{0,6},{2,4},{4,2},{6,0},{10,8},{12,14},{14,12},{8,10},{1,7},{3,5},... | collective-permute-start | bytes 589832 | tf_op jit(solution)/shard_map/ppermute | solution.py:104
  34.5 7.7 %collective-permute-start.6 = (bf16[2,64,384]{2,1,0:T(8,128)(2,1)S(1)}, bf16[2,64,384]{2,1,0:T(8,128)(2,1)S(1)}, u32[]{:S(2)}, u32[]{:S(2)}) collective-permute-start(bf16[2,64,384]{2,1,0:T(8,128)(2,1)S(1)} %fusion.1), channel_id=1, source_target_pairs={{0,6},{2,4},{4,2},{6,0},{10,8},{12,14},{14,12},{8,10},{1,7},{3,5},... | collective-permute-start | bytes 294920 | tf_op jit(solution)/shard_map/ppermute | solution.py:104
  39.0 7.3 %copy-start = (bf16[1024,1024]{1,0:T(8,128)(2,1)S(1)}, bf16[1024,1024]{1,0:T(8,128)(2,1)}, u32[]{:S(2)}) copy-start(bf16[1024,1024]{1,0:T(8,128)(2,1)} %param.8) | copy-start | bytes 6291460
  39.1 7.3 %copy-start.2 = (bf16[1024,128]{1,0:T(8,128)(2,1)S(1)}, bf16[1024,128]{1,0:T(8,128)(2,1)}, u32[]{:S(2)}) copy-start(bf16[1024,128]{1,0:T(8,128)(2,1)} %param.9) | copy-start | bytes 786436
  42.3 13.9 %collective-permute-start.10 = (bf16[4,128,768]{2,1,0:T(8,128)(2,1)S(1)}, bf16[4,128,768]{2,1,0:T(8,128)(2,1)S(1)}, u32[]{:S(2)}, u32[]{:S(2)}) collective-permute-start(bf16[4,128,768]{2,1,0:T(8,128)(2,1)S(1)} %shard_map.80), channel_id=1, source_target_pairs={{0,64},{72,136},{64,0},{136,72},{128,192},{200,264},{192,128},{264... | collective-permute-start | bytes 2359304 | tf_op jit(solution)/shard_map/ppermute | solution.py:317
  48.0 5.4 %collective-permute-start.7 = (bf16[4,512,128]{2,1,0:T(8,128)(2,1)S(1)}, bf16[4,512,128]{2,1,0:T(8,128)(2,1)S(1)}, u32[]{:S(2)}, u32[]{:S(2)}) collective-permute-start(bf16[4,512,128]{2,1,0:T(8,128)(2,1)S(1)} %shard_map.82), channel_id=1, source_target_pairs={{0,8},{8,0},{1,9},{9,1},{2,10},{10,2},{3,11},{11,3},{4,12},{12,4},... | collective-permute-start | bytes 1572872 | tf_op jit(solution)/shard_map/ppermute | solution.py:326
  51.0 11.7 %collective-permute-start.12 = (bf16[4,128,384]{2,1,0:T(8,128)(2,1)S(1)}, bf16[4,128,384]{2,1,0:T(8,128)(2,1)S(1)}, u32[]{:S(2)}, u32[]{:S(2)}) collective-permute-start(bf16[4,128,384]{2,1,0:T(8,128)(2,1)S(1)} %shard_map.86), channel_id=1, source_target_pairs={{0,64},{72,136},{64,0},{136,72},{128,192},{200,264},{192,128},{264... | collective-permute-start | bytes 1179656 | tf_op jit(solution)/shard_map/ppermute | solution.py:317
  57.3 15.2 %collective-permute-start.11 = (bf16[2,128,768]{2,1,0:T(8,128)(2,1)S(1)}, bf16[2,128,768]{2,1,0:T(8,128)(2,1)S(1)}, u32[]{:S(2)}, u32[]{:S(2)}) collective-permute-start(bf16[2,128,768]{2,1,0:T(8,128)(2,1)S(1)} %get-tuple-element.37), channel_id=1, source_target_pairs={{0,448},{72,8},{64,128},{136,200},{128,64},{200,136},{192,256},{26... | collective-permute-start | bytes 1179656 | tf_op jit(solution)/shard_map/ppermute | solution.py:317
  63.8 8.8 %collective-permute-start.13 = (bf16[2,128,384]{2,1,0:T(8,128)(2,1)S(1)}, bf16[2,128,384]{2,1,0:T(8,128)(2,1)S(1)}, u32[]{:S(2)}, u32[]{:S(2)}) collective-permute-start(bf16[2,128,384]{2,1,0:T(8,128)(2,1)S(1)} %get-tuple-element.40), channel_id=1, source_target_pairs={{0,448},{72,8},{64,128},{136,200},{128,64},{200,136},{192,256},{26... | collective-permute-start | bytes 589832 | tf_op jit(solution)/shard_map/ppermute | solution.py:317
  66.9 10.7 %collective-permute-start.8 = (bf16[2,512,128]{2,1,0:T(8,128)(2,1)S(1)}, bf16[2,512,128]{2,1,0:T(8,128)(2,1)S(1)}, u32[]{:S(2)}, u32[]{:S(2)}) collective-permute-start(bf16[2,512,128]{2,1,0:T(8,128)(2,1)S(1)} %get-tuple-element.30), channel_id=1, source_target_pairs={{0,16},{16,0},{32,48},{48,32},{1,17},{17,1},{33,49},{49,33},{2,18}... | collective-permute-start | bytes 786440 | tf_op jit(solution)/shard_map/ppermute | solution.py:328
  72.7 15.2 %collective-permute-start.14 = (bf16[128,1152]{1,0:T(8,128)(2,1)S(1)}, bf16[128,1152]{1,0:T(8,128)(2,1)S(1)}, u32[]{:S(2)}, u32[]{:S(2)}) collective-permute-start(bf16[128,1152]{1,0:T(8,128)(2,1)S(1)} %get-tuple-element.42), channel_id=1, source_target_pairs={{0,192},{72,264},{64,384},{136,456},{128,320},{200,392},{192,0},{2... | collective-permute-start | bytes 884744 | tf_op jit(solution)/shard_map/ppermute | solution.py:317
  77.6 7.8 %collective-permute-start.9 = (bf16[512,128]{1,0:T(8,128)(2,1)S(1)}, bf16[512,128]{1,0:T(8,128)(2,1)S(1)}, u32[]{:S(2)}, u32[]{:S(2)}) collective-permute-start(bf16[512,128]{1,0:T(8,128)(2,1)S(1)} %get-tuple-element.32), channel_id=1, source_target_pairs={{0,32},{16,48},{32,0},{48,16},{1,33},{17,49},{33,1},{49,17},{2,34}... | collective-permute-start | bytes 393224 | tf_op jit(solution)/shard_map/ppermute | solution.py:340

commit v10 on v8

--- a/solution.py
+++ b/solution.py
@@ -133,14 +133,21 @@
     return lax.dot_general(left, right, ((dims[:1], dims[1:]), ((), ())), preferred_element_type=jnp.float32)
 
 
+def joined(blocks, x_ref):
+    return jnp.concatenate(
+        [x_ref[:, pl.ds(pl.multiple_of(blocks[r] * 128, 128), 128)] for r in range(N_PAIRS)], axis=1
+    )
+
+
 def give_body(blocks, x_ref, g_ref, *outs):
-    for r in range(N_PAIRS):
-        columns = x_ref[:, pl.ds(pl.multiple_of(blocks[r] * 128, 128), 128)]
-        at = 0
-        for out in outs:
-            width = out.shape[-1]
-            out[r] = dot(columns, g_ref[:, at : at + width], (0, 0)).astype(out.dtype)
-            at += width
+    columns = joined(blocks, x_ref)
+    at = 0
+    for out in outs:
+        width = out.shape[-1]
+        term = dot(columns, g_ref[:, at : at + width], (0, 0))
+        for r in range(N_PAIRS):
+            out[r] = term[r * 128 : (r + 1) * 128].astype(out.dtype)
+        at += width
 
 
 def give_terms(blocks, x, g):
@@ -156,11 +163,11 @@
 
 def keep_body(at, blocks, x_ref, g_ref, got_ref, give_ref, keep_ref):
     width = got_ref.shape[-1]
+    term = dot(joined(blocks, x_ref), g_ref[:, at : at + width], (0, 0))
     for r in range(N_PAIRS):
-        columns = x_ref[:, pl.ds(pl.multiple_of(blocks[r] * 128, 128), 128)]
-        term = dot(columns, g_ref[:, at : at + width], (0, 0)) + got_ref[r].astype(jnp.float32)
+        total = term[r * 128 : (r + 1) * 128] + got_ref[r].astype(jnp.float32)
         out = give_ref if r < 2 else keep_ref
-        out[r % 2] = term.astype(out.dtype)
+        out[r % 2] = total.astype(out.dtype)
 
 
 def keep_terms(blocks, x, g, got, at):

time: 89 us -> 89 us (level)
  no operation moved by 1% of the time
where the time goes in v10:
time: 89 us; the launch traced here: 87.7 us
  starting transfers between devices  61.3 us (69%)
  waiting for transfers between devices  14.7 us (17%)
  Pallas kernels  8.81 us (10%)
  local copies, waits for them, and re-layouts  1.41 us (2%)
  between operations  1.21 us (1%)
    ppermute x5, starting transfers between devices, along_y(): return lax.ppermute(terms, (*TOK, 'core'), pairs)  20.2 us
    ppermute x4, starting transfers between devices, x_swap(): return lax.ppermute(rows, ('core', 'x'), pairs)  13.8 us
    ppermute x1, starting transfers between devices, local(): far = lax.ppermute(mine, 'zhi', SWAP)  11 us
    ppermute x1, starting transfers between devices, local(): input_got = lax.ppermute(give, 'zlo', [(i, i ^ 1) for i in range(4)])  7.31 us
    ppermute x4, waiting for transfers between devices, x_swap(): return lax.ppermute(rows, ('core', 'x'), pairs)  5.83 us
    ppermute x1, starting transfers between devices, local(): input_got = lax.ppermute(give, 'zlo', [(i, i ^ 2) for i in range(4)])  5.08 us
    ppermute x5, waiting for transfers between devices, along_y(): return lax.ppermute(terms, (*TOK, 'core'), pairs)  4.21 us
    pallas_call x2, Pallas kernels, input_terms(): pl.pallas_call(input_body, grid_spec=pltpu.PrefetchScalarGridSpec(num_sca...  3.31 us
  transfers between devices with their start and end apart: 14, of which 8 were waited for; matrix products, arithmetic and copies ran while one was open for 0% of the time, Pallas kernels for 7%

profile of v10, /device:TPU:6, one launch (start us, length us, event | category | flops | bytes accessed | tf_op | source)
XLA Modules:
  0.0 87.7 jit_solution(16064080938220409027)
XLA Ops:
  0.6 1.9 %collective-permute-start = (bf16[64,256]{1,0:T(8,128)(2,1)}, bf16[64,256]{1,0:T(8,128)(2,1)S(1)}, u32[]{:S(2)}, u32[]{:S(2)}) collective-permute-start(bf16[64,256]{1,0:T(8,128)(2,1)} %share_hbm.1), channel_id=1, source_target_pairs={{0,8},{8,0},{1,9},{9,1},{2,10},{10,2},{3,11},{11,3},{4,12},{12,4},... | collective-permute-start | bytes 98312 | tf_op jit(solution)/shard_map/ppermute | solution.py:292
  2.6 0.1 stack.86
  2.7 0.9 %copy-done.4 = bf16[64,1024]{1,0:T(8,128)(2,1)S(1)} copy-done((bf16[64,1024]{1,0:T(8,128)(2,1)S(1)}, bf16[64,1024]{1,0:T(8,128)(2,1)}, u32[]{:S(2)}) %copy-start.4) | copy-done | bytes 131096
  3.6 0.1 broadcast_add_fusion
  3.7 0.3 collective-permute-done.more_ref
  3.9 0.4 copy-done.3
  4.4 0.1 shard_map.77.rows_ref
  4.5 0.0 copy-start.1
  4.5 11.0 %collective-permute-start.1 = (bf16[64,1152]{1,0:T(8,128)(2,1)S(1)}, bf16[64,1152]{1,0:T(8,128)(2,1)S(1)}, u32[]{:S(2)}, u32[]{:S(2)}) collective-permute-start(bf16[64,1152]{1,0:T(8,128)(2,1)S(1)} %shard_map.77.rows_ref), channel_id=1, source_target_pairs={{0,1},{1,0},{2,3},{3,2},{4,5},{5,4},{6,7},{7,6},{8,9},{9,8},{10,11... | collective-permute-start | bytes 442376 | tf_op jit(solution)/shard_map/ppermute | solution.py:294
  15.5 2.7 %collective-permute-start.2 = (bf16[64,1152]{1,0:T(8,128)(2,1)S(1)}, bf16[64,1152]{1,0:T(8,128)(2,1)S(1)}, u32[]{:S(2)}, u32[]{:S(2)}) collective-permute-start(bf16[64,1152]{1,0:T(8,128)(2,1)S(1)} %shard_map.78), channel_id=1, source_target_pairs={{0,2},{2,0},{4,6},{6,4},{10,12},{12,10},{14,8},{8,14},{1,3},{3,1},... | collective-permute-start | bytes 442376 | tf_op jit(solution)/shard_map/ppermute | solution.py:104
  18.5 0.1 and_select_fusion
  18.6 1.5 %collective-permute-done.1 = bf16[64,1152]{1,0:T(8,128)(2,1)S(1)} collective-permute-done((bf16[64,1152]{1,0:T(8,128)(2,1)S(1)}, bf16[64,1152]{1,0:T(8,128)(2,1)S(1)}, u32[]{:S(2)}, u32[]{:S(2)}) %collective-permute-start.1) | collective-permute-done | bytes 147488 | tf_op jit(solution)/shard_map/ppermute | solution.py:294
  20.1 2.7 %collective-permute-start.4 = (bf16[64,1152]{1,0:T(8,128)(2,1)S(1)}, bf16[64,1152]{1,0:T(8,128)(2,1)S(1)}, u32[]{:S(2)}, u32[]{:S(2)}) collective-permute-start(bf16[64,1152]{1,0:T(8,128)(2,1)S(1)} %collective-permute-done.1), channel_id=1, source_target_pairs={{0,2},{2,0},{4,6},{6,4},{10,12},{12,10},{14,8},{8,14},{1,3},{3,1},... | collective-permute-start | bytes 442376 | tf_op jit(solution)/shard_map/ppermute | solution.py:104
  22.9 0.0 collective-permute-done.2
  22.9 3.6 %collective-permute-start.3 = (bf16[2,64,1152]{2,1,0:T(8,128)(2,1)S(1)}, bf16[2,64,1152]{2,1,0:T(8,128)(2,1)S(1)}, u32[]{:S(2)}, u32[]{:S(2)}) collective-permute-start(bf16[2,64,1152]{2,1,0:T(8,128)(2,1)S(1)} %pad_maximum_fusion.refs_0_), channel_id=1, source_target_pairs={{0,6},{2,4},{4,2},{6,0},{10,8},{12,14},{14,12},{8,10},{1,7},{3,5},... | collective-permute-start | bytes 884744 | tf_op jit(solution)/shard_map/ppermute | solution.py:104
  26.5 0.7 collective-permute-done.4
  27.2 0.0 copy-start
  27.2 0.0 copy-start.2
  27.2 4.8 %collective-permute-start.5 = (bf16[2,64,1152]{2,1,0:T(8,128)(2,1)S(1)}, bf16[2,64,1152]{2,1,0:T(8,128)(2,1)S(1)}, u32[]{:S(2)}, u32[]{:S(2)}) collective-permute-start(bf16[2,64,1152]{2,1,0:T(8,128)(2,1)S(1)} %pad_maximum_fusion.1.refs_2_), channel_id=1, source_target_pairs={{0,6},{2,4},{4,2},{6,0},{10,8},{12,14},{14,12},{8,10},{1,7},{3,5},... | collective-permute-start | bytes 884744 | tf_op jit(solution)/shard_map/ppermute | solution.py:104
  32.0 0.7 collective-permute-done.3.refs_1_
  32.7 4.4 %collective-permute-done.5.refs_3_ = bf16[2,64,1152]{2,1,0:T(8,128)(2,1)S(1)} collective-permute-done((bf16[2,64,1152]{2,1,0:T(8,128)(2,1)S(1)}, bf16[2,64,1152]{2,1,0:T(8,128)(2,1)S(1)}, u32[]{:S(2)}, u32[]{:S(2)}) %collective-permute-start.5) | collective-permute-done | bytes 294944 | tf_op jit(solution)/shard_map/ppermute | solution.py:104
  37.2 0.6 shard_map.79
  37.8 0.0 copy-done.1
  37.8 1.4 %shard_map.80 = (bf16[4,128,768]{2,1,0:T(8,128)(2,1)S(1)}, bf16[4,128,384]{2,1,0:T(8,128)(2,1)S(1)}) custom-call(s32[4]{0:T(128)S(1)} %get-tuple-element.26.blocks, bf16[512,1024]{1,0:T(8,128)(2,1)S(1)} %copy-done.1, bf16[512,1152]{1,0:T(8,128)(2,1)S(1)} %bitcast.25), custom_call_target="tpu_custom_call" | custom-call | flops 1 | bytes 1 | tf_op jit(solution)/shard_map/pallas_call | solution.py:154
  39.3 3.5 %collective-permute-start.9 = (bf16[4,128,768]{2,1,0:T(8,128)(2,1)S(1)}, bf16[4,128,768]{2,1,0:T(8,128)(2,1)S(1)}, u32[]{:S(2)}, u32[]{:S(2)}) collective-permute-start(bf16[4,128,768]{2,1,0:T(8,128)(2,1)S(1)} %get-tuple-element.37), channel_id=1, source_target_pairs={{0,64},{72,136},{64,0},{136,72},{128,192},{200,264},{192,128},{264... | collective-permute-start | bytes 2359304 | tf_op jit(solution)/shard_map/ppermute | solution.py:315
  42.8 0.0 copy-done
  42.8 1.6 %shard_map.81 = bf16[4,512,128]{2,1,0:T(8,128)(2,1)S(1)} custom-call(s32[4]{0:T(128)S(1)} %add_subtract_fusion.blocks, bf16[512,1152]{1,0:T(8,128)(2,1)S(1)} %bitcast.26, bf16[8,128,1024]{2,1,0:T(8,128)(2,1)S(1)} %bitcast.30, bf16[8,128,1024]{2,1,0:T(8,128)(2,1)S(1)} %bitcast.31, bf16[8,128,128]{2,1,0:T(8,128)(2,1)S(1)} %bitcast.34, ...), custom_call_target="tpu_custom_call" | custom-call | flops 1 | bytes 1 | tf_op jit(solution)/shard_map/pallas_call | solution.py:265
  44.4 1.9 %collective-permute-start.6 = (bf16[4,512,128]{2,1,0:T(8,128)(2,1)S(1)}, bf16[4,512,128]{2,1,0:T(8,128)(2,1)S(1)}, u32[]{:S(2)}, u32[]{:S(2)}) collective-permute-start(bf16[4,512,128]{2,1,0:T(8,128)(2,1)S(1)} %shard_map.81), channel_id=1, source_target_pairs={{0,8},{8,0},{1,9},{9,1},{2,10},{10,2},{3,11},{11,3},{4,12},{12,4},... | collective-permute-start | bytes 1572872 | tf_op jit(solution)/shard_map/ppermute | solution.py:321
  46.3 2.4 %collective-permute-start.11 = (bf16[4,128,384]{2,1,0:T(8,128)(2,1)S(1)}, bf16[4,128,384]{2,1,0:T(8,128)(2,1)S(1)}, u32[]{:S(2)}, u32[]{:S(2)}) collective-permute-start(bf16[4,128,384]{2,1,0:T(8,128)(2,1)S(1)} %get-tuple-element.41), channel_id=1, source_target_pairs={{0,64},{72,136},{64,0},{136,72},{128,192},{200,264},{192,128},{264... | collective-permute-start | bytes 1179656 | tf_op jit(solution)/shard_map/ppermute | solution.py:315
  48.7 0.0 collective-permute-done.6.refs_0_
  48.7 1.7 %shard_map.82 = (bf16[2,512,128]{2,1,0:T(8,128)(2,1)S(1)}, bf16[2,512,128]{2,1,0:T(8,128)(2,1)S(1)}) custom-call(s32[4]{0:T(128)S(1)} %get-tuple-element.25.blocks, bf16[512,1152]{1,0:T(8,128)(2,1)S(1)} %bitcast.27, bf16[8,128,1024]{2,1,0:T(8,128)(2,1)S(1)} %bitcast.32, bf16[8,128,1024]{2,1,0:T(8,128)(2,1)S(1)} %bitcast.33, ...), custom_call_target="tpu_custom_call" | custom-call | flops 1 | bytes 1 | tf_op jit(solution)/shard_map/pallas_call | solution.py:265
  50.4 2.7 %collective-permute-done.9.got_ref = bf16[4,128,768]{2,1,0:T(8,128)(2,1)S(1)} collective-permute-done((bf16[4,128,768]{2,1,0:T(8,128)(2,1)S(1)}, bf16[4,128,768]{2,1,0:T(8,128)(2,1)S(1)}, u32[]{:S(2)}, u32[]{:S(2)}) %collective-permute-start.9) | collective-permute-done | bytes 786464 | tf_op jit(solution)/shard_map/ppermute | solution.py:315
  53.2 1.2 %shard_map.84 = (bf16[2,128,768]{2,1,0:T(8,128)(2,1)S(1)}, bf16[2,128,768]{2,1,0:T(8,128)(2,1)S(1)}) custom-call(s32[4]{0:T(128)S(1)} %get-tuple-element.36.blocks, bf16[512,1024]{1,0:T(8,128)(2,1)S(1)} %copy-done.1, bf16[512,1152]{1,0:T(8,128)(2,1)S(1)} %bitcast.28, bf16[4,128,768]{2,1,0:T(8,128)(2,1)S(1)} %collective-permute-done.9.got_ref), custom_call_target="tpu_custom_call" | custom-call | flops 1 | bytes 1 | tf_op jit(solution)/shard_map/pallas_call | solution.py:174
  54.3 5.4 %collective-permute-start.10 = (bf16[2,128,768]{2,1,0:T(8,128)(2,1)S(1)}, bf16[2,128,768]{2,1,0:T(8,128)(2,1)S(1)}, u32[]{:S(2)}, u32[]{:S(2)}) collective-permute-start(bf16[2,128,768]{2,1,0:T(8,128)(2,1)S(1)} %get-tuple-element.40), channel_id=1, source_target_pairs={{0,448},{72,8},{64,128},{136,200},{128,64},{200,136},{192,256},{26... | collective-permute-start | bytes 1179656 | tf_op jit(solution)/shard_map/ppermute | solution.py:315
  59.7 0.0 collective-permute-done.11.got_ref
  59.7 1.0 %shard_map.85 = (bf16[2,128,384]{2,1,0:T(8,128)(2,1)S(1)}, bf16[2,128,384]{2,1,0:T(8,128)(2,1)S(1)}) custom-call(s32[4]{0:T(128)S(1)} %get-tuple-element.36.blocks, bf16[512,1024]{1,0:T(8,128)(2,1)S(1)} %copy-done.1, bf16[512,1152]{1,0:T(8,128)(2,1)S(1)} %bitcast.29, bf16[4,128,384]{2,1,0:T(8,128)(2,1)S(1)} %collective-permute-done.11.got_ref), custom_call_target="tpu_custom_call" | custom-call | flops 1 | bytes 1 | tf_op jit(solution)/shard_map/pallas_call | solution.py:174
  60.8 3.6 %collective-permute-start.12 = (bf16[2,128,384]{2,1,0:T(8,128)(2,1)S(1)}, bf16[2,128,384]{2,1,0:T(8,128)(2,1)S(1)}, u32[]{:S(2)}, u32[]{:S(2)}) collective-permute-start(bf16[2,128,384]{2,1,0:T(8,128)(2,1)S(1)} %get-tuple-element.44), channel_id=1, source_target_pairs={{0,448},{72,8},{64,128},{136,200},{128,64},{200,136},{192,256},{26... | collective-permute-start | bytes 589832 | tf_op jit(solution)/shard_map/ppermute | solution.py:315
  64.4 7.3 %collective-permute-start.7 = (bf16[2,512,128]{2,1,0:T(8,128)(2,1)S(1)}, bf16[2,512,128]{2,1,0:T(8,128)(2,1)S(1)}, u32[]{:S(2)}, u32[]{:S(2)}) collective-permute-start(bf16[2,512,128]{2,1,0:T(8,128)(2,1)S(1)} %get-tuple-element.33), channel_id=1, source_target_pairs={{0,16},{16,0},{32,48},{48,32},{1,17},{17,1},{33,49},{49,33},{2,18}... | collective-permute-start | bytes 786440 | tf_op jit(solution)/shard_map/ppermute | solution.py:323
  71.7 0.0 collective-permute-done.12.refs_3_
  71.7 0.0 collective-permute-done.10.refs_1_
  71.7 0.1 shard_map.86
  71.8 5.4 %collective-permute-start.13 = (bf16[128,1152]{1,0:T(8,128)(2,1)S(1)}, bf16[128,1152]{1,0:T(8,128)(2,1)S(1)}, u32[]{:S(2)}, u32[]{:S(2)}) collective-permute-start(bf16[128,1152]{1,0:T(8,128)(2,1)S(1)} %get-tuple-element.46), channel_id=1, source_target_pairs={{0,192},{72,264},{64,384},{136,456},{128,320},{200,392},{192,0},{2... | collective-permute-start | bytes 884744 | tf_op jit(solution)/shard_map/ppermute | solution.py:315
  77.2 0.0 collective-permute-done.7.refs_1_
  77.2 0.1 shard_map.83
  77.3 5.1 %collective-permute-start.8 = (bf16[512,128]{1,0:T(8,128)(2,1)S(1)}, bf16[512,128]{1,0:T(8,128)(2,1)S(1)}, u32[]{:S(2)}, u32[]{:S(2)}) collective-permute-start(bf16[512,128]{1,0:T(8,128)(2,1)S(1)} %get-tuple-element.35), channel_id=1, source_target_pairs={{0,32},{16,48},{32,0},{48,16},{1,33},{17,49},{33,1},{49,17},{2,34}... | collective-permute-start | bytes 393224 | tf_op jit(solution)/shard_map/ppermute | solution.py:337
  82.4 2.9 %collective-permute-done.8.input_got = bf16[512,128]{1,0:T(8,128)(2,1)S(1)} collective-permute-done((bf16[512,128]{1,0:T(8,128)(2,1)S(1)}, bf16[512,128]{1,0:T(8,128)(2,1)S(1)}, u32[]{:S(2)}, u32[]{:S(2)}) %collective-permute-start.8) | collective-permute-done | bytes 131104 | tf_op jit(solution)/shard_map/ppermute | solution.py:337
  85.3 1.5 %collective-permute-done.13.got = bf16[128,1152]{1,0:T(8,128)(2,1)S(1)} collective-permute-done((bf16[128,1152]{1,0:T(8,128)(2,1)S(1)}, bf16[128,1152]{1,0:T(8,128)(2,1)S(1)}, u32[]{:S(2)}, u32[]{:S(2)}) %collective-permute-start.13) | collective-permute-done | bytes 294944 | tf_op jit(solution)/shard_map/ppermute | solution.py:315
  86.8 0.9 %shard_map.87 = (bf16[512,128]{1,0:T(8,128)(2,1)}, f32[128,1024]{1,0:T(8,128)}, f32[128,128]{1,0:T(8,128)}) custom-call(bf16[512,128]{1,0:T(8,128)(2,1)S(1)} %get-tuple-element.34.input_kept, bf16[512,128]{1,0:T(8,128)(2,1)S(1)} %collective-permute-done.8.input_got, bf16[128,1152]{1,0:T(8,128)(2,1)S(1)} %get-tuple-element.45.kept, ...), custom_call_target="tpu_custom_call" | custom-call | flops 1 | bytes 1 | tf_op jit(solution)/shard_map/pallas_call | solution.py:224
  (9 shorter events, 0.1 us)
Async XLA Ops:
  0.6 3.3 %collective-permute-start = (bf16[64,256]{1,0:T(8,128)(2,1)}, bf16[64,256]{1,0:T(8,128)(2,1)S(1)}, u32[]{:S(2)}, u32[]{:S(2)}) collective-permute-start(bf16[64,256]{1,0:T(8,128)(2,1)} %share_hbm.1), channel_id=1, source_target_pairs={{0,8},{8,0},{1,9},{9,1},{2,10},{10,2},{3,11},{11,3},{4,12},{12,4},... | collective-permute-start | bytes 98312 | tf_op jit(solution)/shard_map/ppermute | solution.py:292
  2.7 0.9 %copy-start.4 = (bf16[64,1024]{1,0:T(8,128)(2,1)S(1)}, bf16[64,1024]{1,0:T(8,128)(2,1)}, u32[]{:S(2)}) copy-start(bf16[64,1024]{1,0:T(8,128)(2,1)} %rows_ref.1) | copy-start | bytes 393220
  3.6 0.8 copy-start.3
  4.5 33.3 %copy-start.1 = (bf16[512,1024]{1,0:T(8,128)(2,1)S(1)}, bf16[512,1024]{1,0:T(8,128)(2,1)}, u32[]{:S(2)}) copy-start(bf16[512,1024]{1,0:T(8,128)(2,1)} %x_ref.5) | copy-start | bytes 3145732
  4.5 15.6 %collective-permute-start.1 = (bf16[64,1152]{1,0:T(8,128)(2,1)S(1)}, bf16[64,1152]{1,0:T(8,128)(2,1)S(1)}, u32[]{:S(2)}, u32[]{:S(2)}) collective-permute-start(bf16[64,1152]{1,0:T(8,128)(2,1)S(1)} %shard_map.77.rows_ref), channel_id=1, source_target_pairs={{0,1},{1,0},{2,3},{3,2},{4,5},{5,4},{6,7},{7,6},{8,9},{9,8},{10,11... | collective-permute-start | bytes 442376 | tf_op jit(solution)/shard_map/ppermute | solution.py:294
  15.5 7.3 %collective-permute-start.2 = (bf16[64,1152]{1,0:T(8,128)(2,1)S(1)}, bf16[64,1152]{1,0:T(8,128)(2,1)S(1)}, u32[]{:S(2)}, u32[]{:S(2)}) collective-permute-start(bf16[64,1152]{1,0:T(8,128)(2,1)S(1)} %shard_map.78), channel_id=1, source_target_pairs={{0,2},{2,0},{4,6},{6,4},{10,12},{12,10},{14,8},{8,14},{1,3},{3,1},... | collective-permute-start | bytes 442376 | tf_op jit(solution)/shard_map/ppermute | solution.py:104
  20.1 7.0 %collective-permute-start.4 = (bf16[64,1152]{1,0:T(8,128)(2,1)S(1)}, bf16[64,1152]{1,0:T(8,128)(2,1)S(1)}, u32[]{:S(2)}, u32[]{:S(2)}) collective-permute-start(bf16[64,1152]{1,0:T(8,128)(2,1)S(1)} %collective-permute-done.1), channel_id=1, source_target_pairs={{0,2},{2,0},{4,6},{6,4},{10,12},{12,10},{14,8},{8,14},{1,3},{3,1},... | collective-permute-start | bytes 442376 | tf_op jit(solution)/shard_map/ppermute | solution.py:104
  22.9 9.8 %collective-permute-start.3 = (bf16[2,64,1152]{2,1,0:T(8,128)(2,1)S(1)}, bf16[2,64,1152]{2,1,0:T(8,128)(2,1)S(1)}, u32[]{:S(2)}, u32[]{:S(2)}) collective-permute-start(bf16[2,64,1152]{2,1,0:T(8,128)(2,1)S(1)} %pad_maximum_fusion.refs_0_), channel_id=1, source_target_pairs={{0,6},{2,4},{4,2},{6,0},{10,8},{12,14},{14,12},{8,10},{1,7},{3,5},... | collective-permute-start | bytes 884744 | tf_op jit(solution)/shard_map/ppermute | solution.py:104
  27.2 15.6 %copy-start = (bf16[1024,1024]{1,0:T(8,128)(2,1)S(1)}, bf16[1024,1024]{1,0:T(8,128)(2,1)}, u32[]{:S(2)}) copy-start(bf16[1024,1024]{1,0:T(8,128)(2,1)} %param.8) | copy-start | bytes 6291460
  27.2 15.6 %copy-start.2 = (bf16[1024,128]{1,0:T(8,128)(2,1)S(1)}, bf16[1024,128]{1,0:T(8,128)(2,1)}, u32[]{:S(2)}) copy-start(bf16[1024,128]{1,0:T(8,128)(2,1)} %param.9) | copy-start | bytes 786436
  27.2 10.0 %collective-permute-start.5 = (bf16[2,64,1152]{2,1,0:T(8,128)(2,1)S(1)}, bf16[2,64,1152]{2,1,0:T(8,128)(2,1)S(1)}, u32[]{:S(2)}, u32[]{:S(2)}) collective-permute-start(bf16[2,64,1152]{2,1,0:T(8,128)(2,1)S(1)} %pad_maximum_fusion.1.refs_2_), channel_id=1, source_target_pairs={{0,6},{2,4},{4,2},{6,0},{10,8},{12,14},{14,12},{8,10},{1,7},{3,5},... | collective-permute-start | bytes 884744 | tf_op jit(solution)/shard_map/ppermute | solution.py:104
  39.3 13.9 %collective-permute-start.9 = (bf16[4,128,768]{2,1,0:T(8,128)(2,1)S(1)}, bf16[4,128,768]{2,1,0:T(8,128)(2,1)S(1)}, u32[]{:S(2)}, u32[]{:S(2)}) collective-permute-start(bf16[4,128,768]{2,1,0:T(8,128)(2,1)S(1)} %get-tuple-element.37), channel_id=1, source_target_pairs={{0,64},{72,136},{64,0},{136,72},{128,192},{200,264},{192,128},{264... | collective-permute-start | bytes 2359304 | tf_op jit(solution)/shard_map/ppermute | solution.py:315
  44.4 4.3 %collective-permute-start.6 = (bf16[4,512,128]{2,1,0:T(8,128)(2,1)S(1)}, bf16[4,512,128]{2,1,0:T(8,128)(2,1)S(1)}, u32[]{:S(2)}, u32[]{:S(2)}) collective-permute-start(bf16[4,512,128]{2,1,0:T(8,128)(2,1)S(1)} %shard_map.81), channel_id=1, source_target_pairs={{0,8},{8,0},{1,9},{9,1},{2,10},{10,2},{3,11},{11,3},{4,12},{12,4},... | collective-permute-start | bytes 1572872 | tf_op jit(solution)/shard_map/ppermute | solution.py:321
  46.3 13.4 %collective-permute-start.11 = (bf16[4,128,384]{2,1,0:T(8,128)(2,1)S(1)}, bf16[4,128,384]{2,1,0:T(8,128)(2,1)S(1)}, u32[]{:S(2)}, u32[]{:S(2)}) collective-permute-start(bf16[4,128,384]{2,1,0:T(8,128)(2,1)S(1)} %get-tuple-element.41), channel_id=1, source_target_pairs={{0,64},{72,136},{64,0},{136,72},{128,192},{200,264},{192,128},{264... | collective-permute-start | bytes 1179656 | tf_op jit(solution)/shard_map/ppermute | solution.py:315
  54.3 17.3 %collective-permute-start.10 = (bf16[2,128,768]{2,1,0:T(8,128)(2,1)S(1)}, bf16[2,128,768]{2,1,0:T(8,128)(2,1)S(1)}, u32[]{:S(2)}, u32[]{:S(2)}) collective-permute-start(bf16[2,128,768]{2,1,0:T(8,128)(2,1)S(1)} %get-tuple-element.40), channel_id=1, source_target_pairs={{0,448},{72,8},{64,128},{136,200},{128,64},{200,136},{192,256},{26... | collective-permute-start | bytes 1179656 | tf_op jit(solution)/shard_map/ppermute | solution.py:315
  60.8 10.9 %collective-permute-start.12 = (bf16[2,128,384]{2,1,0:T(8,128)(2,1)S(1)}, bf16[2,128,384]{2,1,0:T(8,128)(2,1)S(1)}, u32[]{:S(2)}, u32[]{:S(2)}) collective-permute-start(bf16[2,128,384]{2,1,0:T(8,128)(2,1)S(1)} %get-tuple-element.44), channel_id=1, source_target_pairs={{0,448},{72,8},{64,128},{136,200},{128,64},{200,136},{192,256},{26... | collective-permute-start | bytes 589832 | tf_op jit(solution)/shard_map/ppermute | solution.py:315
  64.4 12.9 %collective-permute-start.7 = (bf16[2,512,128]{2,1,0:T(8,128)(2,1)S(1)}, bf16[2,512,128]{2,1,0:T(8,128)(2,1)S(1)}, u32[]{:S(2)}, u32[]{:S(2)}) collective-permute-start(bf16[2,512,128]{2,1,0:T(8,128)(2,1)S(1)} %get-tuple-element.33), channel_id=1, source_target_pairs={{0,16},{16,0},{32,48},{48,32},{1,17},{17,1},{33,49},{49,33},{2,18}... | collective-permute-start | bytes 786440 | tf_op jit(solution)/shard_map/ppermute | solution.py:323
  71.8 15.0 %collective-permute-start.13 = (bf16[128,1152]{1,0:T(8,128)(2,1)S(1)}, bf16[128,1152]{1,0:T(8,128)(2,1)S(1)}, u32[]{:S(2)}, u32[]{:S(2)}) collective-permute-start(bf16[128,1152]{1,0:T(8,128)(2,1)S(1)} %get-tuple-element.46), channel_id=1, source_target_pairs={{0,192},{72,264},{64,384},{136,456},{128,320},{200,392},{192,0},{2... | collective-permute-start | bytes 884744 | tf_op jit(solution)/shard_map/ppermute | solution.py:315
  77.3 8.0 %collective-permute-start.8 = (bf16[512,128]{1,0:T(8,128)(2,1)S(1)}, bf16[512,128]{1,0:T(8,128)(2,1)S(1)}, u32[]{:S(2)}, u32[]{:S(2)}) collective-permute-start(bf16[512,128]{1,0:T(8,128)(2,1)S(1)} %get-tuple-element.35), channel_id=1, source_target_pairs={{0,32},{16,48},{32,0},{48,16},{1,33},{17,49},{33,1},{49,17},{2,34}... | collective-permute-start | bytes 393224 | tf_op jit(solution)/shard_map/ppermute | solution.py:337

commit v11 on v10

--- a/solution.py
+++ b/solution.py
@@ -290,7 +290,7 @@
     y = lax.axis_index(TOK)
 
     more = lax.ppermute(key_value_share_gradient, "core", SWAP)
-    mine = own_rows(core.reshape(1), again(q_grad), key_value_share_gradient, more)
+    mine = own_rows(core.reshape(1), again(q_grad), again(key_value_share_gradient), more)
     far = lax.ppermute(mine, "zhi", SWAP)
 
     v = (y - core) % N_Y

time: 89 us -> 89 us (level)
  transfers between devices with their start and end apart: 14 -> 14, of which waited for: 8 -> 7; matrix products, arithmetic and copies ran while one was open for 0% -> 0% of each run, Pallas kernels for 7% -> 7%
where the time goes in v11:
time: 89 us; the launch traced here: 87.7 us
  starting transfers between devices  61.3 us (69%)
  waiting for transfers between devices  14.5 us (16%)
  Pallas kernels  8.82 us (10%)
  local copies, waits for them, and re-layouts  1.66 us (2%)
  between operations  1.22 us (1%)
    ppermute x5, starting transfers between devices, along_y(): return lax.ppermute(terms, (*TOK, 'core'), pairs)  20.2 us
    ppermute x4, starting transfers between devices, x_swap(): return lax.ppermute(rows, ('core', 'x'), pairs)  13.8 us
    ppermute x1, starting transfers between devices, local(): far = lax.ppermute(mine, 'zhi', SWAP)  11 us
    ppermute x1, starting transfers between devices, local(): input_got = lax.ppermute(give, 'zlo', [(i, i ^ 1) for i in range(4)])  7.3 us
    ppermute x4, waiting for transfers between devices, x_swap(): return lax.ppermute(rows, ('core', 'x'), pairs)  5.83 us
    ppermute x1, starting transfers between devices, local(): input_got = lax.ppermute(give, 'zlo', [(i, i ^ 2) for i in range(4)])  5.08 us
    ppermute x5, waiting for transfers between devices, along_y(): return lax.ppermute(terms, (*TOK, 'core'), pairs)  4.22 us
    pallas_call x2, Pallas kernels, input_terms(): pl.pallas_call(input_body, grid_spec=pltpu.PrefetchScalarGridSpec(num_sca...  3.32 us
  transfers between devices with their start and end apart: 14, of which 7 were waited for; matrix products, arithmetic and copies ran while one was open for 0% of the time, Pallas kernels for 7%

profile of v11, /device:TPU:6, one launch (start us, length us, event | category | flops | bytes accessed | tf_op | source)
XLA Modules:
  0.0 87.7 jit_solution(8910176951401661778)
XLA Ops:
  0.6 1.9 %collective-permute-start = (bf16[64,256]{1,0:T(8,128)(2,1)}, bf16[64,256]{1,0:T(8,128)(2,1)S(1)}, u32[]{:S(2)}, u32[]{:S(2)}) collective-permute-start(bf16[64,256]{1,0:T(8,128)(2,1)} %rows_ref.3), channel_id=1, source_target_pairs={{0,8},{8,0},{1,9},{9,1},{2,10},{10,2},{3,11},{11,3},{4,12},{12,4},... | collective-permute-start | bytes 98312 | tf_op jit(solution)/shard_map/ppermute | solution.py:292
  2.6 0.0 copy-start.4
  2.6 0.7 copy-done.4
  3.3 0.1 stack.86
  3.4 0.8 copy-done.3
  4.3 0.1 broadcast_add_fusion
  4.3 0.0 collective-permute-done.more_ref
  4.3 0.1 shard_map.78.rows_ref
  4.5 0.0 copy-start.1
  4.5 11.0 %collective-permute-start.1 = (bf16[64,1152]{1,0:T(8,128)(2,1)S(1)}, bf16[64,1152]{1,0:T(8,128)(2,1)S(1)}, u32[]{:S(2)}, u32[]{:S(2)}) collective-permute-start(bf16[64,1152]{1,0:T(8,128)(2,1)S(1)} %shard_map.78.rows_ref), channel_id=1, source_target_pairs={{0,1},{1,0},{2,3},{3,2},{4,5},{5,4},{6,7},{7,6},{8,9},{9,8},{10,11... | collective-permute-start | bytes 442376 | tf_op jit(solution)/shard_map/ppermute | solution.py:294
  15.5 2.7 %collective-permute-start.2 = (bf16[64,1152]{1,0:T(8,128)(2,1)S(1)}, bf16[64,1152]{1,0:T(8,128)(2,1)S(1)}, u32[]{:S(2)}, u32[]{:S(2)}) collective-permute-start(bf16[64,1152]{1,0:T(8,128)(2,1)S(1)} %shard_map.79), channel_id=1, source_target_pairs={{0,2},{2,0},{4,6},{6,4},{10,12},{12,10},{14,8},{8,14},{1,3},{3,1},... | collective-permute-start | bytes 442376 | tf_op jit(solution)/shard_map/ppermute | solution.py:104
  18.5 0.1 and_select_fusion
  18.6 1.5 %collective-permute-done.1 = bf16[64,1152]{1,0:T(8,128)(2,1)S(1)} collective-permute-done((bf16[64,1152]{1,0:T(8,128)(2,1)S(1)}, bf16[64,1152]{1,0:T(8,128)(2,1)S(1)}, u32[]{:S(2)}, u32[]{:S(2)}) %collective-permute-start.1) | collective-permute-done | bytes 147488 | tf_op jit(solution)/shard_map/ppermute | solution.py:294
  20.1 2.7 %collective-permute-start.4 = (bf16[64,1152]{1,0:T(8,128)(2,1)S(1)}, bf16[64,1152]{1,0:T(8,128)(2,1)S(1)}, u32[]{:S(2)}, u32[]{:S(2)}) collective-permute-start(bf16[64,1152]{1,0:T(8,128)(2,1)S(1)} %collective-permute-done.1), channel_id=1, source_target_pairs={{0,2},{2,0},{4,6},{6,4},{10,12},{12,10},{14,8},{8,14},{1,3},{3,1},... | collective-permute-start | bytes 442376 | tf_op jit(solution)/shard_map/ppermute | solution.py:104
  22.9 0.0 collective-permute-done.2
  22.9 3.6 %collective-permute-start.3 = (bf16[2,64,1152]{2,1,0:T(8,128)(2,1)S(1)}, bf16[2,64,1152]{2,1,0:T(8,128)(2,1)S(1)}, u32[]{:S(2)}, u32[]{:S(2)}) collective-permute-start(bf16[2,64,1152]{2,1,0:T(8,128)(2,1)S(1)} %pad_maximum_fusion.refs_0_), channel_id=1, source_target_pairs={{0,6},{2,4},{4,2},{6,0},{10,8},{12,14},{14,12},{8,10},{1,7},{3,5},... | collective-permute-start | bytes 884744 | tf_op jit(solution)/shard_map/ppermute | solution.py:104
  26.5 0.7 collective-permute-done.4
  27.2 0.0 copy-start
  27.2 0.0 copy-start.2
  27.2 4.8 %collective-permute-start.5 = (bf16[2,64,1152]{2,1,0:T(8,128)(2,1)S(1)}, bf16[2,64,1152]{2,1,0:T(8,128)(2,1)S(1)}, u32[]{:S(2)}, u32[]{:S(2)}) collective-permute-start(bf16[2,64,1152]{2,1,0:T(8,128)(2,1)S(1)} %pad_maximum_fusion.1.refs_2_), channel_id=1, source_target_pairs={{0,6},{2,4},{4,2},{6,0},{10,8},{12,14},{14,12},{8,10},{1,7},{3,5},... | collective-permute-start | bytes 884744 | tf_op jit(solution)/shard_map/ppermute | solution.py:104
  32.0 0.7 collective-permute-done.3.refs_1_
  32.7 4.4 %collective-permute-done.5.refs_3_ = bf16[2,64,1152]{2,1,0:T(8,128)(2,1)S(1)} collective-permute-done((bf16[2,64,1152]{2,1,0:T(8,128)(2,1)S(1)}, bf16[2,64,1152]{2,1,0:T(8,128)(2,1)S(1)}, u32[]{:S(2)}, u32[]{:S(2)}) %collective-permute-start.5) | collective-permute-done | bytes 294944 | tf_op jit(solution)/shard_map/ppermute | solution.py:104
  37.2 0.6 shard_map.80
  37.8 0.0 copy-done.1
  37.8 1.4 %shard_map.81 = (bf16[4,128,768]{2,1,0:T(8,128)(2,1)S(1)}, bf16[4,128,384]{2,1,0:T(8,128)(2,1)S(1)}) custom-call(s32[4]{0:T(128)S(1)} %get-tuple-element.26.blocks, bf16[512,1024]{1,0:T(8,128)(2,1)S(1)} %copy-done.1, bf16[512,1152]{1,0:T(8,128)(2,1)S(1)} %bitcast.25), custom_call_target="tpu_custom_call" | custom-call | flops 1 | bytes 1 | tf_op jit(solution)/shard_map/pallas_call | solution.py:154
  39.3 3.5 %collective-permute-start.9 = (bf16[4,128,768]{2,1,0:T(8,128)(2,1)S(1)}, bf16[4,128,768]{2,1,0:T(8,128)(2,1)S(1)}, u32[]{:S(2)}, u32[]{:S(2)}) collective-permute-start(bf16[4,128,768]{2,1,0:T(8,128)(2,1)S(1)} %get-tuple-element.37), channel_id=1, source_target_pairs={{0,64},{72,136},{64,0},{136,72},{128,192},{200,264},{192,128},{264... | collective-permute-start | bytes 2359304 | tf_op jit(solution)/shard_map/ppermute | solution.py:315
  42.8 1.6 %shard_map.82 = bf16[4,512,128]{2,1,0:T(8,128)(2,1)S(1)} custom-call(s32[4]{0:T(128)S(1)} %add_subtract_fusion.blocks, bf16[512,1152]{1,0:T(8,128)(2,1)S(1)} %bitcast.26, bf16[8,128,1024]{2,1,0:T(8,128)(2,1)S(1)} %bitcast.30, bf16[8,128,1024]{2,1,0:T(8,128)(2,1)S(1)} %bitcast.31, bf16[8,128,128]{2,1,0:T(8,128)(2,1)S(1)} %bitcast.34, ...), custom_call_target="tpu_custom_call" | custom-call | flops 1 | bytes 1 | tf_op jit(solution)/shard_map/pallas_call | solution.py:265
  44.4 1.9 %collective-permute-start.6 = (bf16[4,512,128]{2,1,0:T(8,128)(2,1)S(1)}, bf16[4,512,128]{2,1,0:T(8,128)(2,1)S(1)}, u32[]{:S(2)}, u32[]{:S(2)}) collective-permute-start(bf16[4,512,128]{2,1,0:T(8,128)(2,1)S(1)} %shard_map.82), channel_id=1, source_target_pairs={{0,8},{8,0},{1,9},{9,1},{2,10},{10,2},{3,11},{11,3},{4,12},{12,4},... | collective-permute-start | bytes 1572872 | tf_op jit(solution)/shard_map/ppermute | solution.py:321
  46.3 2.3 %collective-permute-start.11 = (bf16[4,128,384]{2,1,0:T(8,128)(2,1)S(1)}, bf16[4,128,384]{2,1,0:T(8,128)(2,1)S(1)}, u32[]{:S(2)}, u32[]{:S(2)}) collective-permute-start(bf16[4,128,384]{2,1,0:T(8,128)(2,1)S(1)} %get-tuple-element.41), channel_id=1, source_target_pairs={{0,64},{72,136},{64,0},{136,72},{128,192},{200,264},{192,128},{264... | collective-permute-start | bytes 1179656 | tf_op jit(solution)/shard_map/ppermute | solution.py:315
  48.7 0.0 collective-permute-done.6.refs_0_
  48.7 1.7 %shard_map.83 = (bf16[2,512,128]{2,1,0:T(8,128)(2,1)S(1)}, bf16[2,512,128]{2,1,0:T(8,128)(2,1)S(1)}) custom-call(s32[4]{0:T(128)S(1)} %get-tuple-element.25.blocks, bf16[512,1152]{1,0:T(8,128)(2,1)S(1)} %bitcast.27, bf16[8,128,1024]{2,1,0:T(8,128)(2,1)S(1)} %bitcast.32, bf16[8,128,1024]{2,1,0:T(8,128)(2,1)S(1)} %bitcast.33, ...), custom_call_target="tpu_custom_call" | custom-call | flops 1 | bytes 1 | tf_op jit(solution)/shard_map/pallas_call | solution.py:265
  50.4 2.7 %collective-permute-done.9.got_ref = bf16[4,128,768]{2,1,0:T(8,128)(2,1)S(1)} collective-permute-done((bf16[4,128,768]{2,1,0:T(8,128)(2,1)S(1)}, bf16[4,128,768]{2,1,0:T(8,128)(2,1)S(1)}, u32[]{:S(2)}, u32[]{:S(2)}) %collective-permute-start.9) | collective-permute-done | bytes 786464 | tf_op jit(solution)/shard_map/ppermute | solution.py:315
  53.2 1.2 %shard_map.85 = (bf16[2,128,768]{2,1,0:T(8,128)(2,1)S(1)}, bf16[2,128,768]{2,1,0:T(8,128)(2,1)S(1)}) custom-call(s32[4]{0:T(128)S(1)} %get-tuple-element.36.blocks, bf16[512,1024]{1,0:T(8,128)(2,1)S(1)} %copy-done.1, bf16[512,1152]{1,0:T(8,128)(2,1)S(1)} %bitcast.28, bf16[4,128,768]{2,1,0:T(8,128)(2,1)S(1)} %collective-permute-done.9.got_ref), custom_call_target="tpu_custom_call" | custom-call | flops 1 | bytes 1 | tf_op jit(solution)/shard_map/pallas_call | solution.py:174
  54.3 5.4 %collective-permute-start.10 = (bf16[2,128,768]{2,1,0:T(8,128)(2,1)S(1)}, bf16[2,128,768]{2,1,0:T(8,128)(2,1)S(1)}, u32[]{:S(2)}, u32[]{:S(2)}) collective-permute-start(bf16[2,128,768]{2,1,0:T(8,128)(2,1)S(1)} %get-tuple-element.40), channel_id=1, source_target_pairs={{0,448},{72,8},{64,128},{136,200},{128,64},{200,136},{192,256},{26... | collective-permute-start | bytes 1179656 | tf_op jit(solution)/shard_map/ppermute | solution.py:315
  59.7 0.0 collective-permute-done.11.got_ref
  59.7 1.0 %shard_map.86 = (bf16[2,128,384]{2,1,0:T(8,128)(2,1)S(1)}, bf16[2,128,384]{2,1,0:T(8,128)(2,1)S(1)}) custom-call(s32[4]{0:T(128)S(1)} %get-tuple-element.36.blocks, bf16[512,1024]{1,0:T(8,128)(2,1)S(1)} %copy-done.1, bf16[512,1152]{1,0:T(8,128)(2,1)S(1)} %bitcast.29, bf16[4,128,384]{2,1,0:T(8,128)(2,1)S(1)} %collective-permute-done.11.got_ref), custom_call_target="tpu_custom_call" | custom-call | flops 1 | bytes 1 | tf_op jit(solution)/shard_map/pallas_call | solution.py:174
  60.8 3.6 %collective-permute-start.12 = (bf16[2,128,384]{2,1,0:T(8,128)(2,1)S(1)}, bf16[2,128,384]{2,1,0:T(8,128)(2,1)S(1)}, u32[]{:S(2)}, u32[]{:S(2)}) collective-permute-start(bf16[2,128,384]{2,1,0:T(8,128)(2,1)S(1)} %get-tuple-element.44), channel_id=1, source_target_pairs={{0,448},{72,8},{64,128},{136,200},{128,64},{200,136},{192,256},{26... | collective-permute-start | bytes 589832 | tf_op jit(solution)/shard_map/ppermute | solution.py:315
  64.4 7.3 %collective-permute-start.7 = (bf16[2,512,128]{2,1,0:T(8,128)(2,1)S(1)}, bf16[2,512,128]{2,1,0:T(8,128)(2,1)S(1)}, u32[]{:S(2)}, u32[]{:S(2)}) collective-permute-start(bf16[2,512,128]{2,1,0:T(8,128)(2,1)S(1)} %get-tuple-element.33), channel_id=1, source_target_pairs={{0,16},{16,0},{32,48},{48,32},{1,17},{17,1},{33,49},{49,33},{2,18}... | collective-permute-start | bytes 786440 | tf_op jit(solution)/shard_map/ppermute | solution.py:323
  71.7 0.0 collective-permute-done.12.refs_3_
  71.7 0.0 collective-permute-done.10.refs_1_
  71.7 0.1 shard_map.87
  71.8 5.4 %collective-permute-start.13 = (bf16[128,1152]{1,0:T(8,128)(2,1)S(1)}, bf16[128,1152]{1,0:T(8,128)(2,1)S(1)}, u32[]{:S(2)}, u32[]{:S(2)}) collective-permute-start(bf16[128,1152]{1,0:T(8,128)(2,1)S(1)} %get-tuple-element.46), channel_id=1, source_target_pairs={{0,192},{72,264},{64,384},{136,456},{128,320},{200,392},{192,0},{2... | collective-permute-start | bytes 884744 | tf_op jit(solution)/shard_map/ppermute | solution.py:315
  77.2 0.0 collective-permute-done.7.refs_1_
  77.2 0.1 shard_map.84
  77.3 5.1 %collective-permute-start.8 = (bf16[512,128]{1,0:T(8,128)(2,1)S(1)}, bf16[512,128]{1,0:T(8,128)(2,1)S(1)}, u32[]{:S(2)}, u32[]{:S(2)}) collective-permute-start(bf16[512,128]{1,0:T(8,128)(2,1)S(1)} %get-tuple-element.35), channel_id=1, source_target_pairs={{0,32},{16,48},{32,0},{48,16},{1,33},{17,49},{33,1},{49,17},{2,34}... | collective-permute-start | bytes 393224 | tf_op jit(solution)/shard_map/ppermute | solution.py:337
  82.4 2.9 %collective-permute-done.8.input_got = bf16[512,128]{1,0:T(8,128)(2,1)S(1)} collective-permute-done((bf16[512,128]{1,0:T(8,128)(2,1)S(1)}, bf16[512,128]{1,0:T(8,128)(2,1)S(1)}, u32[]{:S(2)}, u32[]{:S(2)}) %collective-permute-start.8) | collective-permute-done | bytes 131104 | tf_op jit(solution)/shard_map/ppermute | solution.py:337
  85.3 1.5 %collective-permute-done.13.got = bf16[128,1152]{1,0:T(8,128)(2,1)S(1)} collective-permute-done((bf16[128,1152]{1,0:T(8,128)(2,1)S(1)}, bf16[128,1152]{1,0:T(8,128)(2,1)S(1)}, u32[]{:S(2)}, u32[]{:S(2)}) %collective-permute-start.13) | collective-permute-done | bytes 294944 | tf_op jit(solution)/shard_map/ppermute | solution.py:315
  86.8 0.9 %shard_map.88 = (bf16[512,128]{1,0:T(8,128)(2,1)}, f32[128,1024]{1,0:T(8,128)}, f32[128,128]{1,0:T(8,128)}) custom-call(bf16[512,128]{1,0:T(8,128)(2,1)S(1)} %get-tuple-element.34.input_kept, bf16[512,128]{1,0:T(8,128)(2,1)S(1)} %collective-permute-done.8.input_got, bf16[128,1152]{1,0:T(8,128)(2,1)S(1)} %get-tuple-element.45.kept, ...), custom_call_target="tpu_custom_call" | custom-call | flops 1 | bytes 1 | tf_op jit(solution)/shard_map/pallas_call | solution.py:224
  (10 shorter events, 0.1 us)
Async XLA Ops:
  0.6 3.7 %collective-permute-start = (bf16[64,256]{1,0:T(8,128)(2,1)}, bf16[64,256]{1,0:T(8,128)(2,1)S(1)}, u32[]{:S(2)}, u32[]{:S(2)}) collective-permute-start(bf16[64,256]{1,0:T(8,128)(2,1)} %rows_ref.3), channel_id=1, source_target_pairs={{0,8},{8,0},{1,9},{9,1},{2,10},{10,2},{3,11},{11,3},{4,12},{12,4},... | collective-permute-start | bytes 98312 | tf_op jit(solution)/shard_map/ppermute | solution.py:292
  2.6 0.8 copy-start.4
  3.3 0.9 %copy-start.3 = (bf16[64,1024]{1,0:T(8,128)(2,1)S(1)}, bf16[64,1024]{1,0:T(8,128)(2,1)}, u32[]{:S(2)}) copy-start(bf16[64,1024]{1,0:T(8,128)(2,1)} %rows_ref.2) | copy-start | bytes 393220
  4.5 33.3 %copy-start.1 = (bf16[512,1024]{1,0:T(8,128)(2,1)S(1)}, bf16[512,1024]{1,0:T(8,128)(2,1)}, u32[]{:S(2)}) copy-start(bf16[512,1024]{1,0:T(8,128)(2,1)} %x_ref.5) | copy-start | bytes 3145732
  4.5 15.6 %collective-permute-start.1 = (bf16[64,1152]{1,0:T(8,128)(2,1)S(1)}, bf16[64,1152]{1,0:T(8,128)(2,1)S(1)}, u32[]{:S(2)}, u32[]{:S(2)}) collective-permute-start(bf16[64,1152]{1,0:T(8,128)(2,1)S(1)} %shard_map.78.rows_ref), channel_id=1, source_target_pairs={{0,1},{1,0},{2,3},{3,2},{4,5},{5,4},{6,7},{7,6},{8,9},{9,8},{10,11... | collective-permute-start | bytes 442376 | tf_op jit(solution)/shard_map/ppermute | solution.py:294
  15.5 7.3 %collective-permute-start.2 = (bf16[64,1152]{1,0:T(8,128)(2,1)S(1)}, bf16[64,1152]{1,0:T(8,128)(2,1)S(1)}, u32[]{:S(2)}, u32[]{:S(2)}) collective-permute-start(bf16[64,1152]{1,0:T(8,128)(2,1)S(1)} %shard_map.79), channel_id=1, source_target_pairs={{0,2},{2,0},{4,6},{6,4},{10,12},{12,10},{14,8},{8,14},{1,3},{3,1},... | collective-permute-start | bytes 442376 | tf_op jit(solution)/shard_map/ppermute | solution.py:104
  20.1 7.0 %collective-permute-start.4 = (bf16[64,1152]{1,0:T(8,128)(2,1)S(1)}, bf16[64,1152]{1,0:T(8,128)(2,1)S(1)}, u32[]{:S(2)}, u32[]{:S(2)}) collective-permute-start(bf16[64,1152]{1,0:T(8,128)(2,1)S(1)} %collective-permute-done.1), channel_id=1, source_target_pairs={{0,2},{2,0},{4,6},{6,4},{10,12},{12,10},{14,8},{8,14},{1,3},{3,1},... | collective-permute-start | bytes 442376 | tf_op jit(solution)/shard_map/ppermute | solution.py:104
  22.9 9.8 %collective-permute-start.3 = (bf16[2,64,1152]{2,1,0:T(8,128)(2,1)S(1)}, bf16[2,64,1152]{2,1,0:T(8,128)(2,1)S(1)}, u32[]{:S(2)}, u32[]{:S(2)}) collective-permute-start(bf16[2,64,1152]{2,1,0:T(8,128)(2,1)S(1)} %pad_maximum_fusion.refs_0_), channel_id=1, source_target_pairs={{0,6},{2,4},{4,2},{6,0},{10,8},{12,14},{14,12},{8,10},{1,7},{3,5},... | collective-permute-start | bytes 884744 | tf_op jit(solution)/shard_map/ppermute | solution.py:104
  27.2 15.6 %copy-start = (bf16[1024,1024]{1,0:T(8,128)(2,1)S(1)}, bf16[1024,1024]{1,0:T(8,128)(2,1)}, u32[]{:S(2)}) copy-start(bf16[1024,1024]{1,0:T(8,128)(2,1)} %param.8) | copy-start | bytes 6291460
  27.2 15.6 %copy-start.2 = (bf16[1024,128]{1,0:T(8,128)(2,1)S(1)}, bf16[1024,128]{1,0:T(8,128)(2,1)}, u32[]{:S(2)}) copy-start(bf16[1024,128]{1,0:T(8,128)(2,1)} %param.9) | copy-start | bytes 786436
  27.2 10.0 %collective-permute-start.5 = (bf16[2,64,1152]{2,1,0:T(8,128)(2,1)S(1)}, bf16[2,64,1152]{2,1,0:T(8,128)(2,1)S(1)}, u32[]{:S(2)}, u32[]{:S(2)}) collective-permute-start(bf16[2,64,1152]{2,1,0:T(8,128)(2,1)S(1)} %pad_maximum_fusion.1.refs_2_), channel_id=1, source_target_pairs={{0,6},{2,4},{4,2},{6,0},{10,8},{12,14},{14,12},{8,10},{1,7},{3,5},... | collective-permute-start | bytes 884744 | tf_op jit(solution)/shard_map/ppermute | solution.py:104
  39.3 13.9 %collective-permute-start.9 = (bf16[4,128,768]{2,1,0:T(8,128)(2,1)S(1)}, bf16[4,128,768]{2,1,0:T(8,128)(2,1)S(1)}, u32[]{:S(2)}, u32[]{:S(2)}) collective-permute-start(bf16[4,128,768]{2,1,0:T(8,128)(2,1)S(1)} %get-tuple-element.37), channel_id=1, source_target_pairs={{0,64},{72,136},{64,0},{136,72},{128,192},{200,264},{192,128},{264... | collective-permute-start | bytes 2359304 | tf_op jit(solution)/shard_map/ppermute | solution.py:315
  44.4 4.3 %collective-permute-start.6 = (bf16[4,512,128]{2,1,0:T(8,128)(2,1)S(1)}, bf16[4,512,128]{2,1,0:T(8,128)(2,1)S(1)}, u32[]{:S(2)}, u32[]{:S(2)}) collective-permute-start(bf16[4,512,128]{2,1,0:T(8,128)(2,1)S(1)} %shard_map.82), channel_id=1, source_target_pairs={{0,8},{8,0},{1,9},{9,1},{2,10},{10,2},{3,11},{11,3},{4,12},{12,4},... | collective-permute-start | bytes 1572872 | tf_op jit(solution)/shard_map/ppermute | solution.py:321
  46.3 13.4 %collective-permute-start.11 = (bf16[4,128,384]{2,1,0:T(8,128)(2,1)S(1)}, bf16[4,128,384]{2,1,0:T(8,128)(2,1)S(1)}, u32[]{:S(2)}, u32[]{:S(2)}) collective-permute-start(bf16[4,128,384]{2,1,0:T(8,128)(2,1)S(1)} %get-tuple-element.41), channel_id=1, source_target_pairs={{0,64},{72,136},{64,0},{136,72},{128,192},{200,264},{192,128},{264... | collective-permute-start | bytes 1179656 | tf_op jit(solution)/shard_map/ppermute | solution.py:315
  54.3 17.3 %collective-permute-start.10 = (bf16[2,128,768]{2,1,0:T(8,128)(2,1)S(1)}, bf16[2,128,768]{2,1,0:T(8,128)(2,1)S(1)}, u32[]{:S(2)}, u32[]{:S(2)}) collective-permute-start(bf16[2,128,768]{2,1,0:T(8,128)(2,1)S(1)} %get-tuple-element.40), channel_id=1, source_target_pairs={{0,448},{72,8},{64,128},{136,200},{128,64},{200,136},{192,256},{26... | collective-permute-start | bytes 1179656 | tf_op jit(solution)/shard_map/ppermute | solution.py:315
  60.8 10.9 %collective-permute-start.12 = (bf16[2,128,384]{2,1,0:T(8,128)(2,1)S(1)}, bf16[2,128,384]{2,1,0:T(8,128)(2,1)S(1)}, u32[]{:S(2)}, u32[]{:S(2)}) collective-permute-start(bf16[2,128,384]{2,1,0:T(8,128)(2,1)S(1)} %get-tuple-element.44), channel_id=1, source_target_pairs={{0,448},{72,8},{64,128},{136,200},{128,64},{200,136},{192,256},{26... | collective-permute-start | bytes 589832 | tf_op jit(solution)/shard_map/ppermute | solution.py:315
  64.4 12.9 %collective-permute-start.7 = (bf16[2,512,128]{2,1,0:T(8,128)(2,1)S(1)}, bf16[2,512,128]{2,1,0:T(8,128)(2,1)S(1)}, u32[]{:S(2)}, u32[]{:S(2)}) collective-permute-start(bf16[2,512,128]{2,1,0:T(8,128)(2,1)S(1)} %get-tuple-element.33), channel_id=1, source_target_pairs={{0,16},{16,0},{32,48},{48,32},{1,17},{17,1},{33,49},{49,33},{2,18}... | collective-permute-start | bytes 786440 | tf_op jit(solution)/shard_map/ppermute | solution.py:323
  71.8 15.0 %collective-permute-start.13 = (bf16[128,1152]{1,0:T(8,128)(2,1)S(1)}, bf16[128,1152]{1,0:T(8,128)(2,1)S(1)}, u32[]{:S(2)}, u32[]{:S(2)}) collective-permute-start(bf16[128,1152]{1,0:T(8,128)(2,1)S(1)} %get-tuple-element.46), channel_id=1, source_target_pairs={{0,192},{72,264},{64,384},{136,456},{128,320},{200,392},{192,0},{2... | collective-permute-start | bytes 884744 | tf_op jit(solution)/shard_map/ppermute | solution.py:315
  77.3 8.0 %collective-permute-start.8 = (bf16[512,128]{1,0:T(8,128)(2,1)S(1)}, bf16[512,128]{1,0:T(8,128)(2,1)S(1)}, u32[]{:S(2)}, u32[]{:S(2)}) collective-permute-start(bf16[512,128]{1,0:T(8,128)(2,1)S(1)} %get-tuple-element.35), channel_id=1, source_target_pairs={{0,32},{16,48},{32,0},{48,16},{1,33},{17,49},{33,1},{49,17},{2,34}... | collective-permute-start | bytes 393224 | tf_op jit(solution)/shard_map/ppermute | solution.py:337

commit v12 on v11

--- a/solution.py
+++ b/solution.py
@@ -322,7 +322,7 @@
     give, input_keep = input_terms(keep_heads, for_input, q_weight, key_value_weight, core_got)
     input_got = lax.ppermute(give, "zlo", [(i, i ^ 1) for i in range(4)])
 
-    after = input_keep
+    after = combined
     parts = []
     at = 0
     for part in got:

time: 89 us -> 91.3 us (1.026)
  waiting for transfers between devices: 14.5 us -> 19.2 us
  starting transfers between devices: 61.3 us -> 59.5 us
    ppermute x1, waiting for transfers between devices: 2.93 us -> 5.81 us  [local(): input_got = lax.ppermute(give, 'zlo', [(i, i ^ 2) for i in range(4)])]
    ppermute x5, waiting for transfers between devices: 4.22 us -> 6.2 us  [along_y(): return lax.ppermute(terms, (*TOK, 'core'), pairs)]
    ppermute x1, starting transfers between devices: 5.08 us -> 3.34 us  [local(): input_got = lax.ppermute(give, 'zlo', [(i, i ^ 2) for i in range(4)])]
  transfers between devices with their start and end apart: 14 -> 14, of which waited for: 7 -> 7; matrix products, arithmetic and copies ran while one was open for 0% -> 0% of each run, Pallas kernels for 7% -> 6%
where the time goes in v12:
time: 91.3 us; the launch traced here: 90.7 us
  starting transfers between devices  59.5 us (65%)
  waiting for transfers between devices  19.2 us (21%)
  Pallas kernels  8.82 us (10%)
  local copies, waits for them, and re-layouts  1.66 us (2%)
  between operations  1.21 us (1%)
    ppermute x5, starting transfers between devices, along_y(): return lax.ppermute(terms, (*TOK, 'core'), pairs)  19.6 us
    ppermute x4, starting transfers between devices, x_swap(): return lax.ppermute(rows, ('core', 'x'), pairs)  13.9 us
    ppermute x1, starting transfers between devices, local(): far = lax.ppermute(mine, 'zhi', SWAP)  10.9 us
    ppermute x1, starting transfers between devices, local(): input_got = lax.ppermute(give, 'zlo', [(i, i ^ 1) for i in range(4)])  7.87 us
    ppermute x5, waiting for transfers between devices, along_y(): return lax.ppermute(terms, (*TOK, 'core'), pairs)  6.2 us
    ppermute x4, waiting for transfers between devices, x_swap(): return lax.ppermute(rows, ('core', 'x'), pairs)  5.83 us
    ppermute x1, waiting for transfers between devices, local(): input_got = lax.ppermute(give, 'zlo', [(i, i ^ 2) for i in range(4)])  5.81 us
    ppermute x1, starting transfers between devices, local(): input_got = lax.ppermute(give, 'zlo', [(i, i ^ 2) for i in range(4)])  3.34 us
  transfers between devices with their start and end apart: 14, of which 7 were waited for; matrix products, arithmetic and copies ran while one was open for 0% of the time, Pallas kernels for 6%

profile of v12, /device:TPU:6, one launch (start us, length us, event | category | flops | bytes accessed | tf_op | source)
XLA Modules:
  0.0 90.7 jit_solution(16851701662985590612)
XLA Ops:
  0.6 1.9 %collective-permute-start = (bf16[64,256]{1,0:T(8,128)(2,1)}, bf16[64,256]{1,0:T(8,128)(2,1)S(1)}, u32[]{:S(2)}, u32[]{:S(2)}) collective-permute-start(bf16[64,256]{1,0:T(8,128)(2,1)} %rows_ref.3), channel_id=1, source_target_pairs={{0,8},{8,0},{1,9},{9,1},{2,10},{10,2},{3,11},{11,3},{4,12},{12,4},... | collective-permute-start | bytes 98312 | tf_op jit(solution)/shard_map/ppermute | solution.py:292
  2.6 0.0 copy-start.4
  2.6 0.7 copy-done.4
  3.3 0.1 stack.86
  3.4 0.8 copy-done.3
  4.3 0.1 broadcast_add_fusion
  4.3 0.0 collective-permute-done.more_ref
  4.3 0.1 shard_map.78.rows_ref
  4.4 10.9 %collective-permute-start.1 = (bf16[64,1152]{1,0:T(8,128)(2,1)S(1)}, bf16[64,1152]{1,0:T(8,128)(2,1)S(1)}, u32[]{:S(2)}, u32[]{:S(2)}) collective-permute-start(bf16[64,1152]{1,0:T(8,128)(2,1)S(1)} %shard_map.78.rows_ref), channel_id=1, source_target_pairs={{0,1},{1,0},{2,3},{3,2},{4,5},{5,4},{6,7},{7,6},{8,9},{9,8},{10,11... | collective-permute-start | bytes 442376 | tf_op jit(solution)/shard_map/ppermute | solution.py:294
  15.4 0.0 copy-start.1
  15.4 2.9 %collective-permute-start.2 = (bf16[64,1152]{1,0:T(8,128)(2,1)S(1)}, bf16[64,1152]{1,0:T(8,128)(2,1)S(1)}, u32[]{:S(2)}, u32[]{:S(2)}) collective-permute-start(bf16[64,1152]{1,0:T(8,128)(2,1)S(1)} %shard_map.79), channel_id=1, source_target_pairs={{0,2},{2,0},{4,6},{6,4},{10,12},{12,10},{14,8},{8,14},{1,3},{3,1},... | collective-permute-start | bytes 442376 | tf_op jit(solution)/shard_map/ppermute | solution.py:104
  18.5 0.1 and_select_fusion
  18.6 1.3 %collective-permute-done.1 = bf16[64,1152]{1,0:T(8,128)(2,1)S(1)} collective-permute-done((bf16[64,1152]{1,0:T(8,128)(2,1)S(1)}, bf16[64,1152]{1,0:T(8,128)(2,1)S(1)}, u32[]{:S(2)}, u32[]{:S(2)}) %collective-permute-start.1) | collective-permute-done | bytes 147488 | tf_op jit(solution)/shard_map/ppermute | solution.py:294
  20.0 2.7 %collective-permute-start.4 = (bf16[64,1152]{1,0:T(8,128)(2,1)S(1)}, bf16[64,1152]{1,0:T(8,128)(2,1)S(1)}, u32[]{:S(2)}, u32[]{:S(2)}) collective-permute-start(bf16[64,1152]{1,0:T(8,128)(2,1)S(1)} %collective-permute-done.1), channel_id=1, source_target_pairs={{0,2},{2,0},{4,6},{6,4},{10,12},{12,10},{14,8},{8,14},{1,3},{3,1},... | collective-permute-start | bytes 442376 | tf_op jit(solution)/shard_map/ppermute | solution.py:104
  22.7 0.0 collective-permute-done.2
  22.8 3.6 %collective-permute-start.3 = (bf16[2,64,1152]{2,1,0:T(8,128)(2,1)S(1)}, bf16[2,64,1152]{2,1,0:T(8,128)(2,1)S(1)}, u32[]{:S(2)}, u32[]{:S(2)}) collective-permute-start(bf16[2,64,1152]{2,1,0:T(8,128)(2,1)S(1)} %pad_maximum_fusion.refs_0_), channel_id=1, source_target_pairs={{0,6},{2,4},{4,2},{6,0},{10,8},{12,14},{14,12},{8,10},{1,7},{3,5},... | collective-permute-start | bytes 884744 | tf_op jit(solution)/shard_map/ppermute | solution.py:104
  26.3 0.7 collective-permute-done.4
  27.0 0.0 copy-start
  27.0 0.0 copy-start.2
  27.1 4.8 %collective-permute-start.5 = (bf16[2,64,1152]{2,1,0:T(8,128)(2,1)S(1)}, bf16[2,64,1152]{2,1,0:T(8,128)(2,1)S(1)}, u32[]{:S(2)}, u32[]{:S(2)}) collective-permute-start(bf16[2,64,1152]{2,1,0:T(8,128)(2,1)S(1)} %pad_maximum_fusion.1.refs_2_), channel_id=1, source_target_pairs={{0,6},{2,4},{4,2},{6,0},{10,8},{12,14},{14,12},{8,10},{1,7},{3,5},... | collective-permute-start | bytes 884744 | tf_op jit(solution)/shard_map/ppermute | solution.py:104
  31.8 0.7 collective-permute-done.3.refs_1_
  32.6 4.4 %collective-permute-done.5.refs_3_ = bf16[2,64,1152]{2,1,0:T(8,128)(2,1)S(1)} collective-permute-done((bf16[2,64,1152]{2,1,0:T(8,128)(2,1)S(1)}, bf16[2,64,1152]{2,1,0:T(8,128)(2,1)S(1)}, u32[]{:S(2)}, u32[]{:S(2)}) %collective-permute-start.5) | collective-permute-done | bytes 294944 | tf_op jit(solution)/shard_map/ppermute | solution.py:104
  37.0 0.6 shard_map.80
  37.7 1.4 %shard_map.81 = (bf16[4,128,768]{2,1,0:T(8,128)(2,1)S(1)}, bf16[4,128,384]{2,1,0:T(8,128)(2,1)S(1)}) custom-call(s32[4]{0:T(128)S(1)} %get-tuple-element.26.blocks, bf16[512,1024]{1,0:T(8,128)(2,1)S(1)} %copy-done.1, bf16[512,1152]{1,0:T(8,128)(2,1)S(1)} %bitcast.25), custom_call_target="tpu_custom_call" | custom-call | flops 1 | bytes 1 | tf_op jit(solution)/shard_map/pallas_call | solution.py:154
  39.1 3.5 %collective-permute-start.9 = (bf16[4,128,768]{2,1,0:T(8,128)(2,1)S(1)}, bf16[4,128,768]{2,1,0:T(8,128)(2,1)S(1)}, u32[]{:S(2)}, u32[]{:S(2)}) collective-permute-start(bf16[4,128,768]{2,1,0:T(8,128)(2,1)S(1)} %get-tuple-element.37), channel_id=1, source_target_pairs={{0,64},{72,136},{64,0},{136,72},{128,192},{200,264},{192,128},{264... | collective-permute-start | bytes 2359304 | tf_op jit(solution)/shard_map/ppermute | solution.py:315
  42.6 0.0 copy-done
  42.6 1.6 %shard_map.82 = bf16[4,512,128]{2,1,0:T(8,128)(2,1)S(1)} custom-call(s32[4]{0:T(128)S(1)} %add_subtract_fusion.blocks, bf16[512,1152]{1,0:T(8,128)(2,1)S(1)} %bitcast.26, bf16[8,128,1024]{2,1,0:T(8,128)(2,1)S(1)} %bitcast.30, bf16[8,128,1024]{2,1,0:T(8,128)(2,1)S(1)} %bitcast.31, bf16[8,128,128]{2,1,0:T(8,128)(2,1)S(1)} %bitcast.34, ...), custom_call_target="tpu_custom_call" | custom-call | flops 1 | bytes 1 | tf_op jit(solution)/shard_map/pallas_call | solution.py:265
  44.2 1.9 %collective-permute-start.6 = (bf16[4,512,128]{2,1,0:T(8,128)(2,1)S(1)}, bf16[4,512,128]{2,1,0:T(8,128)(2,1)S(1)}, u32[]{:S(2)}, u32[]{:S(2)}) collective-permute-start(bf16[4,512,128]{2,1,0:T(8,128)(2,1)S(1)} %shard_map.82), channel_id=1, source_target_pairs={{0,8},{8,0},{1,9},{9,1},{2,10},{10,2},{3,11},{11,3},{4,12},{12,4},... | collective-permute-start | bytes 1572872 | tf_op jit(solution)/shard_map/ppermute | solution.py:321
  46.2 2.4 %collective-permute-start.11 = (bf16[4,128,384]{2,1,0:T(8,128)(2,1)S(1)}, bf16[4,128,384]{2,1,0:T(8,128)(2,1)S(1)}, u32[]{:S(2)}, u32[]{:S(2)}) collective-permute-start(bf16[4,128,384]{2,1,0:T(8,128)(2,1)S(1)} %get-tuple-element.41), channel_id=1, source_target_pairs={{0,64},{72,136},{64,0},{136,72},{128,192},{200,264},{192,128},{264... | collective-permute-start | bytes 1179656 | tf_op jit(solution)/shard_map/ppermute | solution.py:315
  48.5 4.5 %collective-permute-done.9.got_ref = bf16[4,128,768]{2,1,0:T(8,128)(2,1)S(1)} collective-permute-done((bf16[4,128,768]{2,1,0:T(8,128)(2,1)S(1)}, bf16[4,128,768]{2,1,0:T(8,128)(2,1)S(1)}, u32[]{:S(2)}, u32[]{:S(2)}) %collective-permute-start.9) | collective-permute-done | bytes 786464 | tf_op jit(solution)/shard_map/ppermute | solution.py:315
  53.0 1.2 %shard_map.85 = (bf16[2,128,768]{2,1,0:T(8,128)(2,1)S(1)}, bf16[2,128,768]{2,1,0:T(8,128)(2,1)S(1)}) custom-call(s32[4]{0:T(128)S(1)} %get-tuple-element.36.blocks, bf16[512,1024]{1,0:T(8,128)(2,1)S(1)} %copy-done.1, bf16[512,1152]{1,0:T(8,128)(2,1)S(1)} %bitcast.27, bf16[4,128,768]{2,1,0:T(8,128)(2,1)S(1)} %collective-permute-done.9.got_ref), custom_call_target="tpu_custom_call" | custom-call | flops 1 | bytes 1 | tf_op jit(solution)/shard_map/pallas_call | solution.py:174
  54.2 5.4 %collective-permute-start.10 = (bf16[2,128,768]{2,1,0:T(8,128)(2,1)S(1)}, bf16[2,128,768]{2,1,0:T(8,128)(2,1)S(1)}, u32[]{:S(2)}, u32[]{:S(2)}) collective-permute-start(bf16[2,128,768]{2,1,0:T(8,128)(2,1)S(1)} %get-tuple-element.40), channel_id=1, source_target_pairs={{0,448},{72,8},{64,128},{136,200},{128,64},{200,136},{192,256},{26... | collective-permute-start | bytes 1179656 | tf_op jit(solution)/shard_map/ppermute | solution.py:315
  59.6 0.0 collective-permute-done.11.got_ref
  59.6 1.0 %shard_map.86 = (bf16[2,128,384]{2,1,0:T(8,128)(2,1)S(1)}, bf16[2,128,384]{2,1,0:T(8,128)(2,1)S(1)}) custom-call(s32[4]{0:T(128)S(1)} %get-tuple-element.36.blocks, bf16[512,1024]{1,0:T(8,128)(2,1)S(1)} %copy-done.1, bf16[512,1152]{1,0:T(8,128)(2,1)S(1)} %bitcast.28, bf16[4,128,384]{2,1,0:T(8,128)(2,1)S(1)} %collective-permute-done.11.got_ref), custom_call_target="tpu_custom_call" | custom-call | flops 1 | bytes 1 | tf_op jit(solution)/shard_map/pallas_call | solution.py:174
  60.6 3.6 %collective-permute-start.12 = (bf16[2,128,384]{2,1,0:T(8,128)(2,1)S(1)}, bf16[2,128,384]{2,1,0:T(8,128)(2,1)S(1)}, u32[]{:S(2)}, u32[]{:S(2)}) collective-permute-start(bf16[2,128,384]{2,1,0:T(8,128)(2,1)S(1)} %get-tuple-element.44), channel_id=1, source_target_pairs={{0,448},{72,8},{64,128},{136,200},{128,64},{200,136},{192,256},{26... | collective-permute-start | bytes 589832 | tf_op jit(solution)/shard_map/ppermute | solution.py:315
  64.2 0.0 collective-permute-done.6.refs_0_
  64.2 1.7 %shard_map.83 = (bf16[2,512,128]{2,1,0:T(8,128)(2,1)S(1)}, bf16[2,512,128]{2,1,0:T(8,128)(2,1)S(1)}) custom-call(s32[4]{0:T(128)S(1)} %get-tuple-element.25.blocks, bf16[512,1152]{1,0:T(8,128)(2,1)S(1)} %bitcast.29, bf16[8,128,1024]{2,1,0:T(8,128)(2,1)S(1)} %bitcast.32, bf16[8,128,1024]{2,1,0:T(8,128)(2,1)S(1)} %bitcast.33, ...), custom_call_target="tpu_custom_call" | custom-call | flops 1 | bytes 1 | tf_op jit(solution)/shard_map/pallas_call | solution.py:265
  65.9 7.9 %collective-permute-start.7 = (bf16[2,512,128]{2,1,0:T(8,128)(2,1)S(1)}, bf16[2,512,128]{2,1,0:T(8,128)(2,1)S(1)}, u32[]{:S(2)}, u32[]{:S(2)}) collective-permute-start(bf16[2,512,128]{2,1,0:T(8,128)(2,1)S(1)} %get-tuple-element.33), channel_id=1, source_target_pairs={{0,16},{16,0},{32,48},{48,32},{1,17},{17,1},{33,49},{49,33},{2,18}... | collective-permute-start | bytes 786440 | tf_op jit(solution)/shard_map/ppermute | solution.py:323
  73.8 0.0 collective-permute-done.12.refs_3_
  73.8 0.0 collective-permute-done.10.refs_1_
  73.8 0.1 shard_map.87
  74.0 4.8 %collective-permute-start.13 = (bf16[128,1152]{1,0:T(8,128)(2,1)S(1)}, bf16[128,1152]{1,0:T(8,128)(2,1)S(1)}, u32[]{:S(2)}, u32[]{:S(2)}) collective-permute-start(bf16[128,1152]{1,0:T(8,128)(2,1)S(1)} %get-tuple-element.46), channel_id=1, source_target_pairs={{0,192},{72,264},{64,384},{136,456},{128,320},{200,392},{192,0},{2... | collective-permute-start | bytes 884744 | tf_op jit(solution)/shard_map/ppermute | solution.py:315
  78.8 0.0 collective-permute-done.7.refs_1_
  78.8 0.1 shard_map.84
  78.9 3.3 %collective-permute-start.8 = (bf16[512,128]{1,0:T(8,128)(2,1)S(1)}, bf16[512,128]{1,0:T(8,128)(2,1)S(1)}, u32[]{:S(2)}, u32[]{:S(2)}) collective-permute-start(bf16[512,128]{1,0:T(8,128)(2,1)S(1)} %get-tuple-element.35), channel_id=1, source_target_pairs={{0,32},{16,48},{32,0},{48,16},{1,33},{17,49},{33,1},{49,17},{2,34}... | collective-permute-start | bytes 393224 | tf_op jit(solution)/shard_map/ppermute | solution.py:337
  82.2 5.8 %collective-permute-done.8.input_got = bf16[512,128]{1,0:T(8,128)(2,1)S(1)} collective-permute-done((bf16[512,128]{1,0:T(8,128)(2,1)S(1)}, bf16[512,128]{1,0:T(8,128)(2,1)S(1)}, u32[]{:S(2)}, u32[]{:S(2)}) %collective-permute-start.8) | collective-permute-done | bytes 131104 | tf_op jit(solution)/shard_map/ppermute | solution.py:337
  88.0 1.7 %collective-permute-done.13.got = bf16[128,1152]{1,0:T(8,128)(2,1)S(1)} collective-permute-done((bf16[128,1152]{1,0:T(8,128)(2,1)S(1)}, bf16[128,1152]{1,0:T(8,128)(2,1)S(1)}, u32[]{:S(2)}, u32[]{:S(2)}) %collective-permute-start.13) | collective-permute-done | bytes 294944 | tf_op jit(solution)/shard_map/ppermute | solution.py:315
  89.8 0.9 shard_map.88
  (10 shorter events, 0.1 us)
Async XLA Ops:
  0.6 3.7 %collective-permute-start = (bf16[64,256]{1,0:T(8,128)(2,1)}, bf16[64,256]{1,0:T(8,128)(2,1)S(1)}, u32[]{:S(2)}, u32[]{:S(2)}) collective-permute-start(bf16[64,256]{1,0:T(8,128)(2,1)} %rows_ref.3), channel_id=1, source_target_pairs={{0,8},{8,0},{1,9},{9,1},{2,10},{10,2},{3,11},{11,3},{4,12},{12,4},... | collective-permute-start | bytes 98312 | tf_op jit(solution)/shard_map/ppermute | solution.py:292
  2.6 0.8 copy-start.4
  3.3 0.9 copy-start.3
  4.4 15.5 %collective-permute-start.1 = (bf16[64,1152]{1,0:T(8,128)(2,1)S(1)}, bf16[64,1152]{1,0:T(8,128)(2,1)S(1)}, u32[]{:S(2)}, u32[]{:S(2)}) collective-permute-start(bf16[64,1152]{1,0:T(8,128)(2,1)S(1)} %shard_map.78.rows_ref), channel_id=1, source_target_pairs={{0,1},{1,0},{2,3},{3,2},{4,5},{5,4},{6,7},{7,6},{8,9},{9,8},{10,11... | collective-permute-start | bytes 442376 | tf_op jit(solution)/shard_map/ppermute | solution.py:294
  15.4 22.3 %copy-start.1 = (bf16[512,1024]{1,0:T(8,128)(2,1)S(1)}, bf16[512,1024]{1,0:T(8,128)(2,1)}, u32[]{:S(2)}) copy-start(bf16[512,1024]{1,0:T(8,128)(2,1)} %x_ref.5) | copy-start | bytes 3145732
  15.4 7.3 %collective-permute-start.2 = (bf16[64,1152]{1,0:T(8,128)(2,1)S(1)}, bf16[64,1152]{1,0:T(8,128)(2,1)S(1)}, u32[]{:S(2)}, u32[]{:S(2)}) collective-permute-start(bf16[64,1152]{1,0:T(8,128)(2,1)S(1)} %shard_map.79), channel_id=1, source_target_pairs={{0,2},{2,0},{4,6},{6,4},{10,12},{12,10},{14,8},{8,14},{1,3},{3,1},... | collective-permute-start | bytes 442376 | tf_op jit(solution)/shard_map/ppermute | solution.py:104
  20.0 7.0 %collective-permute-start.4 = (bf16[64,1152]{1,0:T(8,128)(2,1)S(1)}, bf16[64,1152]{1,0:T(8,128)(2,1)S(1)}, u32[]{:S(2)}, u32[]{:S(2)}) collective-permute-start(bf16[64,1152]{1,0:T(8,128)(2,1)S(1)} %collective-permute-done.1), channel_id=1, source_target_pairs={{0,2},{2,0},{4,6},{6,4},{10,12},{12,10},{14,8},{8,14},{1,3},{3,1},... | collective-permute-start | bytes 442376 | tf_op jit(solution)/shard_map/ppermute | solution.py:104
  22.8 9.8 %collective-permute-start.3 = (bf16[2,64,1152]{2,1,0:T(8,128)(2,1)S(1)}, bf16[2,64,1152]{2,1,0:T(8,128)(2,1)S(1)}, u32[]{:S(2)}, u32[]{:S(2)}) collective-permute-start(bf16[2,64,1152]{2,1,0:T(8,128)(2,1)S(1)} %pad_maximum_fusion.refs_0_), channel_id=1, source_target_pairs={{0,6},{2,4},{4,2},{6,0},{10,8},{12,14},{14,12},{8,10},{1,7},{3,5},... | collective-permute-start | bytes 884744 | tf_op jit(solution)/shard_map/ppermute | solution.py:104
  27.0 15.6 %copy-start = (bf16[1024,1024]{1,0:T(8,128)(2,1)S(1)}, bf16[1024,1024]{1,0:T(8,128)(2,1)}, u32[]{:S(2)}) copy-start(bf16[1024,1024]{1,0:T(8,128)(2,1)} %param.8) | copy-start | bytes 6291460
  27.0 15.6 %copy-start.2 = (bf16[1024,128]{1,0:T(8,128)(2,1)S(1)}, bf16[1024,128]{1,0:T(8,128)(2,1)}, u32[]{:S(2)}) copy-start(bf16[1024,128]{1,0:T(8,128)(2,1)} %param.9) | copy-start | bytes 786436
  27.1 10.0 %collective-permute-start.5 = (bf16[2,64,1152]{2,1,0:T(8,128)(2,1)S(1)}, bf16[2,64,1152]{2,1,0:T(8,128)(2,1)S(1)}, u32[]{:S(2)}, u32[]{:S(2)}) collective-permute-start(bf16[2,64,1152]{2,1,0:T(8,128)(2,1)S(1)} %pad_maximum_fusion.1.refs_2_), channel_id=1, source_target_pairs={{0,6},{2,4},{4,2},{6,0},{10,8},{12,14},{14,12},{8,10},{1,7},{3,5},... | collective-permute-start | bytes 884744 | tf_op jit(solution)/shard_map/ppermute | solution.py:104
  39.1 13.9 %collective-permute-start.9 = (bf16[4,128,768]{2,1,0:T(8,128)(2,1)S(1)}, bf16[4,128,768]{2,1,0:T(8,128)(2,1)S(1)}, u32[]{:S(2)}, u32[]{:S(2)}) collective-permute-start(bf16[4,128,768]{2,1,0:T(8,128)(2,1)S(1)} %get-tuple-element.37), channel_id=1, source_target_pairs={{0,64},{72,136},{64,0},{136,72},{128,192},{200,264},{192,128},{264... | collective-permute-start | bytes 2359304 | tf_op jit(solution)/shard_map/ppermute | solution.py:315
  44.2 20.0 %collective-permute-start.6 = (bf16[4,512,128]{2,1,0:T(8,128)(2,1)S(1)}, bf16[4,512,128]{2,1,0:T(8,128)(2,1)S(1)}, u32[]{:S(2)}, u32[]{:S(2)}) collective-permute-start(bf16[4,512,128]{2,1,0:T(8,128)(2,1)S(1)} %shard_map.82), channel_id=1, source_target_pairs={{0,8},{8,0},{1,9},{9,1},{2,10},{10,2},{3,11},{11,3},{4,12},{12,4},... | collective-permute-start | bytes 1572872 | tf_op jit(solution)/shard_map/ppermute | solution.py:321
  46.2 13.4 %collective-permute-start.11 = (bf16[4,128,384]{2,1,0:T(8,128)(2,1)S(1)}, bf16[4,128,384]{2,1,0:T(8,128)(2,1)S(1)}, u32[]{:S(2)}, u32[]{:S(2)}) collective-permute-start(bf16[4,128,384]{2,1,0:T(8,128)(2,1)S(1)} %get-tuple-element.41), channel_id=1, source_target_pairs={{0,64},{72,136},{64,0},{136,72},{128,192},{200,264},{192,128},{264... | collective-permute-start | bytes 1179656 | tf_op jit(solution)/shard_map/ppermute | solution.py:315
  54.2 19.6 %collective-permute-start.10 = (bf16[2,128,768]{2,1,0:T(8,128)(2,1)S(1)}, bf16[2,128,768]{2,1,0:T(8,128)(2,1)S(1)}, u32[]{:S(2)}, u32[]{:S(2)}) collective-permute-start(bf16[2,128,768]{2,1,0:T(8,128)(2,1)S(1)} %get-tuple-element.40), channel_id=1, source_target_pairs={{0,448},{72,8},{64,128},{136,200},{128,64},{200,136},{192,256},{26... | collective-permute-start | bytes 1179656 | tf_op jit(solution)/shard_map/ppermute | solution.py:315
  60.6 13.2 %collective-permute-start.12 = (bf16[2,128,384]{2,1,0:T(8,128)(2,1)S(1)}, bf16[2,128,384]{2,1,0:T(8,128)(2,1)S(1)}, u32[]{:S(2)}, u32[]{:S(2)}) collective-permute-start(bf16[2,128,384]{2,1,0:T(8,128)(2,1)S(1)} %get-tuple-element.44), channel_id=1, source_target_pairs={{0,448},{72,8},{64,128},{136,200},{128,64},{200,136},{192,256},{26... | collective-permute-start | bytes 589832 | tf_op jit(solution)/shard_map/ppermute | solution.py:315
  65.9 12.9 %collective-permute-start.7 = (bf16[2,512,128]{2,1,0:T(8,128)(2,1)S(1)}, bf16[2,512,128]{2,1,0:T(8,128)(2,1)S(1)}, u32[]{:S(2)}, u32[]{:S(2)}) collective-permute-start(bf16[2,512,128]{2,1,0:T(8,128)(2,1)S(1)} %get-tuple-element.33), channel_id=1, source_target_pairs={{0,16},{16,0},{32,48},{48,32},{1,17},{17,1},{33,49},{49,33},{2,18}... | collective-permute-start | bytes 786440 | tf_op jit(solution)/shard_map/ppermute | solution.py:323
  74.0 15.8 %collective-permute-start.13 = (bf16[128,1152]{1,0:T(8,128)(2,1)S(1)}, bf16[128,1152]{1,0:T(8,128)(2,1)S(1)}, u32[]{:S(2)}, u32[]{:S(2)}) collective-permute-start(bf16[128,1152]{1,0:T(8,128)(2,1)S(1)} %get-tuple-element.46), channel_id=1, source_target_pairs={{0,192},{72,264},{64,384},{136,456},{128,320},{200,392},{192,0},{2... | collective-permute-start | bytes 884744 | tf_op jit(solution)/shard_map/ppermute | solution.py:315
  78.9 9.2 %collective-permute-start.8 = (bf16[512,128]{1,0:T(8,128)(2,1)S(1)}, bf16[512,128]{1,0:T(8,128)(2,1)S(1)}, u32[]{:S(2)}, u32[]{:S(2)}) collective-permute-start(bf16[512,128]{1,0:T(8,128)(2,1)S(1)} %get-tuple-element.35), channel_id=1, source_target_pairs={{0,32},{16,48},{32,0},{48,16},{1,33},{17,49},{33,1},{49,17},{2,34}... | collective-permute-start | bytes 393224 | tf_op jit(solution)/shard_map/ppermute | solution.py:337
